TPU v7x, 512 devices: a whole 4x8x8 slice. The times are simulated.
512 devices in a mesh: gx: 128 (over y, z, core), gz: 4 (over x).
Axes of the slice: x: 4, y: 8, z: 8, core: 2. Of those that a mesh axis runs over, the one named last changes fastest.
Arguments:
- field: bfloat16 [1024, 8, 32, 1024], P('gx', 'gz'), may hold values from -6 to 6
- cotangent: bfloat16 [1024, 8, 32, 1024], P('gx', 'gz'), may hold values from -6 to 6
- spectral_weight: bfloat16 [8192, 2048], P('gx'), may hold values from -8 to 8
- local_weight: bfloat16 [32, 32], replicated, may hold values from -1 to 1
- bias: float32 [32], replicated, may hold values from -1 to 1
Outputs:
- field_grad: bfloat16 [1024, 8, 32, 1024], P('gx', 'gz')
- spectral_grad: bfloat16 [8192, 2048], P('gx')
- local_grad: float32 [32, 32], replicated
- bias_grad: float32 [32], replicated
All inputs are finite; a program needn't handle non-finite values.
Results may differ from a plain program's by a relative error of at most 0.022.
Values may be sent and summed in bfloat16 or wider, within the bound.
No kernel may reach another device: no remote copies, remote signals or barrier semaphores. Data moves between devices by JAX's collectives and lax.ppermute only.
A program may use at most 64 MiB of HBM per device.

v0:
```python
import jax
import jax.numpy as jnp
from jax import lax
from jax.sharding import PartitionSpec as P

KX = 128
KY = 64


def twiddles(freq, pos, length):
    prod_index = freq[:, None] * pos[None, :] % length
    angle = prod_index.astype(jnp.float32) * (2.0 * jnp.pi / length)
    return (jnp.cos(angle), jnp.sin(angle))


def local(field, cotangent, spectral_weight, local_weight, bias):
    rows, depth, chans, ylen = field.shape
    count = lax.axis_size("gx")
    place = lax.axis_index("gx")
    xlen = rows * count
    zlen = depth * lax.axis_size("gz")
    modes_here = spectral_weight.shape[0]
    columns = 1
    copies = KX // modes_here
    inner = depth * chans
    packed = 2 * inner
    xscale = xlen ** (-0.5)
    yscale = ylen ** (-0.5)
    ky_all = jnp.arange(KY, dtype=jnp.int32)
    ycos, ysin = twiddles(jnp.arange(ylen, dtype=jnp.int32), ky_all, ylen)
    ytab = jnp.stack([ycos, -ysin], axis=2).reshape(ylen, 2 * KY).astype(jnp.bfloat16)
    jpos = place % copies * modes_here + jnp.arange(modes_here, dtype=jnp.int32)
    freq = jnp.where(jpos < KX // 2, jpos, jpos - KX)
    xcos, xsin = twiddles(freq, jnp.arange(xlen, dtype=jnp.int32), xlen)
    xcos = xcos.astype(jnp.bfloat16)
    xsin = xsin.astype(jnp.bfloat16)
    ky_here = place // copies * columns + jnp.arange(columns, dtype=jnp.int32)
    weight_column_vector = jnp.where(ky_here == 0, 1.0, 2.0).astype(jnp.float32)
    ones_col = jnp.ones((columns,), jnp.float32)
    weights = spectral_weight.reshape(columns, modes_here, 2, chans, chans)
    weight_real_part = weights[:, :, 0]
    weight_imaginary_part = weights[:, :, 1]
    forward_block = jnp.concatenate(
        [
            jnp.stack([weight_real_part, weight_imaginary_part], axis=3),
            jnp.stack([-weight_imaginary_part, weight_real_part], axis=3),
        ],
        axis=2,
    )
    wret = jnp.swapaxes(weight_real_part, -1, -2)
    wimt = jnp.swapaxes(weight_imaginary_part, -1, -2)
    adjoint_block = jnp.concatenate(
        [jnp.stack([wret, -wimt], axis=3), jnp.stack([wimt, wret], axis=3)], axis=2
    )

    def to_modes(values):
        spectra = (
            jnp.einsum("rzcy,yq->rqzc", values, ytab, preferred_element_type=jnp.float32) * yscale
        )
        spectra = spectra.astype(jnp.bfloat16).reshape(rows, KY, packed)
        spectra = jnp.repeat(spectra, copies, axis=1)
        pencils = lax.all_to_all(spectra, "gx", split_axis=1, concat_axis=0, tiled=True)
        return pencils.reshape(xlen, columns, 2, inner)

    def forward_x(pencils, factor):
        real = pencils[:, :, 0]
        imag = pencils[:, :, 1]
        total_re = jnp.einsum("jx,xkn->kjn", xcos, real, preferred_element_type=jnp.float32)
        total_re = total_re + jnp.einsum(
            "jx,xkn->kjn", xsin, imag, preferred_element_type=jnp.float32
        )
        total_im = jnp.einsum("jx,xkn->kjn", xcos, imag, preferred_element_type=jnp.float32)
        total_im = total_im - jnp.einsum(
            "jx,xkn->kjn", xsin, real, preferred_element_type=jnp.float32
        )
        scale = (xscale * factor)[:, None, None]
        shape = (columns, modes_here, depth, chans)
        return (
            (total_re * scale).astype(jnp.bfloat16).reshape(shape),
            (total_im * scale).astype(jnp.bfloat16).reshape(shape),
        )

    def mix(real, imag, block):
        joined = jnp.concatenate([real, imag], axis=-1)
        return jnp.einsum("kjzi,kjipo->kjpzo", joined, block, preferred_element_type=jnp.float32)

    def back_rows(coeffs):
        whole = lax.all_gather(coeffs.reshape(modes_here, packed), "gx", axis=0, tiled=True)
        whole = whole.reshape(KY, KX, 2, inner)
        jall = jnp.arange(KX, dtype=jnp.int32)
        fall = jnp.where(jall < KX // 2, jall, jall - KX)
        xrows = place * rows + jnp.arange(rows, dtype=jnp.int32)
        rcos, rsin = twiddles(xrows, fall, xlen)
        rcos = rcos.astype(jnp.bfloat16)
        rsin = rsin.astype(jnp.bfloat16)
        query_real_part = whole[:, :, 0]
        qim = whole[:, :, 1]
        back_re = jnp.einsum(
            "xj,kjn->xkn", rcos, query_real_part, preferred_element_type=jnp.float32
        )
        back_re = back_re - jnp.einsum("xj,kjn->xkn", rsin, qim, preferred_element_type=jnp.float32)
        back_im = jnp.einsum("xj,kjn->xkn", rcos, qim, preferred_element_type=jnp.float32)
        back_im = back_im + jnp.einsum(
            "xj,kjn->xkn", rsin, query_real_part, preferred_element_type=jnp.float32
        )
        result = (jnp.stack([back_re, back_im], axis=2) * xscale).astype(jnp.bfloat16)
        return result.reshape(rows, 2 * KY, depth, chans)

    def to_rows(coeffs):
        return (
            jnp.einsum("rqzc,yq->rzcy", back_rows(coeffs), ytab, preferred_element_type=jnp.float32)
            * yscale
        )

    first_real_part, first_imaginary_part = forward_x(to_modes(field), ones_col)
    mixed = (
        mix(first_real_part, first_imaginary_part, forward_block)
        * weight_column_vector[:, None, None, None, None]
    ).astype(jnp.bfloat16)
    spec = to_rows(mixed)
    local_part = jnp.einsum(
        "rzcy,co->rzoy", field, local_weight, preferred_element_type=jnp.float32
    )
    pre = spec + local_part + bias[None, None, :, None]
    sig = jax.nn.sigmoid(pre)
    delta = (cotangent * (sig * (1.0 + pre * (1.0 - sig)))).astype(jnp.bfloat16)
    local_grad = jnp.einsum("rziy,rzoy->io", field, delta, preferred_element_type=jnp.float32)
    bias_grad = jnp.sum(delta, axis=(0, 1, 3), dtype=jnp.float32)
    dre, dim = forward_x(to_modes(delta), weight_column_vector)
    grad_re = jnp.einsum(
        "kjzi,kjzo->kjio", first_real_part, dre, preferred_element_type=jnp.float32
    )
    grad_re = grad_re + jnp.einsum(
        "kjzi,kjzo->kjio", first_imaginary_part, dim, preferred_element_type=jnp.float32
    )
    grad_im = jnp.einsum(
        "kjzi,kjzo->kjio", first_real_part, dim, preferred_element_type=jnp.float32
    )
    grad_im = grad_im - jnp.einsum(
        "kjzi,kjzo->kjio", first_imaginary_part, dre, preferred_element_type=jnp.float32
    )
    mode_terms = jnp.stack([grad_re, grad_im], axis=2).reshape(modes_here, 2 * chans * chans)
    local_grad, bias_grad = lax.psum((local_grad, bias_grad), ("gx", "gz"))
    mode_total = lax.psum(mode_terms.astype(jnp.bfloat16), "gz")
    adjoint = mix(dre, dim, adjoint_block).astype(jnp.bfloat16)
    field_grad = to_rows(adjoint) + jnp.einsum(
        "rzoy,io->rziy", delta, local_weight, preferred_element_type=jnp.float32
    )
    gscale = (xlen * ylen * zlen) ** (-0.5)
    return (field_grad.astype(jnp.bfloat16), mode_total, local_grad * gscale, bias_grad * gscale)


def solution(mesh):
    placed = (P("gx", "gz", None, None), P("gx", "gz", None, None), P("gx", None), P(), P())
    return jax.shard_map(
        local,
        mesh=mesh,
        in_specs=placed,
        out_specs=(P("gx", "gz", None, None), P("gx", None), P(), P()),
        check_vma=False,
    )
```

profile of v0, /device:TPU:1, one launch (start us, length us, event | category | flops | bytes accessed | tf_op | source)
XLA Modules:
  0.0 400.1 jit_solution(9650463930114497545)
XLA Ops:
  7.2 1.1 sine_negate_fusion
  9.9 0.7 broadcast_in_dim.8
  10.7 18.4 %all-to-all-start = ((bf16[8,128,128]{2,0,1:T(8,128)(2,1)}), bf16[8,128,128]{2,0,1:T(8,128)(2,1)S(1)}, u32[]{:S(2)}, u32[]{:S(2)}) async-start(bf16[8,128,128]{2,0,1:T(8,128)(2,1)} %bitcast.19), calls=%async_computation | async-start | bytes 524288 | tf_op jit(solution)/shard_map/all_to_all | solution.py:62
  29.8 1.7 copy.179
  31.5 0.9 copy.180
  32.4 0.9 bitcast_negate_fusion.1
  33.3 10.0 %all-to-all-done = bf16[8,128,128]{2,0,1:T(8,128)(2,1)S(1)} async-done(((bf16[8,128,128]{2,0,1:T(8,128)(2,1)}), bf16[8,128,128]{2,0,1:T(8,128)(2,1)S(1)}, u32[]{:S(2)}, u32[]{:S(2)}) %all-to-all-start) | async-done | bytes 262176 | tf_op jit(solution)/shard_map/all_to_all | solution.py:62
  43.6 0.7 fusion.174
  45.0 1.2 fusion.79
  46.2 1.2 fusion.83
  47.4 1.8 fusion.29
  49.3 1.8 fusion.28
  51.3 1.5 fusion.23
  53.7 76.6 %all-gather.3.cloned.1.call-done = bf16[8192,128]{1,0:T(8,128)(2,1)} async-done(((bf16[64,128]{1,0:T(8,128)(2,1)}), bf16[8192,128]{1,0:T(8,128)(2,1)}) %all-gather.3.cloned.1.call-update) | async-done | bytes 2097168 | tf_op jit(solution)/shard_map/all_gather | solution.py:88
  130.3 8.2 %reshape.343 = bf16[64,128,2,64]{3,2,1,0:T(2,128)(2,1)} reshape(bf16[8192,128]{1,0:T(8,128)(2,1)} %all-gather.3.cloned.1.call-done) | data formatting | bytes 4194304 | tf_op jit(solution)/shard_map/reshape | solution.py:89
  138.5 11.4 %fusion.172 = (bf16[64,128,1,64]{3,2,1,0:T(2,128)(2,1)}, bf16[64,128,1,64]{3,2,1,0:T(2,128)(2,1)}) fusion(bf16[64,128,2,64]{3,2,1,0:T(2,128)(2,1)} %reshape.343), kind=kLoop, calls=%fused_computation.209 | loop fusion | bytes 4194304 | tf_op jit(solution)/shard_map/slice | solution.py:96
  149.9 8.3 %copy.182 = bf16[64,128,1,64]{1,3,0,2:T(8,128)(2,1)S(1)} copy(bf16[64,128,1,64]{3,2,1,0:T(2,128)(2,1)} %get-tuple-element.25) | data formatting | bytes 2097152
  158.2 8.8 %copy.181 = bf16[64,128,1,64]{1,3,0,2:T(8,128)(2,1)S(1)} copy(bf16[64,128,1,64]{3,2,1,0:T(2,128)(2,1)} %get-tuple-element.24) | data formatting | bytes 2097152
  167.0 1.0 fusion.44
  168.0 1.0 fusion.48
  169.0 1.0 fusion.10
  170.0 1.0 fusion.11
  172.3 1.9 convert_reduce_fusion
  175.4 0.7 broadcast_in_dim.9
  176.2 9.6 %all-to-all-start.1 = ((bf16[8,128,128]{2,0,1:T(8,128)(2,1)}), bf16[8,128,128]{2,0,1:T(8,128)(2,1)S(1)}, u32[]{:S(2)}, u32[]{:S(2)}) async-start(bf16[8,128,128]{2,0,1:T(8,128)(2,1)} %bitcast.45), calls=%async_computation.1 | async-start | bytes 524288 | tf_op jit(solution)/shard_map/all_to_all | solution.py:62
  186.1 14.0 %all-to-all-done.1 = bf16[8,128,128]{2,0,1:T(8,128)(2,1)S(1)} async-done(((bf16[8,128,128]{2,0,1:T(8,128)(2,1)}), bf16[8,128,128]{2,0,1:T(8,128)(2,1)S(1)}, u32[]{:S(2)}, u32[]{:S(2)}) %all-to-all-start.1) | async-done | bytes 262176 | tf_op jit(solution)/shard_map/all_to_all | solution.py:62
  200.3 1.5 fusion.173
  201.8 1.3 copy.136
  203.2 1.2 fusion.73
  204.7 1.2 fusion.77
  205.9 1.2 fusion.31
  207.1 1.2 fusion.30
  210.3 1.2 pad_maximum_fusion
  211.5 3.1 copy.156
  214.7 0.9 fusion.52
  215.8 1.5 fusion.20
  218.6 98.0 %all-reduce = (f32[32,32]{0,1:T(8,128)S(1)}, f32[32]{0:T(128)S(1)}) all-reduce(f32[32,32]{0,1:T(8,128)S(1)} %convolution_bitcast_fusion, f32[32]{0:T(128)S(1)} %copy-done.19), channel_id=1, replica_groups=mesh['gx'=128,'gz'=4] {'gx','gz'}, use_global_device_ids=true, to_apply=%region_1.2 | all-reduce | flops 1056 | bytes 8448 | tf_op jit(solution)/shard_map/psum | solution.py:143
  317.7 1.9 copy.157
  319.7 29.1 %all-gather.5.cloned.1.call-done = bf16[8192,128]{1,0:T(8,128)(2,1)} async-done(((bf16[64,128]{1,0:T(8,128)(2,1)}), bf16[8192,128]{1,0:T(8,128)(2,1)}) %all-gather.5.cloned.1.call-update) | async-done | bytes 2097168 | tf_op jit(solution)/shard_map/all_gather | solution.py:88
  348.8 8.3 %reshape.344 = bf16[64,128,2,64]{3,2,1,0:T(2,128)(2,1)} reshape(bf16[8192,128]{1,0:T(8,128)(2,1)} %all-gather.5.cloned.1.call-done) | data formatting | bytes 4194304 | tf_op jit(solution)/shard_map/reshape | solution.py:89
  357.1 11.3 %fusion.171 = (bf16[64,128,1,64]{3,2,1,0:T(2,128)(2,1)}, bf16[64,128,1,64]{3,2,1,0:T(2,128)(2,1)}) fusion(bf16[64,128,2,64]{3,2,1,0:T(2,128)(2,1)} %reshape.344), kind=kLoop, calls=%fused_computation.208 | loop fusion | bytes 4194304 | tf_op jit(solution)/shard_map/slice | solution.py:96
  368.4 8.3 %copy.184 = bf16[64,128,1,64]{1,3,0,2:T(8,128)(2,1)S(1)} copy(bf16[64,128,1,64]{3,2,1,0:T(2,128)(2,1)} %get-tuple-element.23) | data formatting | bytes 2097152
  376.7 1.7 fusion.38
  378.4 8.3 %copy.183 = bf16[64,128,1,64]{1,3,0,2:T(8,128)(2,1)S(1)} copy(bf16[64,128,1,64]{3,2,1,0:T(2,128)(2,1)} %get-tuple-element.22) | data formatting | bytes 2097152
  386.7 1.0 fusion.42
  387.7 1.9 fusion.8
  389.6 1.0 fusion.9
  392.0 1.4 fusion
  (104 shorter events, 13.5 us)
Async XLA Ops:
  7.2 1.5 copy-start
  8.7 20.8 %copy-start.8 = (bf16[64,2048]{1,0:T(8,128)(2,1)S(1)}, bf16[64,2048]{1,0:T(8,128)(2,1)}, u32[]{:S(2)}) copy-start(bf16[64,2048]{1,0:T(8,128)(2,1)} %param.7) | copy-start | bytes 786436
  10.7 32.7 %all-to-all-start = ((bf16[8,128,128]{2,0,1:T(8,128)(2,1)}), bf16[8,128,128]{2,0,1:T(8,128)(2,1)S(1)}, u32[]{:S(2)}, u32[]{:S(2)}) async-start(bf16[8,128,128]{2,0,1:T(8,128)(2,1)} %bitcast.19), calls=%async_computation | async-start | bytes 524288 | tf_op jit(solution)/shard_map/all_to_all | solution.py:62
  29.1 101.2 %all-gather.3.cloned.1.call-start = ((), (), s32[]{:S(2)}) async-start(), calls=%async_computation.2 | async-start | bytes 2113536 | tf_op jit(solution)/shard_map/all_gather | solution.py:88
  32.4 18.9 %copy-start.3 = (bf16[1,64,1,32,32]{3,4,1,2,0:T(8,128)(2,1)}, bf16[1,64,1,32,32]{3,4,1,2,0:T(8,128)(2,1)S(1)}, u32[]{:S(2)}) copy-start(bf16[1,64,1,32,32]{3,4,1,2,0:T(8,128)(2,1)S(1)} %copy.180) | copy-start | bytes 393220
  32.4 13.7 %copy-start.22 = (s32[64]{0:T(128)}, s32[64]{0:T(128)S(1)}, u32[]{:S(2)}) copy-start(s32[64]{0:T(128)S(1)} %compare_select_fusion) | copy-start | bytes 772
  46.2 5.1 %copy-start.5 = (bf16[1,64,1,32,32]{3,4,1,2,0:T(8,128)(2,1)S(1)}, bf16[1,64,1,32,32]{3,4,1,2,0:T(8,128)(2,1)}, u32[]{:S(2)}) copy-start(bf16[1,64,1,32,32]{3,4,1,2,0:T(8,128)(2,1)} %copy.179) | copy-start | bytes 393220
  46.2 5.1 %copy-start.7 = (bf16[1,64,32,1,32]{2,4,3,1,0:T(8,128)(2,1)S(1)}, bf16[1,64,32,1,32]{2,4,3,1,0:T(8,128)(2,1)}, u32[]{:S(2)}) copy-start(bf16[1,64,32,1,32]{2,4,3,1,0:T(8,128)(2,1)} %bitcast_negate_fusion.1) | copy-start | bytes 393220
  51.2 1.7 copy-start.9
  53.7 116.3 %copy-start.13 = (s32[128]{0:T(128)}, s32[128]{0:T(128)S(1)}, u32[]{:S(2)}) copy-start(s32[128]{0:T(128)S(1)} %compare_select_fusion.1) | copy-start | bytes 1540
  53.7 116.2 %copy-start.15 = (s32[8]{0:T(128)}, s32[8]{0:T(128)S(1)}, u32[]{:S(2)}) copy-start(s32[8]{0:T(128)S(1)} %iota_add_fusion) | copy-start | bytes 100
  171.1 0.8 copy-start.17
  171.1 1.2 copy-start.20
  171.1 1.2 copy-start.21
  174.2 43.9 %copy-start.1 = (bf16[8,2,32,1024]{3,2,1,0:T(8,128)(2,1)}, bf16[8,2,32,1024]{3,2,1,0:T(8,128)(2,1)S(1)}, u32[]{:S(2)}) copy-start(bf16[8,2,32,1024]{3,2,1,0:T(8,128)(2,1)S(1)} %get-tuple-element.33) | copy-start | bytes 3145732
  174.2 11.7 %copy-start.10 = (bf16[64,64]{1,0:T(8,128)(2,1)S(1)}, bf16[64,64]{1,0:T(8,128)(2,1)}, u32[]{:S(2)}) copy-start(bf16[64,64]{1,0:T(8,128)(2,1)} %copy-done.9) | copy-start | bytes 24580
  176.2 27.0 %copy-start.23 = (s32[64]{0:T(128)S(1)}, s32[64]{0:T(128)}, u32[]{:S(2)}) copy-start(s32[64]{0:T(128)} %copy-done.22) | copy-start | bytes 772
  176.2 23.9 %all-to-all-start.1 = ((bf16[8,128,128]{2,0,1:T(8,128)(2,1)}), bf16[8,128,128]{2,0,1:T(8,128)(2,1)S(1)}, u32[]{:S(2)}, u32[]{:S(2)}) async-start(bf16[8,128,128]{2,0,1:T(8,128)(2,1)} %bitcast.45), calls=%async_computation.1 | async-start | bytes 524288 | tf_op jit(solution)/shard_map/all_to_all | solution.py:62
  185.8 131.9 %all-reduce.3.cloned.1.call-start = ((), (), s32[]{:S(2)}) async-start(), calls=%async_computation.4 | async-start | bytes 1048576 | tf_op jit(solution)/shard_map/psum | solution.py:144
  208.3 0.6 copy-start.11
  210.3 4.4 %copy-start.4 = (bf16[1,64,1,32,32]{3,4,1,2,0:T(8,128)(2,1)S(1)}, bf16[1,64,1,32,32]{3,4,1,2,0:T(8,128)(2,1)}, u32[]{:S(2)}) copy-start(bf16[1,64,1,32,32]{3,4,1,2,0:T(8,128)(2,1)} %copy-done.3) | copy-start | bytes 393220
  211.5 4.1 %copy-start.12 = (bf16[64,64]{1,0:T(8,128)(2,1)S(1)}, bf16[64,64]{1,0:T(8,128)(2,1)}, u32[]{:S(2)}) copy-start(bf16[64,64]{1,0:T(8,128)(2,1)} %copy-done.11) | copy-start | bytes 24580
  211.5 4.2 %copy-start.6 = (bf16[1,64,1,32,32]{3,4,1,2,0:T(8,128)(2,1)S(1)}, bf16[1,64,1,32,32]{3,4,1,2,0:T(8,128)(2,1)}, u32[]{:S(2)}) copy-start(bf16[1,64,1,32,32]{3,4,1,2,0:T(8,128)(2,1)} %copy.179) | copy-start | bytes 393220
  214.6 134.2 %all-gather.5.cloned.1.call-start = ((), (), s32[]{:S(2)}) async-start(), calls=%async_computation.3 | async-start | bytes 2113536 | tf_op jit(solution)/shard_map/all_gather | solution.py:88
  217.3 1.2 copy-start.19
  368.4 8.3 %copy-start.14 = (s32[128]{0:T(128)S(1)}, s32[128]{0:T(128)}, u32[]{:S(2)}) copy-start(s32[128]{0:T(128)} %copy-done.13) | copy-start | bytes 1540
  368.4 8.3 %copy-start.16 = (s32[8]{0:T(128)S(1)}, s32[8]{0:T(128)}, u32[]{:S(2)}) copy-start(s32[8]{0:T(128)} %copy-done.15) | copy-start | bytes 100
  390.7 1.2 copy-start.2
  390.7 1.2 copy-start.18
Sparse Core Ops, SparseCore 0:
  53.8 76.4 all-gather.2
  214.7 44.7 all-reduce.2
  262.6 86.1 all-gather.4
where the time goes:
time: 405 us; the launch traced here: 400 us
  waiting for transfers between devices  130 us (32%)
  blocking collectives  98 us (24%)
  local copies, waits for them, and re-layouts  94.2 us (23%)
  matrix products  30.3 us (7%)
  starting transfers between devices  28.5 us (7%)
  between operations  14.7 us (4%)
  other arithmetic  4.81 us (1%)
    all_gather x2, waiting for transfers between devices, back_rows(): lax.all_gather(coeffs.reshape(modes_here, packed), 'gx', axis=0, tiled=True)  106 us
    psum x1, blocking collectives, local(): local_grad, bias_grad = lax.psum((local_grad, bias_grad), ('gx', 'gz'))  98 us
    unnamed x57, local copies, waits for them, and re-layouts  40.4 us
    all_to_all x2, starting transfers between devices, to_modes(): lax.all_to_all(spectra, 'gx', split_axis=1, concat_axis=0, tiled=True)  28.1 us
    all_to_all x2, waiting for transfers between devices, to_modes(): lax.all_to_all(spectra, 'gx', split_axis=1, concat_axis=0, tiled=True)  24 us
    slice x2, local copies, waits for them, and re-layouts, back_rows(): query_real_part = whole[:, :, 0]  22.7 us
    reshape x2, local copies, waits for them, and re-layouts, back_rows(): whole = whole.reshape(KY, KX, 2, inner)  16.5 us
  transfers between devices with their start and end apart: 5, of which 4 were waited for; matrix products, arithmetic and copies ran while one was open for 3% of the time, Pallas kernels for 0%

commit v1 on v0

v1 whole, which is shorter than its diff:
```python
import jax
import jax.numpy as jnp
import ml_dtypes
import numpy as np
from jax import lax
from jax.experimental import pallas as pl
from jax.experimental.pallas import tpu as pltpu
from jax.sharding import Mesh
from jax.sharding import PartitionSpec as P

KX = 128
KY = 64
C = 32
N = 1024
F32 = jnp.float32
BF16 = jnp.bfloat16
GX = ("y", "zh", "zl", "core")
VM = pl.BlockSpec(memory_space=pltpu.VMEM)


def angles(freq, pos):
    product = (freq[:, None].astype(np.int64) * pos[None, :].astype(np.int64)) % N
    angle = product.astype(np.float32) * np.float32(2.0 * np.pi / N)
    return np.cos(angle).astype(np.float32), np.sin(angle).astype(np.float32)


def tables():
    ycos, ysin = angles(np.arange(KY), np.arange(N))
    ytab = np.concatenate([ycos, -ysin], axis=0).astype(ml_dtypes.bfloat16)
    ytab = (ytab.astype(np.float32) / 32.0).astype(ml_dtypes.bfloat16)
    j = np.arange(KX)
    freq = np.where(j < KX // 2, j, j - KX)
    r, h, d = np.meshgrid(np.arange(4), np.arange(2), np.arange(128), indexing="ij")
    xcos, xsin = angles(freq, (8 * d + 4 * h + r).reshape(-1))
    forward = np.concatenate([xcos, xsin], axis=0).astype(ml_dtypes.bfloat16)
    inverse = forward.reshape(2 * KX, 4, 256).transpose(2, 1, 0).reshape(256, 1024)
    return ytab, forward, np.ascontiguousarray(inverse)


def nt(a, b):
    return lax.dot_general(a, b, (((1,), (1,)), ((), ())), preferred_element_type=F32)


def nn(a, b):
    return jnp.dot(a, b, preferred_element_type=F32)


def block_of(shape):
    return (lax.broadcasted_iota(jnp.int32, shape, 1) >> 5) & 3


def fold(v):
    v = v + pltpu.roll(v, 64, 1)
    return v + pltpu.roll(v, 32, 1)


def spread(base):
    block = block_of(base.shape)
    return jnp.concatenate([jnp.where(block == r, base, 0.0) for r in range(4)], axis=0).astype(BF16)


def rounded(v):
    return v.astype(BF16).astype(F32)


def mode_weight():
    first = (lax.axis_index("y") + lax.axis_index("zh") + lax.axis_index("zl")) == 0
    return jnp.where(first, 1.0, 2.0).astype(F32)


def x_forward(recv, table, held):
    held[...] = recv[...].astype(F32)
    parts = [
        jnp.concatenate([held[pl.ds(2 * p + h, 128, stride=4), :] for h in range(2)], axis=0)
        for p in range(2)
    ]
    out = nn(table[...], spread(jnp.concatenate(parts, axis=1)))
    real = out[:KX, :128] + out[KX:, 128:]
    imag = out[:KX, 128:] - out[KX:, :128]
    return fold(real) * (1.0 / 32.0), fold(imag) * (1.0 / 32.0)


def x_inverse(real, imag, table, held, stride):
    base = jnp.concatenate(
        [jnp.concatenate([real, imag], axis=1), jnp.concatenate([-imag, real], axis=1)], axis=0
    )
    out = nn(table[...], spread(base)) * (1.0 / 32.0)
    for p in range(2):
        for h in range(2):
            held[pl.ds(2 * p + h, 128, stride=stride), :] = out[
                128 * h : 128 * (h + 1), 128 * p : 128 * (p + 1)
            ]


def y_kernel(field, ytab, send, held):
    for z in range(2):
        for h in range(2):
            rows = field[4 * h : 4 * h + 4, z].reshape(128, N)
            out = nt(ytab[...], rows)
            for p in range(2):
                held[pl.ds(4 * z + 2 * p + h, KY, stride=8), :] = out[KY * p : KY * (p + 1)]
    send[...] = held[...].astype(BF16)


def mix_kernel(recv, weight, forward, inverse, send, kept, held):
    real, imag = x_forward(recv, forward, held)
    real = rounded(real)
    imag = rounded(imag)
    kept[:KX] = real
    kept[KX:] = imag
    k = lax.broadcasted_iota(jnp.int32, (128, 1024), 0)
    lane = lax.broadcasted_iota(jnp.int32, (128, 1024), 1)
    expand = jnp.where((lane >> 5) == k, 1.0, 0.0).astype(BF16)
    wide = nn(jnp.concatenate([real, imag], axis=0).astype(BF16), expand)
    vre = jnp.zeros((KX, 128), F32)
    vim = jnp.zeros((KX, 128), F32)
    for t in range(8):
        wre = weight[:, 128 * t : 128 * (t + 1)].astype(F32)
        wim = weight[:, 1024 + 128 * t : 1024 + 128 * (t + 1)].astype(F32)
        ure = wide[:KX, 128 * t : 128 * (t + 1)]
        uim = wide[KX:, 128 * t : 128 * (t + 1)]
        vre = vre + (ure * wre - uim * wim)
        vim = vim + (ure * wim + uim * wre)
    factor = mode_weight()
    x_inverse(rounded(fold(vre) * factor), rounded(fold(vim) * factor), inverse, held, 4)
    send[...] = held[...].astype(BF16)


def point_kernel(recv, field, cotangent, local4, bias4, ytab, send, delta, sums, held):
    held[...] = recv[...].astype(F32)
    ones = jnp.ones((16, N), BF16)
    total = jnp.zeros((128, 128), F32)
    bias_total = jnp.zeros((16, 128), F32)
    outs = []
    for z in range(2):
        for h in range(2):
            spectrum = jnp.concatenate(
                [held[pl.ds(4 * z + 2 * p + h, KY, stride=8), :] for p in range(2)], axis=0
            )
            left = jnp.concatenate([spectrum.T.astype(BF16), local4[...]], axis=1)
            rows = field[4 * h : 4 * h + 4, z].reshape(128, N)
            cot = cotangent[4 * h : 4 * h + 4, z].reshape(128, N)
            for part in range(4):
                cols = slice(256 * part, 256 * (part + 1))
                right = jnp.concatenate([ytab[:, cols], rows[:, cols]], axis=0)
                pre = nn(left, right) + bias4[...]
                sig = 0.5 * jnp.tanh(0.5 * pre) + 0.5
                slope = sig * (1.0 + pre * (1.0 - sig))
                delta[2 * z + h, :, cols] = (cot[:, cols].astype(F32) * slope).astype(BF16)
            grad = delta[2 * z + h]
            outs.append((z, h, nt(ytab[...], grad)))
            total = total + nt(rows, grad)
            bias_total = bias_total + nt(ones, grad)
    for z, h, out in outs:
        for p in range(2):
            held[pl.ds(4 * z + 2 * p + h, KY, stride=8), :] = out[KY * p : KY * (p + 1)]
    send[...] = held[...].astype(BF16)
    block = block_of((32, 128))
    diag = jnp.zeros((32, 128), F32)
    for r in range(4):
        diag = diag + jnp.where(block == r, total[32 * r : 32 * (r + 1)], 0.0)
    held[0:32, :] = fold(diag)
    block = block_of((8, 128))
    flat = jnp.zeros((8, 128), F32)
    for q in range(4):
        flat = flat + jnp.where(block == q, held[pl.ds(q, 8, stride=4), :], 0.0)
    sums[0:8, :] = flat
    sums[8:16, :] = fold(bias_total[0:8])
    sums[16:, :] = jnp.zeros((112, 128), F32)


def back_kernel(recv, forward, kept, held):
    real, imag = x_forward(recv, forward, held)
    factor = mode_weight()
    kept[:KX] = rounded(real * factor)
    kept[KX:] = rounded(imag * factor)


def adjoint_kernel(kept, weight, inverse, gathered, send, held, high, low):
    dre = kept[:KX]
    dim = kept[KX:]
    for t in range(8):
        cols = slice(128 * t, 128 * (t + 1))
        wre = weight[:, cols].astype(F32)
        wim = weight[:, 1024 + 128 * t : 1024 + 128 * (t + 1)].astype(F32)
        for k, term in ((0, dre * wre + dim * wim), (1, dim * wre - dre * wim)):
            top = term.astype(BF16)
            high[KX * k : KX * (k + 1), cols] = top
            low[KX * k : KX * (k + 1), cols] = (term - top.astype(F32)).astype(BF16)
    k = lax.broadcasted_iota(jnp.int32, (1024, 128), 0)
    lane = lax.broadcasted_iota(jnp.int32, (1024, 128), 1)
    gather = jnp.where((k >> 5) == (lane & 31), 1.0, 0.0).astype(BF16)
    back = rounded(nn(high[...], gather) + nn(low[...], gather))
    x_inverse(back[:KX], back[KX:], inverse, held, 8)
    quarter = 2 * lax.axis_index("zl") + lax.axis_index("core")
    summed = gathered[0:16, :]
    for k in range(1, 16):
        summed = summed + gathered[128 * k : 128 * k + 16, :]
    own = jnp.zeros((2, 128), F32)
    for q in range(4):
        own = own + jnp.where(quarter == q, summed[2 * q : 2 * q + 2], 0.0)
    first = rounded(own)
    second = rounded(own - first)
    bias = summed[8:9]
    bias_1 = rounded(bias)
    bias_2 = rounded(bias - bias_1)
    bias_3 = rounded(bias - bias_1 - bias_2)
    piece = jnp.where(
        quarter == 0, bias_1, jnp.where(quarter == 1, bias_2, jnp.where(quarter == 2, bias_3, 0.0))
    )
    last = jnp.where(block_of((1, 128)) == 3, piece, second[1:2])
    for k, row in enumerate((first[0:1], first[1:2], second[0:1], last)):
        held[pl.ds(4 + k, 128, stride=8), :] = jnp.broadcast_to(row, (128, 128))
    send[...] = held[...].astype(BF16)


def grad_kernel(recv, delta, local4, ytab, field_grad, local_grad, bias_grad, held):
    held[...] = recv[...].astype(F32)
    for z in range(2):
        for h in range(2):
            spectrum = jnp.concatenate(
                [held[pl.ds(8 * z + 2 * p + h, KY, stride=16), :] for p in range(2)], axis=0
            )
            left = jnp.concatenate([spectrum.T.astype(BF16), local4[...]], axis=1)
            for part in range(4):
                cols = slice(256 * part, 256 * (part + 1))
                right = jnp.concatenate([ytab[:, cols], delta[2 * z + h, :, cols]], axis=0)
                field_grad[4 * h : 4 * h + 4, z, :, cols] = (
                    nn(left, right).astype(BF16).reshape(4, 32, 256)
                )
    gscale = float((N * N * 8) ** -0.5)
    block = block_of((1, 128))
    rows = []
    bias = jnp.zeros((1, 128), F32)
    for q in range(4):
        took = [
            jnp.sum(held[pl.ds(8 * q + 4 + k, 32, stride=32), :], axis=0, keepdims=True)
            for k in range(4)
        ]
        bias = bias + jnp.where(block == 3, took[3], 0.0)
        rows.append(took[0] + took[2])
        rows.append(took[1] + jnp.where(block == 3, 0.0, took[3]))
    flat = jnp.concatenate(rows, axis=0) * gscale
    for q in range(4):
        local_grad[pl.ds(q, 8, stride=4), :] = flat[:, 32 * q : 32 * (q + 1)]
    bias_grad[...] = fold(bias)[:, :32] * gscale


def outer_kernel(first, second, out):
    start = 64 * lax.axis_index("core")
    k = lax.broadcasted_iota(jnp.int32, (128, 1024), 0)
    lane = lax.broadcasted_iota(jnp.int32, (128, 1024), 1)
    expand = jnp.where((lane >> 5) == k, 1.0, 0.0).astype(BF16)
    picks = [pl.ds(pl.multiple_of(KX * k + start, 64), 64) for k in range(16)]
    compact = jnp.concatenate([first[pick, :] for pick in picks], axis=0).astype(BF16)
    for pair in range(4):
        wide = nn(compact, expand[:, 256 * pair : 256 * (pair + 1)])
        for half in range(2):
            t = 2 * pair + half
            real = jnp.zeros((64, 128), F32)
            imag = jnp.zeros((64, 128), F32)
            for level in range(8):
                ure = wide[128 * level : 128 * level + 64, 128 * half : 128 * (half + 1)]
                uim = wide[128 * level + 64 : 128 * level + 128, 128 * half : 128 * (half + 1)]
                dre = second[picks[2 * level], :]
                dim = second[picks[2 * level + 1], :]
                real = real + (ure * dre + uim * dim)
                imag = imag + (ure * dim - uim * dre)
            out[:, 128 * t : 128 * (t + 1)] = real.astype(BF16)
            out[:, 1024 + 128 * t : 1024 + 128 * (t + 1)] = imag.astype(BF16)


def run(kernel, operands, outs, scratch, name, flops=200_000_000):
    shapes = [jax.ShapeDtypeStruct(shape, dtype) for shape, dtype in outs]
    return pl.pallas_call(
        kernel,
        out_shape=shapes,
        in_specs=[VM] * len(operands),
        out_specs=[VM] * len(shapes),
        scratch_shapes=[pltpu.VMEM(shape, dtype) for shape, dtype in scratch],
        compiler_params=pltpu.CompilerParams(vmem_limit_bytes=24 * 1024 * 1024),
        cost_estimate=pl.CostEstimate(flops=flops, bytes_accessed=1 << 20, transcendentals=0),
        name=name,
    )(*operands)


def exchange(values, rows):
    blocks = values.reshape(128, rows, 128)
    return lax.all_to_all(blocks, GX, 0, 0, tiled=True).reshape(128 * rows, 128)


def local(field, cotangent, spectral_weight, local_weight, bias):
    ytab, forward, inverse = (jnp.asarray(table) for table in tables())
    same = jnp.asarray(np.kron(np.eye(4), np.ones((C, C))).astype(ml_dtypes.bfloat16))
    local_in = jnp.tile(local_weight, (4, 4)) * same
    local_out = jnp.tile(local_weight.T, (4, 4)) * same
    bias4 = jnp.tile(bias, 4)[:, None]
    slab = ((512, 128), BF16)
    held = ((512, 128), F32)
    kept = ((256, 128), F32)

    (send,) = run(y_kernel, (field, ytab), [slab], [held], "y_forward")
    recv = exchange(send, 4)
    weight = lax.all_gather(spectral_weight, "core", axis=0, tiled=True)
    send, first = run(
        mix_kernel, (recv, weight, forward, inverse), [slab, kept], [held], "mix"
    )
    first_all = lax.all_gather(first, ("core", "gz"), axis=0, tiled=True)
    recv = exchange(send, 4)
    send, delta, sums = run(
        point_kernel,
        (recv, field, cotangent, local_out, bias4, ytab),
        [slab, ((4, 128, N), BF16), ((128, 128), F32)],
        [held],
        "pointwise",
    )
    sums_all = lax.all_gather(sums, ("zl", "core", "gz"), axis=0, tiled=True)
    recv = exchange(send, 4)
    (second,) = run(back_kernel, (recv, forward), [kept], [held], "x_forward")
    second_all = lax.all_gather(second, ("core", "gz"), axis=0, tiled=True)
    (send,) = run(
        adjoint_kernel,
        (second, weight, inverse, sums_all),
        [((1024, 128), BF16)],
        [((1024, 128), F32), ((256, 1024), BF16), ((256, 1024), BF16)],
        "adjoint",
    )
    recv = exchange(send, 8)
    field_grad, local_grad, bias_grad = run(
        grad_kernel,
        (recv, delta, local_in, ytab),
        [((8, 2, C, N), BF16), ((C, C), F32), ((1, C), F32)],
        [((1024, 128), F32)],
        "y_inverse",
    )
    (spectral_grad,) = run(
        outer_kernel, (first_all, second_all), [((64, 2048), BF16)], [], "outer"
    )
    return field_grad, spectral_grad, local_grad, bias_grad.reshape(C)


def solution(mesh):
    fine = Mesh(mesh.devices.reshape(8, 4, 2, 2, 4), GX + ("gz",))
    cells = P(GX, "gz", None, None)
    return jax.shard_map(
        local,
        mesh=fine,
        in_specs=(cells, cells, P(GX, None), P(), P()),
        out_specs=(cells, P(GX, None), P(), P()),
        check_vma=False,
    )
```

time: 405 us -> 187 us (0.46); the launches traced: 400 us -> 187 us
  local copies, waits for them, and re-layouts: 94.2 us -> 9.03 us
  blocking collectives: 98 us -> 20.9 us
  waiting for transfers between devices: 130 us -> 90.6 us
  matrix products: 30.3 us -> 0 us
  Pallas kernels: 0 us -> 13 us
  starting transfers between devices: 28.5 us -> 39.2 us
  other arithmetic: 4.81 us -> 0.12 us
    psum x1 -> x0, blocking collectives: 98 us -> none  [local(): local_grad, bias_grad = lax.psum((local_grad, bias_grad), ('gx', 'gz'))]
    all_gather x2 -> x3, waiting for transfers between devices: 106 us -> 69.1 us  [the longest x1 31.5 us: local(): second_all = lax.all_gather(second, ('core', 'gz'), axis=0, tiled=True)]
    unnamed x57 -> x32, local copies, waits for them, and re-layouts: 40.4 us -> 8.59 us
    dot_general x29 -> x0, matrix products: 30.3 us -> none  [the longest x2 3.06 us: mix(): jnp.einsum('kjzi,kjipo->kjpzo', joined, block, preferred_element_type=jnp...]
    slice x9 -> x0, local copies, waits for them, and re-layouts: 27.3 us -> none  [the longest x2 22.7 us: back_rows(): query_real_part = whole[:, :, 0]]
    reshape x14 -> x0, local copies, waits for them, and re-layouts: 19.5 us -> none  [the longest x2 16.5 us: back_rows(): whole = whole.reshape(KY, KX, 2, inner)]
    all_to_all x0 -> x1, blocking collectives: none -> 18.2 us  [exchange(): return lax.all_to_all(blocks, GX, 0, 0, tiled=True).reshape(128 * rows, 128)]
    pallas_call x0 -> x7, Pallas kernels: none -> 13 us  [run(): pl.pallas_call(kernel, out_shape=shapes, in_specs=[VM] * len(operands), o...]
  transfers between devices with their start and end apart: 5 -> 6, of which waited for: 4 -> 5; matrix products, arithmetic and copies ran while one was open for 3% -> 0% of each run, Pallas kernels for 0% -> 3%
where the time goes in v1:
time: 187 us
  waiting for transfers between devices  90.6 us (48%)
  starting transfers between devices  39.2 us (21%)
  blocking collectives  20.9 us (11%)
  between operations  13.9 us (7%)
  Pallas kernels  13 us (7%)
  local copies, waits for them, and re-layouts  9.03 us (5%)
    all_to_all x3, starting transfers between devices, exchange(): return lax.all_to_all(blocks, GX, 0, 0, tiled=True).reshape(128 * rows, 128)  39.1 us
    all_gather x1, waiting for transfers between devices, local(): second_all = lax.all_gather(second, ('core', 'gz'), axis=0, tiled=True)  31.5 us
    all_gather x1, waiting for transfers between devices, local(): sums_all = lax.all_gather(sums, ('zl', 'core', 'gz'), axis=0, tiled=True)  23.5 us
    all_to_all x3, waiting for transfers between devices, exchange(): return lax.all_to_all(blocks, GX, 0, 0, tiled=True).reshape(128 * rows, 128)  20.7 us
    all_to_all x1, blocking collectives, exchange(): return lax.all_to_all(blocks, GX, 0, 0, tiled=True).reshape(128 * rows, 128)  18.2 us
    all_gather x1, waiting for transfers between devices, local(): first_all = lax.all_gather(first, ('core', 'gz'), axis=0, tiled=True)  14 us
    pallas_call x7, Pallas kernels, run(): pl.pallas_call(kernel, out_shape=shapes, in_specs=[VM] * len(operands), o...  13 us
    unnamed x32, local copies, waits for them, and re-layouts  8.59 us
  transfers between devices with their start and end apart: 6, of which 5 were waited for; matrix products, arithmetic and copies ran while one was open for 0% of the time, Pallas kernels for 3%

profile of v1, /device:TPU:1, one launch (start us, length us, event | category | flops | bytes accessed | tf_op | source)
XLA Modules:
  0.0 186.7 jit_solution(2379662758823088182)
XLA Ops:
  7.2 0.0 copy-start
  7.2 1.2 copy-done
  8.4 0.9 copy-done.2
  9.3 1.1 y_forward.1
  10.5 18.6 %all-to-all-start = ((bf16[128,4,128]{2,1,0:T(4,128)(2,1)}), bf16[128,4,128]{2,1,0:T(4,128)(2,1)S(1)}, u32[]{:S(2)}, u32[]{:S(2)}) async-start(bf16[128,4,128]{2,1,0:T(4,128)(2,1)} %bitcast), calls=%async_computation | async-start | bytes 262144 | tf_op jit(solution)/shard_map/all_to_all | solution.py:289
  29.0 0.0 copy-done.12
  29.0 2.7 %all_gather.12.weight = bf16[128,2048]{1,0:T(8,128)(2,1)S(1)} all-gather(bf16[64,2048]{1,0:T(8,128)(2,1)S(1)} %copy-done.12), channel_id=1, replica_groups=mesh['y'=8,'zh'=4,'zl'=2,'core'=2,'gz'=4] {'core'}, dimensions={0}, use_global_device_ids=true | all-gather | bytes 786432 | tf_op jit(solution)/shard_map/all_gather | solution.py:304
  31.7 9.5 %all-to-all-done = bf16[128,4,128]{2,1,0:T(4,128)(2,1)S(1)} async-done(((bf16[128,4,128]{2,1,0:T(4,128)(2,1)}), bf16[128,4,128]{2,1,0:T(4,128)(2,1)S(1)}, u32[]{:S(2)}, u32[]{:S(2)}) %all-to-all-start) | async-done | bytes 131104 | tf_op jit(solution)/shard_map/all_to_all | solution.py:289
  41.2 0.0 copy-done.4
  41.2 0.0 copy-done.5
  41.2 2.1 %mix.1 = (bf16[512,128]{1,0:T(8,128)(2,1)}, f32[256,128]{1,0:T(8,128)}) custom-call(bf16[512,128]{1,0:T(8,128)(2,1)S(1)} %bitcast.13, bf16[128,2048]{1,0:T(8,128)(2,1)S(1)} %all_gather.12.weight, bf16[256,1024]{1,0:T(8,128)(2,1)S(1)} %copy-done.5, bf16[256,1024]{1,0:T(8,128)(2,1)S(1)} %copy-done.4), custom_call_target="tpu_custom_call" | custom-call | flops 200000000 | bytes 1048576 | tf_op jit(solution)/shard_map/mix/pallas_call | solution.py:275
  43.4 6.3 %all-to-all-start.1 = ((bf16[128,4,128]{2,1,0:T(4,128)(2,1)}), bf16[128,4,128]{2,1,0:T(4,128)(2,1)S(1)}, u32[]{:S(2)}, u32[]{:S(2)}) async-start(bf16[128,4,128]{2,1,0:T(4,128)(2,1)} %bitcast.2), calls=%async_computation.1 | async-start | bytes 262144 | tf_op jit(solution)/shard_map/all_to_all | solution.py:289
  49.7 0.0 all-gather.4.cloned.1.call-start
  49.7 0.0 copy-done.14
  49.8 0.1 copy.13
  49.8 0.0 copy-done.13
  49.8 0.1 broadcast_multiply_fusion
  50.0 0.0 copy-start.15
  50.0 0.1 reshape.48.local4
  50.1 0.5 copy-done.15
  50.6 0.1 broadcast_in_dim_tile.4.bias4
  50.7 11.3 %all-to-all-done.1 = bf16[128,4,128]{2,1,0:T(4,128)(2,1)S(1)} async-done(((bf16[128,4,128]{2,1,0:T(4,128)(2,1)}), bf16[128,4,128]{2,1,0:T(4,128)(2,1)S(1)}, u32[]{:S(2)}, u32[]{:S(2)}) %all-to-all-start.1) | async-done | bytes 131104 | tf_op jit(solution)/shard_map/all_to_all | solution.py:289
  62.0 0.0 copy-done.1
  62.0 0.0 copy-done.3
  62.0 1.2 copy-done.6
  63.2 2.6 %pointwise.1 = (bf16[512,128]{1,0:T(8,128)(2,1)S(1)}, bf16[4,128,1024]{2,1,0:T(8,128)(2,1)S(1)}, f32[128,128]{1,0:T(8,128)}) custom-call(bf16[512,128]{1,0:T(8,128)(2,1)S(1)} %bitcast.11, bf16[8,2,32,1024]{3,2,1,0:T(8,128)(2,1)S(1)} %copy-done.1, bf16[8,2,32,1024]{3,2,1,0:T(8,128)(2,1)S(1)} %copy-done.6, bf16[128,128]{1,0:T(8,128)(2,1)S(1)} %reshape.48.local4, ...), custom_call_target="tpu_custom_call" | custom-call | flops 200000000 | bytes 1048576 | tf_op jit(solution)/shard_map/pointwise/pallas_call | solution.py:275
  65.9 1.0 copy-done.7
  66.8 0.0 all-gather.4.cloned.1.call-update
  66.9 0.0 all-gather.6.cloned.1.call-start
  66.9 0.7 all-gather.6.cloned.1.call-update
  67.6 0.0 all-gather.8.cloned.1.call-start
  67.7 18.2 %all_to_all.20 = bf16[128,4,128]{2,1,0:T(4,128)(2,1)S(1)} all-to-all(bf16[128,4,128]{2,1,0:T(4,128)(2,1)S(1)} %bitcast.14), channel_id=1, replica_groups=mesh['y'=8,'zh'=4,'zl'=2,'core'=2,'gz'=4] {'y','zh','zl','core'}, dimensions={0} | all-to-all | bytes 262144 | tf_op jit(solution)/shard_map/all_to_all | solution.py:289
  85.8 1.1 x_forward.1.kept
  86.9 0.0 all-gather.8.cloned.1.call-update
  87.0 23.5 %all-gather.4.cloned.1.call-done.gathered = f32[2048,128]{1,0:T(8,128)} async-done(((f32[128,128]{1,0:T(8,128)}), f32[2048,128]{1,0:T(8,128)}) %all-gather.4.cloned.1.call-update) | async-done | bytes 1048592 | tf_op jit(solution)/shard_map/all_gather | solution.py:317
  110.5 1.2 copy-done.10
  111.7 2.9 %adjoint.1 = bf16[1024,128]{1,0:T(8,128)(2,1)} custom-call(f32[256,128]{1,0:T(8,128)} %x_forward.1.kept, bf16[128,2048]{1,0:T(8,128)(2,1)S(1)} %all_gather.12.weight, bf16[256,1024]{1,0:T(8,128)(2,1)S(1)} %copy-done.4, f32[2048,128]{1,0:T(8,128)S(1)} %copy-done.10), custom_call_target="tpu_custom_call" | custom-call | flops 200000000 | bytes 1048576 | tf_op jit(solution)/shard_map/adjoint/pallas_call | solution.py:275
  114.6 14.2 %all-to-all-start.3 = ((bf16[128,8,128]{2,1,0:T(8,128)(2,1)}), bf16[128,8,128]{2,1,0:T(8,128)(2,1)S(1)}, u32[]{:S(2)}, u32[]{:S(2)}) async-start(bf16[128,8,128]{2,1,0:T(8,128)(2,1)} %bitcast.7), calls=%async_computation.3 | async-start | bytes 524288 | tf_op jit(solution)/shard_map/all_to_all | solution.py:289
  128.8 0.1 reshape.50.local4
  128.9 0.0 copy-start.8
  128.9 14.0 %all-gather.6.cloned.1.call-done.first = f32[2048,128]{1,0:T(8,128)} async-done(((f32[256,128]{1,0:T(8,128)}), f32[2048,128]{1,0:T(8,128)}) %all-gather.6.cloned.1.call-update) | async-done | bytes 1048592 | tf_op jit(solution)/shard_map/all_gather | solution.py:308
  143.0 31.5 %all-gather.8.cloned.1.call-done.second = f32[2048,128]{1,0:T(8,128)} async-done(((f32[256,128]{1,0:T(8,128)}), f32[2048,128]{1,0:T(8,128)}) %all-gather.8.cloned.1.call-update) | async-done | bytes 1048592 | tf_op jit(solution)/shard_map/all_gather | solution.py:320
  174.5 1.2 copy-done.9
  175.7 1.2 copy-done.11
  177.0 1.6 outer.1
  178.6 0.0 all-to-all-done.3
  178.6 0.0 copy-done.8
  178.6 1.6 y_inverse.1
  (14 shorter events, 0.0 us)
Async XLA Ops:
  7.2 1.2 copy-start
  8.4 0.9 copy-start.2
  9.3 19.7 %copy-start.12 = (bf16[64,2048]{1,0:T(8,128)(2,1)S(1)}, bf16[64,2048]{1,0:T(8,128)(2,1)}, u32[]{:S(2)}) copy-start(bf16[64,2048]{1,0:T(8,128)(2,1)} %param.11) | copy-start | bytes 786436
  10.5 30.8 %copy-start.4 = (bf16[256,1024]{1,0:T(8,128)(2,1)S(1)}, bf16[256,1024]{1,0:T(8,128)(2,1)}, u32[]{:S(2)}) copy-start(bf16[256,1024]{1,0:T(8,128)(2,1)} %constant.10.clone.inverse) | copy-start | bytes 1572868
  10.5 30.8 %copy-start.5 = (bf16[256,1024]{1,0:T(8,128)(2,1)S(1)}, bf16[256,1024]{1,0:T(8,128)(2,1)}, u32[]{:S(2)}) copy-start(bf16[256,1024]{1,0:T(8,128)(2,1)} %constant.9.clone.forward) | copy-start | bytes 1572868
  10.5 30.8 %all-to-all-start = ((bf16[128,4,128]{2,1,0:T(4,128)(2,1)}), bf16[128,4,128]{2,1,0:T(4,128)(2,1)S(1)}, u32[]{:S(2)}, u32[]{:S(2)}) async-start(bf16[128,4,128]{2,1,0:T(4,128)(2,1)} %bitcast), calls=%async_computation | async-start | bytes 262144 | tf_op jit(solution)/shard_map/all_to_all | solution.py:289
  41.2 20.8 %copy-start.1 = (bf16[8,2,32,1024]{3,2,1,0:T(8,128)(2,1)S(1)}, bf16[8,2,32,1024]{3,2,1,0:T(8,128)(2,1)}, u32[]{:S(2)}) copy-start(bf16[8,2,32,1024]{3,2,1,0:T(8,128)(2,1)} %field.3) | copy-start | bytes 3145732
  43.4 6.4 %copy-start.14 = (bf16[32,32]{1,0:T(8,128)(2,1)S(1)}, bf16[32,32]{1,0:T(8,128)(2,1)}, u32[]{:S(2)}) copy-start(bf16[32,32]{1,0:T(8,128)(2,1)} %param.12) | copy-start | bytes 6148
  43.4 6.5 %copy-start.13 = (bf16[4,32,4,32]{3,2,1,0:T(4,128)(2,1)S(1)}, bf16[4,32,4,32]{3,2,1,0:T(4,128)(2,1)}, u32[]{:S(2)}) copy-start(bf16[4,32,4,32]{3,2,1,0:T(4,128)(2,1)} %constant.15) | copy-start | bytes 98308
  43.4 18.6 %all-to-all-start.1 = ((bf16[128,4,128]{2,1,0:T(4,128)(2,1)}), bf16[128,4,128]{2,1,0:T(4,128)(2,1)S(1)}, u32[]{:S(2)}, u32[]{:S(2)}) async-start(bf16[128,4,128]{2,1,0:T(4,128)(2,1)} %bitcast.2), calls=%async_computation.1 | async-start | bytes 262144 | tf_op jit(solution)/shard_map/all_to_all | solution.py:289
  49.7 60.8 %all-gather.4.cloned.1.call-start = ((), (), s32[]{:S(2)}) async-start(), calls=%async_computation.4 | async-start | bytes 1114112 | tf_op jit(solution)/shard_map/all_gather | solution.py:317
  49.8 12.2 %copy-start.3 = (bf16[128,1024]{1,0:T(8,128)(2,1)S(1)}, bf16[128,1024]{1,0:T(8,128)(2,1)}, u32[]{:S(2)}) copy-start(bf16[128,1024]{1,0:T(8,128)(2,1)} %constant.8.clone.ytab) | copy-start | bytes 786436
  50.0 0.7 copy-start.15
  62.0 1.2 copy-start.6
  65.9 1.0 copy-start.7
  66.9 76.1 %all-gather.6.cloned.1.call-start = ((), (), s32[]{:S(2)}) async-start(), calls=%async_computation.5 | async-start | bytes 1179648 | tf_op jit(solution)/shard_map/all_gather | solution.py:308
  67.6 106.9 %all-gather.8.cloned.1.call-start = ((), (), s32[]{:S(2)}) async-start(), calls=%async_computation.6 | async-start | bytes 1179648 | tf_op jit(solution)/shard_map/all_gather | solution.py:320
  110.5 1.2 copy-start.10
  114.6 64.0 %all-to-all-start.3 = ((bf16[128,8,128]{2,1,0:T(8,128)(2,1)}), bf16[128,8,128]{2,1,0:T(8,128)(2,1)S(1)}, u32[]{:S(2)}, u32[]{:S(2)}) async-start(bf16[128,8,128]{2,1,0:T(8,128)(2,1)} %bitcast.7), calls=%async_computation.3 | async-start | bytes 524288 | tf_op jit(solution)/shard_map/all_to_all | solution.py:289
  128.9 49.7 %copy-start.8 = (bf16[4,128,1024]{2,1,0:T(8,128)(2,1)S(1)}, bf16[4,128,1024]{2,1,0:T(8,128)(2,1)}, u32[]{:S(2)}) copy-start(bf16[4,128,1024]{2,1,0:T(8,128)(2,1)} %copy-done.7) | copy-start | bytes 3145732
  174.5 1.2 copy-start.9
  175.7 1.2 copy-start.11
Sparse Core Ops, SparseCore 0:
  67.0 43.4 all-gather.3
  112.7 30.2 all-gather.5
  145.7 28.7 all-gather.7

commit v2 on v1

v2 whole, which is shorter than its diff:
```python
import jax
import jax.numpy as jnp
import ml_dtypes
import numpy as np
from jax import lax
from jax.experimental import pallas as pl
from jax.experimental.pallas import tpu as pltpu
from jax.sharding import Mesh
from jax.sharding import PartitionSpec as P

KX = 128
KY = 64
C = 32
N = 1024
F32 = jnp.float32
BF16 = jnp.bfloat16
GX = ("y", "z", "core")
VM = pl.BlockSpec(memory_space=pltpu.VMEM)
ANY = pl.BlockSpec(memory_space=pl.ANY)


def angles(freq, pos):
    product = (freq[:, None].astype(np.int64) * pos[None, :].astype(np.int64)) % N
    angle = product.astype(np.float32) * np.float32(2.0 * np.pi / N)
    return np.cos(angle).astype(np.float32), np.sin(angle).astype(np.float32)


def tables():
    ycos, ysin = angles(np.arange(KY), np.arange(N))
    ytab = np.concatenate([ycos, -ysin], axis=0).astype(ml_dtypes.bfloat16)
    ytab = (ytab.astype(np.float32) / 32.0).astype(ml_dtypes.bfloat16)
    j = np.arange(KX)
    freq = np.where(j < KX // 2, j, j - KX)
    r, h, d = np.meshgrid(np.arange(4), np.arange(2), np.arange(128), indexing="ij")
    xcos, xsin = angles(freq, (8 * d + 4 * h + r).reshape(-1))
    forward = np.concatenate([xcos, xsin], axis=0).astype(ml_dtypes.bfloat16)
    inverse = forward.reshape(2 * KX, 4, 256).transpose(2, 1, 0).reshape(256, 1024)
    return ytab, forward, np.ascontiguousarray(inverse)


def nt(a, b):
    return lax.dot_general(a, b, (((1,), (1,)), ((), ())), preferred_element_type=F32)


def nn(a, b):
    return jnp.dot(a, b, preferred_element_type=F32)


def block_of(shape):
    return (lax.broadcasted_iota(jnp.int32, shape, 1) >> 5) & 3


def fold(v):
    v = v + pltpu.roll(v, 64, 1)
    return v + pltpu.roll(v, 32, 1)


def spread(base):
    block = block_of(base.shape)
    return jnp.concatenate([jnp.where(block == r, base, 0.0) for r in range(4)], axis=0).astype(BF16)


def rounded(v):
    return v.astype(BF16).astype(F32)


def mode_weight():
    first = (lax.axis_index("y") + lax.axis_index("z")) == 0
    return jnp.where(first, 1.0, 2.0).astype(F32)


def x_forward(recv, table, held, stride):
    held[...] = recv[...].astype(F32)
    parts = [
        jnp.concatenate([held[pl.ds(2 * p + h, 128, stride=stride), :] for h in range(2)], axis=0)
        for p in range(2)
    ]
    out = nn(table[...], spread(jnp.concatenate(parts, axis=1)))
    real = out[:KX, :128] + out[KX:, 128:]
    imag = out[:KX, 128:] - out[KX:, :128]
    return fold(real) * (1.0 / 32.0), fold(imag) * (1.0 / 32.0)


def paired(real, imag):
    return jnp.where((block_of(real.shape) & 1) == 0, real, imag)


def x_inverse(real, imag, table, held, stride):
    base = jnp.concatenate(
        [jnp.concatenate([real, imag], axis=1), jnp.concatenate([-imag, real], axis=1)], axis=0
    )
    out = nn(table[...], spread(base)) * (1.0 / 32.0)
    for p in range(2):
        for h in range(2):
            held[pl.ds(2 * p + h, 128, stride=stride), :] = out[
                128 * h : 128 * (h + 1), 128 * p : 128 * (p + 1)
            ]


def y_kernel(field, ytab, send, held, rows, table, sems):
    copies = [pltpu.make_async_copy(ytab, table, sems.at[4])]
    for k in range(4):
        part = field.at[pl.ds(4 * (k % 2), 4), k // 2]
        copies.append(pltpu.make_async_copy(part, rows.at[k], sems.at[k]))
    for copy in copies:
        copy.start()
    copies[0].wait()
    for k in range(4):
        z, h = k // 2, k % 2
        copies[1 + k].wait()
        out = nt(table[...], rows[k].reshape(128, N))
        for p in range(2):
            held[pl.ds(4 * z + 2 * p + h, KY, stride=8), :] = out[KY * p : KY * (p + 1)]
    send[...] = held[...].astype(BF16)


def mix_kernel(recv, weight, forward, inverse, send, kept, held):
    real, imag = x_forward(recv, forward, held, 4)
    real = rounded(real)
    imag = rounded(imag)
    kept[...] = paired(real, imag).astype(BF16)
    k = lax.broadcasted_iota(jnp.int32, (128, 1024), 0)
    lane = lax.broadcasted_iota(jnp.int32, (128, 1024), 1)
    expand = jnp.where((lane >> 5) == k, 1.0, 0.0).astype(BF16)
    wide = nn(jnp.concatenate([real, imag], axis=0).astype(BF16), expand)
    vre = jnp.zeros((KX, 128), F32)
    vim = jnp.zeros((KX, 128), F32)
    for t in range(8):
        wre = weight[:, 128 * t : 128 * (t + 1)].astype(F32)
        wim = weight[:, 1024 + 128 * t : 1024 + 128 * (t + 1)].astype(F32)
        ure = wide[:KX, 128 * t : 128 * (t + 1)]
        uim = wide[KX:, 128 * t : 128 * (t + 1)]
        vre = vre + (ure * wre - uim * wim)
        vim = vim + (ure * wim + uim * wre)
    factor = mode_weight()
    x_inverse(rounded(fold(vre) * factor), rounded(fold(vim) * factor), inverse, held, 4)
    send[...] = held[...].astype(BF16)


def point_kernel(recv, field, cotangent, local4, bias4, ytab, send, delta, held, wide):
    held[...] = recv[...].astype(F32)
    ones = jnp.ones((16, N), BF16)
    total = jnp.zeros((128, 128), F32)
    bias_total = jnp.zeros((16, 128), F32)
    outs = []
    for z in range(2):
        for h in range(2):
            spectrum = jnp.concatenate(
                [held[pl.ds(4 * z + 2 * p + h, KY, stride=8), :] for p in range(2)], axis=0
            )
            left = jnp.concatenate([spectrum.T.astype(BF16), local4[...]], axis=1)
            rows = field[4 * h : 4 * h + 4, z].reshape(128, N)
            cot = cotangent[4 * h : 4 * h + 4, z].reshape(128, N)
            for part in range(4):
                cols = slice(256 * part, 256 * (part + 1))
                right = jnp.concatenate([ytab[:, cols], rows[:, cols]], axis=0)
                pre = nn(left, right) + bias4[...]
                sig = 0.5 * jnp.tanh(0.5 * pre) + 0.5
                slope = sig * (1.0 + pre * (1.0 - sig))
                delta[2 * z + h, :, cols] = (cot[:, cols].astype(F32) * slope).astype(BF16)
            grad = delta[2 * z + h]
            outs.append((z, h, nt(ytab[...], grad)))
            total = total + nt(rows, grad)
            bias_total = bias_total + nt(ones, grad)
    block = block_of((32, 128))
    diag = jnp.zeros((32, 128), F32)
    for r in range(4):
        diag = diag + jnp.where(block == r, total[32 * r : 32 * (r + 1)], 0.0)
    held[0:32, :] = fold(diag)
    block = block_of((8, 128))
    flat = jnp.zeros((8, 128), F32)
    for q in range(4):
        flat = flat + jnp.where(block == q, held[pl.ds(q, 8, stride=4), :], 0.0)
    bias = fold(bias_total[0:8])[0:1]
    bias_1 = rounded(bias)
    bias_2 = rounded(bias - bias_1)
    bias_3 = bias - bias_1 - bias_2
    block = block_of((1, 128))
    pieces = jnp.where(
        block == 0, bias_1, jnp.where(block == 1, bias_2, jnp.where(block == 2, bias_3, 0.0))
    )
    for z, h, out in outs:
        for p in range(2):
            wide[pl.ds(10 * z + 2 * p + h, KY, stride=20), :] = out[KY * p : KY * (p + 1)]
    for z in range(2):
        lines = [flat[4 * z + k : 4 * z + k + 1] for k in range(4)]
        lines = lines + [pieces, jnp.zeros((1, 128), F32)]
        for k, line in enumerate(lines):
            wide[pl.ds(10 * z + 4 + k, KY, stride=20), :] = jnp.broadcast_to(line, (KY, 128))
    send[...] = wide[...].astype(BF16)


def back_kernel(recv, forward, kept, share, held):
    real, imag = x_forward(recv, forward, held, 10)
    factor = mode_weight()
    real = rounded(real * factor)
    imag = rounded(imag * factor)
    kept[:KX] = real
    kept[KX:] = imag
    share[:KX] = paired(real, imag).astype(BF16)
    lines = [
        jnp.sum(held[pl.ds(4 + k, 128, stride=10), :], axis=0, keepdims=True) for k in range(5)
    ]
    total = jnp.concatenate(lines[:4], axis=0)
    bias = fold(lines[4])
    share[KX:] = jnp.concatenate(
        [
            rounded(total),
            total - rounded(total),
            rounded(bias),
            bias - rounded(bias),
            jnp.zeros((6, 128), F32),
        ],
        axis=0,
    ).astype(BF16)


def adjoint_kernel(kept, weight, inverse, firsts, seconds, send, group, held, high, low):
    dre = kept[:KX]
    dim = kept[KX:]
    for t in range(8):
        cols = slice(128 * t, 128 * (t + 1))
        wre = weight[:, cols].astype(F32)
        wim = weight[:, 1024 + 128 * t : 1024 + 128 * (t + 1)].astype(F32)
        for k, term in ((0, dre * wre + dim * wim), (1, dim * wre - dre * wim)):
            top = term.astype(BF16)
            high[KX * k : KX * (k + 1), cols] = top
            low[KX * k : KX * (k + 1), cols] = (term - top.astype(F32)).astype(BF16)
    k = lax.broadcasted_iota(jnp.int32, (1024, 128), 0)
    lane = lax.broadcasted_iota(jnp.int32, (1024, 128), 1)
    gather = jnp.where((k >> 5) == (lane & 31), 1.0, 0.0).astype(BF16)
    back = rounded(nn(high[...], gather) + nn(low[...], gather))
    x_inverse(back[:KX], back[KX:], inverse, held, 4)
    send[...] = held[...].astype(BF16)
    start = 64 * lax.axis_index("core")
    left = block_of((64, 128)) < 2
    for k, (both, step) in enumerate(((firsts, KX), (seconds, KX + 16))):
        one = both[pl.ds(pl.multiple_of(start, 16), 64), :].astype(F32)
        two = both[pl.ds(pl.multiple_of(step + start, 16), 64), :].astype(F32)
        group[64 * k : 64 * (k + 1)] = jnp.where(left, one, two).astype(BF16)
    group[128:144] = seconds[KX : KX + 16]
    group[144:160] = seconds[2 * KX + 16 : 2 * KX + 32]


def grad_kernel(recv, delta, local4, ytab, field_grad, held, rows, sems):
    held[...] = recv[...].astype(F32)
    copies = []
    for k in range(4):
        z, h = k // 2, k % 2
        spectrum = jnp.concatenate(
            [held[pl.ds(4 * z + 2 * p + h, KY, stride=8), :] for p in range(2)], axis=0
        )
        left = jnp.concatenate([spectrum.T.astype(BF16), local4[...]], axis=1)
        for part in range(4):
            cols = slice(256 * part, 256 * (part + 1))
            right = jnp.concatenate([ytab[:, cols], delta[k, :, cols]], axis=0)
            rows[k, :, :, cols] = nn(left, right).astype(BF16).reshape(4, 32, 256)
        copies.append(
            pltpu.make_async_copy(rows.at[k], field_grad.at[pl.ds(4 * h, 4), z], sems.at[k])
        )
        copies[k].start()
    for copy in copies:
        copy.wait()


def outer_kernel(groups, out, local_grad, bias_grad, tiles):
    lane = lax.broadcasted_iota(jnp.int32, (128, 1024), 1)
    k = lax.broadcasted_iota(jnp.int32, (128, 1024), 0)
    expand = jnp.where((lane >> 5) == k, 1.0, 0.0).astype(BF16)
    first = jnp.concatenate([groups[160 * g : 160 * g + 64] for g in range(4)], axis=0).astype(F32)
    turned = [first] + [pltpu.roll(first, 128 - 32 * b, 1) for b in range(1, 4)]
    compact = jnp.concatenate(turned, axis=0).astype(BF16)
    block = block_of((64, 128))
    for g in range(4):
        second = groups[160 * g + 64 : 160 * g + 128].astype(F32)
        for b in range(4):
            tiles[64 * (4 * g + b) : 64 * (4 * g + b + 1)] = fold(
                jnp.where(block == b, second, 0.0)
            )
    for pair in range(4):
        wide = nn(compact, expand[:, 256 * pair : 256 * (pair + 1)])
        for half in range(2):
            t = 2 * pair + half
            cols = slice(128 * half, 128 * (half + 1))
            real = jnp.zeros((64, 128), F32)
            imag = jnp.zeros((64, 128), F32)
            for g in range(4):
                for z in range(2):
                    b = 2 * z
                    ure = wide[256 * b + 64 * g : 256 * b + 64 * (g + 1), cols]
                    uim = wide[256 * (b + 1) + 64 * g : 256 * (b + 1) + 64 * (g + 1), cols]
                    dre = tiles[64 * (4 * g + b) : 64 * (4 * g + b + 1)]
                    dim = tiles[64 * (4 * g + b + 1) : 64 * (4 * g + b + 2)]
                    real = real + (ure * dre + uim * dim)
                    imag = imag + (ure * dim - uim * dre)
            out[:, 128 * t : 128 * (t + 1)] = real.astype(BF16)
            out[:, 1024 + 128 * t : 1024 + 128 * (t + 1)] = imag.astype(BF16)
    gscale = float((N * N * 8) ** -0.5)
    total = groups[128:160].astype(F32)
    for g in range(1, 4):
        total = total + groups[160 * g + 128 : 160 * g + 160].astype(F32)
    flat = jnp.concatenate(
        [total[0:4] + total[4:8], total[16:20] + total[20:24]], axis=0
    ) * gscale
    for q in range(4):
        local_grad[pl.ds(q, 8, stride=4), :] = flat[:, 32 * q : 32 * (q + 1)]
    bias_grad[...] = ((total[8:9] + total[9:10]) * gscale)[:, :32]


def run(kernel, operands, outs, scratch, name, specs=None, out_specs=None):
    shapes = [jax.ShapeDtypeStruct(shape, dtype) for shape, dtype in outs]
    return pl.pallas_call(
        kernel,
        out_shape=shapes,
        in_specs=specs or [VM] * len(operands),
        out_specs=out_specs or [VM] * len(shapes),
        scratch_shapes=scratch,
        compiler_params=pltpu.CompilerParams(vmem_limit_bytes=16 * 1024 * 1024),
        cost_estimate=pl.CostEstimate(
            flops=200_000_000, bytes_accessed=1 << 20, transcendentals=0
        ),
        name=name,
    )(*operands)


def exchange(values, *shape):
    blocks = values.reshape((128,) + shape)
    return lax.all_to_all(blocks, GX, 0, 0, tiled=True).reshape(values.shape)


def local(field, cotangent, spectral_weight, local_weight, bias):
    ytab, forward, inverse = (jnp.asarray(table) for table in tables())
    same = jnp.asarray(np.kron(np.eye(4), np.ones((C, C))).astype(ml_dtypes.bfloat16))
    local_in = jnp.tile(local_weight, (4, 4)) * same
    local_out = jnp.tile(local_weight.T, (4, 4)) * same
    bias4 = jnp.tile(bias, 4)[:, None]
    slab = ((512, 128), BF16)
    slab_wide = ((1280, 128), BF16)
    held = pltpu.VMEM((512, 128), F32)
    held_wide = pltpu.VMEM((1280, 128), F32)
    quarters = pltpu.VMEM((4, 4, C, N), BF16)

    (send,) = run(
        y_kernel,
        (field, ytab),
        [slab],
        [held, quarters, pltpu.VMEM((128, N), BF16), pltpu.SemaphoreType.DMA((5,))],
        "y_forward",
        [ANY, ANY],
    )
    recv = exchange(send, 4, 128)
    weight = lax.all_gather(spectral_weight, "core", axis=0, tiled=True)
    send, first = run(
        mix_kernel,
        (recv, weight, forward, inverse),
        [slab, ((KX, 128), BF16)],
        [held],
        "mix",
    )
    recv = exchange(send, 4, 128)
    firsts = lax.all_gather(first, "core", axis=0, tiled=True)
    send, delta = run(
        point_kernel,
        (recv, field, cotangent, local_out, bias4, ytab),
        [slab_wide, ((4, 128, N), BF16)],
        [held, held_wide],
        "pointwise",
    )
    recv = exchange(send, 5, 2, 128)
    second, share = run(
        back_kernel,
        (recv, forward),
        [((2 * KX, 128), F32), ((KX + 16, 128), BF16)],
        [held_wide],
        "x_forward",
    )
    seconds = lax.all_gather(share, "core", axis=0, tiled=True)
    send, group = run(
        adjoint_kernel,
        (second, weight, inverse, firsts, seconds),
        [slab, ((160, 128), BF16)],
        [held, pltpu.VMEM((256, 1024), BF16), pltpu.VMEM((256, 1024), BF16)],
        "adjoint",
    )
    recv = exchange(send, 4, 128)
    groups = lax.all_gather(group, "gz", axis=0, tiled=True)
    (field_grad,) = run(
        grad_kernel,
        (recv, delta, local_in, ytab),
        [((8, 2, C, N), BF16)],
        [held, quarters, pltpu.SemaphoreType.DMA((4,))],
        "y_inverse",
        None,
        [ANY],
    )
    spectral_grad, local_grad, bias_grad = run(
        outer_kernel,
        (groups,),
        [((64, 2048), BF16), ((C, C), F32), ((1, C), F32)],
        [pltpu.VMEM((1024, 128), F32)],
        "outer",
    )
    return field_grad, spectral_grad, local_grad, bias_grad.reshape(C)


def solution(mesh):
    fine = Mesh(mesh.devices.reshape(8, 8, 2, 4), GX + ("gz",))
    cells = P(GX, "gz", None, None)
    return jax.shard_map(
        local,
        mesh=fine,
        in_specs=(cells, cells, P(GX, None), P(), P()),
        out_specs=(cells, P(GX, None), P(), P()),
        check_vma=False,
    )
```

time: 187 us -> 111 us (0.59)
  waiting for transfers between devices: 90.6 us -> 33.9 us
  between operations: 13.9 us -> 0.95 us
  local copies, waits for them, and re-layouts: 9.03 us -> 5.4 us
  starting transfers between devices: 39.2 us -> 36.8 us
  blocking collectives: 20.9 us -> 19 us
    all_gather x3 -> x0, waiting for transfers between devices: 69.1 us -> none  [the longest x1 31.5 us: local(): second_all = lax.all_gather(second, ('core', 'gz'), axis=0, tiled=True)]
    all_to_all x1 -> x0, blocking collectives: 18.2 us -> none  [exchange(): return lax.all_to_all(blocks, GX, 0, 0, tiled=True).reshape(128 * rows, 128)]
    all_gather x0 -> x3, blocking collectives: none -> 16.3 us  [the longest x1 10.4 us: local(): groups = lax.all_gather(group, 'gz', axis=0, tiled=True)]
    all_to_all x3 -> x4, waiting for transfers between devices: 20.7 us -> 33.9 us  [exchange(): return lax.all_to_all(blocks, GX, 0, 0, tiled=True).reshape(values.shape)]
    unnamed x32 -> x26, local copies, waits for them, and re-layouts: 8.59 us -> 4.97 us
    all_to_all x3 -> x4, starting transfers between devices: 39.1 us -> 36.8 us  [exchange(): return lax.all_to_all(blocks, GX, 0, 0, tiled=True).reshape(values.shape)]
  transfers between devices with their start and end apart: 6 -> 4, of which waited for: 5 -> 3; matrix products, arithmetic and copies ran while one was open for 0% -> 1% of each run, Pallas kernels for 3% -> 2%
where the time goes in v2:
time: 111 us; the launch traced here: 109 us
  starting transfers between devices  36.8 us (33%)
  waiting for transfers between devices  33.9 us (31%)
  blocking collectives  19 us (17%)
  Pallas kernels  12.9 us (12%)
  local copies, waits for them, and re-layouts  5.4 us (5%)
    all_to_all x4, starting transfers between devices, exchange(): return lax.all_to_all(blocks, GX, 0, 0, tiled=True).reshape(values.shape)  36.8 us
    all_to_all x4, waiting for transfers between devices, exchange(): return lax.all_to_all(blocks, GX, 0, 0, tiled=True).reshape(values.shape)  33.9 us
    pallas_call x7, Pallas kernels, run(): pl.pallas_call(kernel, out_shape=shapes, in_specs=specs or [VM] * len(ope...  12.9 us
    all_gather x1, blocking collectives, local(): groups = lax.all_gather(group, 'gz', axis=0, tiled=True)  10.4 us
    unnamed x26, local copies, waits for them, and re-layouts  4.97 us
    all_gather x1, blocking collectives, local(): seconds = lax.all_gather(share, 'core', axis=0, tiled=True)  3.34 us
    all_gather x1, blocking collectives, local(): weight = lax.all_gather(spectral_weight, 'core', axis=0, tiled=True)  2.7 us
    all_gather x1, blocking collectives, local(): firsts = lax.all_gather(first, 'core', axis=0, tiled=True)  2.51 us
  transfers between devices with their start and end apart: 4, of which 3 were waited for; matrix products, arithmetic and copies ran while one was open for 1% of the time, Pallas kernels for 2%

profile of v2, /device:TPU:1, one launch (start us, length us, event | category | flops | bytes accessed | tf_op | source)
XLA Modules:
  0.0 109.0 jit_solution(12948667676267616080)
XLA Ops:
  0.6 0.0 copy-start
  0.6 1.2 %copy-done = bf16[8,2,32,1024]{3,2,1,0:T(8,128)(2,1)S(1)} copy-done((bf16[8,2,32,1024]{3,2,1,0:T(8,128)(2,1)S(1)}, bf16[8,2,32,1024]{3,2,1,0:T(8,128)(2,1)}, u32[]{:S(2)}) %copy-start) | copy-done | bytes 1048600
  1.9 0.0 copy-start.2
  1.9 0.9 copy-done.2
  2.8 0.0 copy-start.9
  2.8 1.9 %y_forward.1 = bf16[512,128]{1,0:T(8,128)(2,1)} custom-call(bf16[8,2,32,1024]{3,2,1,0:T(8,128)(2,1)S(1)} %copy-done, bf16[128,1024]{1,0:T(8,128)(2,1)S(1)} %copy-done.2), custom_call_target="tpu_custom_call" | custom-call | flops 200000000 | bytes 1048576 | tf_op jit(solution)/shard_map/y_forward/pallas_call | solution.py:312
  4.8 0.0 copy-start.4
  4.8 0.0 copy-start.5
  4.8 18.6 %all-to-all-start = ((bf16[128,4,128]{2,1,0:T(4,128)(2,1)}), bf16[128,4,128]{2,1,0:T(4,128)(2,1)S(1)}, u32[]{:S(2)}, u32[]{:S(2)}) async-start(bf16[128,4,128]{2,1,0:T(4,128)(2,1)} %bitcast), calls=%async_computation | async-start | bytes 262144 | tf_op jit(solution)/shard_map/all_to_all | solution.py:328
  23.4 0.0 copy-done.9
  23.4 2.7 %all_gather.12.weight = bf16[128,2048]{1,0:T(8,128)(2,1)S(1)} all-gather(bf16[64,2048]{1,0:T(8,128)(2,1)S(1)} %copy-done.9), channel_id=1, replica_groups=mesh['y'=8,'z'=8,'core'=2,'gz'=4] {'core'}, dimensions={0}, use_global_device_ids=true | all-gather | bytes 786432 | tf_op jit(solution)/shard_map/all_gather | solution.py:352
  26.1 9.5 %all-to-all-done = bf16[128,4,128]{2,1,0:T(4,128)(2,1)S(1)} async-done(((bf16[128,4,128]{2,1,0:T(4,128)(2,1)}), bf16[128,4,128]{2,1,0:T(4,128)(2,1)S(1)}, u32[]{:S(2)}, u32[]{:S(2)}) %all-to-all-start) | async-done | bytes 131104 | tf_op jit(solution)/shard_map/all_to_all | solution.py:328
  35.6 0.0 copy-done.4
  35.6 0.0 copy-done.5
  35.6 0.0 copy-start.1
  35.6 2.1 %mix.1 = (bf16[512,128]{1,0:T(8,128)(2,1)}, bf16[128,128]{1,0:T(8,128)(2,1)S(1)}) custom-call(bf16[512,128]{1,0:T(8,128)(2,1)S(1)} %bitcast.13, bf16[128,2048]{1,0:T(8,128)(2,1)S(1)} %all_gather.12.weight, bf16[256,1024]{1,0:T(8,128)(2,1)S(1)} %copy-done.5, bf16[256,1024]{1,0:T(8,128)(2,1)S(1)} %copy-done.4), custom_call_target="tpu_custom_call" | custom-call | flops 200000000 | bytes 1048576 | tf_op jit(solution)/shard_map/mix/pallas_call | solution.py:312
  37.7 0.0 copy-start.11
  37.7 0.0 copy-start.10
  37.7 6.3 %all-to-all-start.1 = ((bf16[128,4,128]{2,1,0:T(4,128)(2,1)}), bf16[128,4,128]{2,1,0:T(4,128)(2,1)S(1)}, u32[]{:S(2)}, u32[]{:S(2)}) async-start(bf16[128,4,128]{2,1,0:T(4,128)(2,1)} %bitcast.2), calls=%async_computation.1 | async-start | bytes 262144 | tf_op jit(solution)/shard_map/all_to_all | solution.py:328
  44.0 0.0 copy-done.11
  44.0 0.0 copy-start.12
  44.1 0.1 copy.13
  44.1 0.6 copy-done.12
  44.7 0.1 broadcast_in_dim_tile.4.bias4
  44.8 0.0 copy-done.10
  44.8 0.0 copy-start.3
  44.8 0.1 broadcast_multiply_fusion
  45.0 0.1 reshape.48.local4
  45.1 11.2 %all-to-all-done.1 = bf16[128,4,128]{2,1,0:T(4,128)(2,1)S(1)} async-done(((bf16[128,4,128]{2,1,0:T(4,128)(2,1)}), bf16[128,4,128]{2,1,0:T(4,128)(2,1)S(1)}, u32[]{:S(2)}, u32[]{:S(2)}) %all-to-all-start.1) | async-done | bytes 131104 | tf_op jit(solution)/shard_map/all_to_all | solution.py:328
  56.3 0.0 copy-done.1
  56.3 0.0 copy-done.3
  56.3 0.0 copy-start.6
  56.4 1.2 %copy-done.6 = bf16[8,2,32,1024]{3,2,1,0:T(8,128)(2,1)S(1)} copy-done((bf16[8,2,32,1024]{3,2,1,0:T(8,128)(2,1)S(1)}, bf16[8,2,32,1024]{3,2,1,0:T(8,128)(2,1)}, u32[]{:S(2)}) %copy-start.6) | copy-done | bytes 1048600
  57.6 2.8 %pointwise.1 = (bf16[1280,128]{1,0:T(8,128)(2,1)}, bf16[4,128,1024]{2,1,0:T(8,128)(2,1)S(1)}) custom-call(bf16[512,128]{1,0:T(8,128)(2,1)S(1)} %bitcast.12, bf16[8,2,32,1024]{3,2,1,0:T(8,128)(2,1)S(1)} %copy-done.1, bf16[8,2,32,1024]{3,2,1,0:T(8,128)(2,1)S(1)} %copy-done.6, bf16[128,128]{1,0:T(8,128)(2,1)S(1)} %reshape.48.local4, ...), custom_call_target="tpu_custom_call" | custom-call | flops 200000000 | bytes 1048576 | tf_op jit(solution)/shard_map/pointwise/pallas_call | solution.py:312
  60.4 1.0 copy-done.7
  61.3 6.2 %all-to-all-start.2 = ((bf16[128,5,2,128]{3,2,1,0:T(2,128)(2,1)}), bf16[128,5,2,128]{3,2,1,0:T(2,128)(2,1)S(1)}, u32[]{:S(2)}, u32[]{:S(2)}) async-start(bf16[128,5,2,128]{3,2,1,0:T(2,128)(2,1)} %bitcast.5), calls=%async_computation.2 | async-start | bytes 655360 | tf_op jit(solution)/shard_map/all_to_all | solution.py:328
  67.5 2.5 %all_gather.13.firsts = bf16[256,128]{1,0:T(8,128)(2,1)S(1)} all-gather(bf16[128,128]{1,0:T(8,128)(2,1)S(1)} %get-tuple-element.18), channel_id=1, replica_groups=mesh['y'=8,'z'=8,'core'=2,'gz'=4] {'core'}, dimensions={0}, use_global_device_ids=true | all-gather | bytes 98304 | tf_op jit(solution)/shard_map/all_gather | solution.py:361
  70.1 13.2 %all-to-all-done.2 = bf16[128,5,2,128]{3,2,1,0:T(2,128)(2,1)S(1)} async-done(((bf16[128,5,2,128]{3,2,1,0:T(2,128)(2,1)}), bf16[128,5,2,128]{3,2,1,0:T(2,128)(2,1)S(1)}, u32[]{:S(2)}, u32[]{:S(2)}) %all-to-all-start.2) | async-done | bytes 327712 | tf_op jit(solution)/shard_map/all_to_all | solution.py:328
  83.2 0.5 x_forward.1
  83.7 3.3 %all_gather.14.seconds = bf16[288,128]{1,0:T(8,128)(2,1)S(1)} all-gather(bf16[144,128]{1,0:T(8,128)(2,1)S(1)} %get-tuple-element.19), channel_id=1, replica_groups=mesh['y'=8,'z'=8,'core'=2,'gz'=4] {'core'}, dimensions={0}, use_global_device_ids=true | all-gather | bytes 110592 | tf_op jit(solution)/shard_map/all_gather | solution.py:377
  87.1 1.9 %adjoint.1 = (bf16[512,128]{1,0:T(8,128)(2,1)}, bf16[160,128]{1,0:T(8,128)(2,1)S(1)}) custom-call(f32[256,128]{1,0:T(8,128)S(1)} %get-tuple-element.17.kept, bf16[128,2048]{1,0:T(8,128)(2,1)S(1)} %all_gather.12.weight, bf16[256,1024]{1,0:T(8,128)(2,1)S(1)} %copy-done.4, bf16[256,128]{1,0:T(8,128)(2,1)S(1)} %all_gather.13.firsts, ...), custom_call_target="tpu_custom_call" | custom-call | flops 200000000 | bytes 1048576 | tf_op jit(solution)/shard_map/adjoint/pallas_call | solution.py:312
  89.0 5.7 %all-to-all-start.3 = ((bf16[128,4,128]{2,1,0:T(4,128)(2,1)}), bf16[128,4,128]{2,1,0:T(4,128)(2,1)S(1)}, u32[]{:S(2)}, u32[]{:S(2)}) async-start(bf16[128,4,128]{2,1,0:T(4,128)(2,1)} %bitcast.7), calls=%async_computation.3 | async-start | bytes 262144 | tf_op jit(solution)/shard_map/all_to_all | solution.py:328
  94.6 0.1 reshape.50.local4
  94.8 10.4 %all_gather.15.groups = bf16[640,128]{1,0:T(8,128)(2,1)S(1)} all-gather(bf16[160,128]{1,0:T(8,128)(2,1)S(1)} %get-tuple-element.22), channel_id=1, replica_groups=mesh['y'=8,'z'=8,'core'=2,'gz'=4] {'gz'}, dimensions={0}, use_global_device_ids=true | all-gather | bytes 204800 | tf_op jit(solution)/shard_map/all_gather | solution.py:386
  105.2 2.4 %outer.1 = (bf16[64,2048]{1,0:T(8,128)(2,1)}, f32[32,32]{1,0:T(8,128)}, f32[1,32]{1,0:T(1,128)}) custom-call(bf16[640,128]{1,0:T(8,128)(2,1)S(1)} %all_gather.15.groups), custom_call_target="tpu_custom_call" | custom-call | flops 200000000 | bytes 1048576 | tf_op jit(solution)/shard_map/outer/pallas_call | solution.py:312
  107.5 0.0 all-to-all-done.3
  107.6 0.0 copy-done.8
  107.6 1.3 %y_inverse.1 = bf16[8,2,32,1024]{3,2,1,0:T(8,128)(2,1)} custom-call(bf16[512,128]{1,0:T(8,128)(2,1)S(1)} %bitcast.11, bf16[4,128,1024]{2,1,0:T(8,128)(2,1)S(1)} %copy-done.8, bf16[128,128]{1,0:T(8,128)(2,1)S(1)} %reshape.50.local4, bf16[128,1024]{1,0:T(8,128)(2,1)S(1)} %copy-done.3), custom_call_target="tpu_custom_call" | custom-call | flops 200000000 | bytes 1048576 | tf_op jit(solution)/shard_map/y_inverse/pallas_call | solution.py:312
  (3 shorter events, 0.0 us)
Async XLA Ops:
  0.6 1.2 %copy-start = (bf16[8,2,32,1024]{3,2,1,0:T(8,128)(2,1)S(1)}, bf16[8,2,32,1024]{3,2,1,0:T(8,128)(2,1)}, u32[]{:S(2)}) copy-start(bf16[8,2,32,1024]{3,2,1,0:T(8,128)(2,1)} %field.3) | copy-start | bytes 3145732
  1.9 0.9 copy-start.2
  2.8 20.6 %copy-start.9 = (bf16[64,2048]{1,0:T(8,128)(2,1)S(1)}, bf16[64,2048]{1,0:T(8,128)(2,1)}, u32[]{:S(2)}) copy-start(bf16[64,2048]{1,0:T(8,128)(2,1)} %param.11) | copy-start | bytes 786436
  4.8 30.8 %copy-start.4 = (bf16[256,1024]{1,0:T(8,128)(2,1)S(1)}, bf16[256,1024]{1,0:T(8,128)(2,1)}, u32[]{:S(2)}) copy-start(bf16[256,1024]{1,0:T(8,128)(2,1)} %constant.10.clone.inverse) | copy-start | bytes 1572868
  4.8 30.8 %copy-start.5 = (bf16[256,1024]{1,0:T(8,128)(2,1)S(1)}, bf16[256,1024]{1,0:T(8,128)(2,1)}, u32[]{:S(2)}) copy-start(bf16[256,1024]{1,0:T(8,128)(2,1)} %constant.9.clone.forward) | copy-start | bytes 1572868
  4.8 30.8 %all-to-all-start = ((bf16[128,4,128]{2,1,0:T(4,128)(2,1)}), bf16[128,4,128]{2,1,0:T(4,128)(2,1)S(1)}, u32[]{:S(2)}, u32[]{:S(2)}) async-start(bf16[128,4,128]{2,1,0:T(4,128)(2,1)} %bitcast), calls=%async_computation | async-start | bytes 262144 | tf_op jit(solution)/shard_map/all_to_all | solution.py:328
  35.6 20.8 %copy-start.1 = (bf16[8,2,32,1024]{3,2,1,0:T(8,128)(2,1)S(1)}, bf16[8,2,32,1024]{3,2,1,0:T(8,128)(2,1)}, u32[]{:S(2)}) copy-start(bf16[8,2,32,1024]{3,2,1,0:T(8,128)(2,1)} %field.3) | copy-start | bytes 3145732
  37.7 6.3 %copy-start.11 = (bf16[32,32]{1,0:T(8,128)(2,1)S(1)}, bf16[32,32]{1,0:T(8,128)(2,1)}, u32[]{:S(2)}) copy-start(bf16[32,32]{1,0:T(8,128)(2,1)} %param.12) | copy-start | bytes 6148
  37.7 7.1 %copy-start.10 = (bf16[4,32,4,32]{3,2,1,0:T(4,128)(2,1)S(1)}, bf16[4,32,4,32]{3,2,1,0:T(4,128)(2,1)}, u32[]{:S(2)}) copy-start(bf16[4,32,4,32]{3,2,1,0:T(4,128)(2,1)} %constant.15) | copy-start | bytes 98308
  37.7 18.6 %all-to-all-start.1 = ((bf16[128,4,128]{2,1,0:T(4,128)(2,1)}), bf16[128,4,128]{2,1,0:T(4,128)(2,1)S(1)}, u32[]{:S(2)}, u32[]{:S(2)}) async-start(bf16[128,4,128]{2,1,0:T(4,128)(2,1)} %bitcast.2), calls=%async_computation.1 | async-start | bytes 262144 | tf_op jit(solution)/shard_map/all_to_all | solution.py:328
  44.0 0.7 copy-start.12
  44.8 11.5 %copy-start.3 = (bf16[128,1024]{1,0:T(8,128)(2,1)S(1)}, bf16[128,1024]{1,0:T(8,128)(2,1)}, u32[]{:S(2)}) copy-start(bf16[128,1024]{1,0:T(8,128)(2,1)} %constant.8.clone.ytab) | copy-start | bytes 786436
  56.3 1.2 %copy-start.6 = (bf16[8,2,32,1024]{3,2,1,0:T(8,128)(2,1)S(1)}, bf16[8,2,32,1024]{3,2,1,0:T(8,128)(2,1)}, u32[]{:S(2)}) copy-start(bf16[8,2,32,1024]{3,2,1,0:T(8,128)(2,1)} %cotangent.1) | copy-start | bytes 3145732
  60.4 1.0 copy-start.7
  61.3 21.9 %all-to-all-start.2 = ((bf16[128,5,2,128]{3,2,1,0:T(2,128)(2,1)}), bf16[128,5,2,128]{3,2,1,0:T(2,128)(2,1)S(1)}, u32[]{:S(2)}, u32[]{:S(2)}) async-start(bf16[128,5,2,128]{3,2,1,0:T(2,128)(2,1)} %bitcast.5), calls=%async_computation.2 | async-start | bytes 655360 | tf_op jit(solution)/shard_map/all_to_all | solution.py:328
  87.1 20.5 %copy-start.8 = (bf16[4,128,1024]{2,1,0:T(8,128)(2,1)S(1)}, bf16[4,128,1024]{2,1,0:T(8,128)(2,1)}, u32[]{:S(2)}) copy-start(bf16[4,128,1024]{2,1,0:T(8,128)(2,1)} %copy-done.7) | copy-start | bytes 3145732
  89.0 18.6 %all-to-all-start.3 = ((bf16[128,4,128]{2,1,0:T(4,128)(2,1)}), bf16[128,4,128]{2,1,0:T(4,128)(2,1)S(1)}, u32[]{:S(2)}, u32[]{:S(2)}) async-start(bf16[128,4,128]{2,1,0:T(4,128)(2,1)} %bitcast.7), calls=%async_computation.3 | async-start | bytes 262144 | tf_op jit(solution)/shard_map/all_to_all | solution.py:328

commit v3 on v2

--- a/solution.py
+++ b/solution.py
@@ -16,7 +16,7 @@
 BF16 = jnp.bfloat16
 GX = ("y", "z", "core")
 VM = pl.BlockSpec(memory_space=pltpu.VMEM)
-ANY = pl.BlockSpec(memory_space=pl.ANY)
+HBM = pl.BlockSpec(memory_space=pltpu.HBM)
 
 
 def angles(freq, pos):
@@ -137,31 +137,40 @@
     send[...] = held[...].astype(BF16)
 
 
-def point_kernel(recv, field, cotangent, local4, bias4, ytab, send, delta, held, wide):
+def point_kernel(
+    recv, field, cotangent, local4, bias4, ytab, send, delta, held, wide, cots, grads, sems
+):
+    copies = []
+    for k in range(4):
+        part = cotangent.at[pl.ds(4 * (k % 2), 4), k // 2]
+        copies.append(pltpu.make_async_copy(part, cots.at[k], sems.at[k]))
+        copies[k].start()
     held[...] = recv[...].astype(F32)
     ones = jnp.ones((16, N), BF16)
-    total = jnp.zeros((128, 128), F32)
-    bias_total = jnp.zeros((16, 128), F32)
+    total = jnp.zeros((144, 128), F32)
     outs = []
-    for z in range(2):
-        for h in range(2):
-            spectrum = jnp.concatenate(
-                [held[pl.ds(4 * z + 2 * p + h, KY, stride=8), :] for p in range(2)], axis=0
-            )
-            left = jnp.concatenate([spectrum.T.astype(BF16), local4[...]], axis=1)
-            rows = field[4 * h : 4 * h + 4, z].reshape(128, N)
-            cot = cotangent[4 * h : 4 * h + 4, z].reshape(128, N)
-            for part in range(4):
-                cols = slice(256 * part, 256 * (part + 1))
-                right = jnp.concatenate([ytab[:, cols], rows[:, cols]], axis=0)
-                pre = nn(left, right) + bias4[...]
-                sig = 0.5 * jnp.tanh(0.5 * pre) + 0.5
-                slope = sig * (1.0 + pre * (1.0 - sig))
-                delta[2 * z + h, :, cols] = (cot[:, cols].astype(F32) * slope).astype(BF16)
-            grad = delta[2 * z + h]
-            outs.append((z, h, nt(ytab[...], grad)))
-            total = total + nt(rows, grad)
-            bias_total = bias_total + nt(ones, grad)
+    for k in range(4):
+        z, h = k // 2, k % 2
+        spectrum = jnp.concatenate(
+            [held[pl.ds(4 * z + 2 * p + h, KY, stride=8), :] for p in range(2)], axis=0
+        )
+        left = jnp.concatenate([spectrum.T.astype(BF16), local4[...]], axis=1)
+        rows = field[4 * h : 4 * h + 4, z].reshape(128, N)
+        copies[k].wait()
+        cot = cots[k].reshape(128, N)
+        for part in range(4):
+            cols = slice(256 * part, 256 * (part + 1))
+            right = jnp.concatenate([ytab[:, cols], rows[:, cols]], axis=0)
+            pre = nn(left, right) + bias4[...]
+            sig = 0.5 * jnp.tanh(0.5 * pre) + 0.5
+            slope = sig * (1.0 + pre * (1.0 - sig))
+            grads[k, :, cols] = (cot[:, cols].astype(F32) * slope).astype(BF16)
+        copies.append(pltpu.make_async_copy(grads.at[k], delta.at[k], sems.at[4 + k]))
+        copies[4 + k].start()
+        out = nt(jnp.concatenate([ytab[...], rows, ones], axis=0), grads[k])
+        outs.append((z, h, out[:128]))
+        total = total + out[128:]
+    bias_total = total[128:]
     block = block_of((32, 128))
     diag = jnp.zeros((32, 128), F32)
     for r in range(4):
@@ -188,6 +197,8 @@
         for k, line in enumerate(lines):
             wide[pl.ds(10 * z + 4 + k, KY, stride=20), :] = jnp.broadcast_to(line, (KY, 128))
     send[...] = wide[...].astype(BF16)
+    for copy in copies[4:]:
+        copy.wait()
 
 
 def back_kernel(recv, forward, kept, share, held):
@@ -346,7 +357,7 @@
         [slab],
         [held, quarters, pltpu.VMEM((128, N), BF16), pltpu.SemaphoreType.DMA((5,))],
         "y_forward",
-        [ANY, ANY],
+        [HBM, HBM],
     )
     recv = exchange(send, 4, 128)
     weight = lax.all_gather(spectral_weight, "core", axis=0, tiled=True)
@@ -363,8 +374,16 @@
         point_kernel,
         (recv, field, cotangent, local_out, bias4, ytab),
         [slab_wide, ((4, 128, N), BF16)],
-        [held, held_wide],
+        [
+            held,
+            held_wide,
+            quarters,
+            pltpu.VMEM((4, 128, N), BF16),
+            pltpu.SemaphoreType.DMA((8,)),
+        ],
         "pointwise",
+        [VM, VM, HBM, VM, VM, VM],
+        [VM, HBM],
     )
     recv = exchange(send, 5, 2, 128)
     second, share = run(
@@ -391,7 +410,7 @@
         [held, quarters, pltpu.SemaphoreType.DMA((4,))],
         "y_inverse",
         None,
-        [ANY],
+        [HBM],
     )
     spectral_grad, local_grad, bias_grad = run(
         outer_kernel,

time: 111 us -> 112 us (level)
  Pallas kernels: 12.9 us -> 14.4 us
    pallas_call x7, Pallas kernels: 12.9 us -> 14.4 us  [run(): pl.pallas_call(kernel, out_shape=shapes, in_specs=specs or [VM] * len(ope...]
where the time goes in v3:
time: 112 us; the launch traced here: 111 us
  starting transfers between devices  36.8 us (33%)
  waiting for transfers between devices  33.9 us (30%)
  blocking collectives  19 us (17%)
  Pallas kernels  14.4 us (13%)
  local copies, waits for them, and re-layouts  5.4 us (5%)
    all_to_all x4, starting transfers between devices, exchange(): return lax.all_to_all(blocks, GX, 0, 0, tiled=True).reshape(values.shape)  36.8 us
    all_to_all x4, waiting for transfers between devices, exchange(): return lax.all_to_all(blocks, GX, 0, 0, tiled=True).reshape(values.shape)  33.9 us
    pallas_call x7, Pallas kernels, run(): pl.pallas_call(kernel, out_shape=shapes, in_specs=specs or [VM] * len(ope...  14.4 us
    all_gather x1, blocking collectives, local(): groups = lax.all_gather(group, 'gz', axis=0, tiled=True)  10.4 us
    unnamed x26, local copies, waits for them, and re-layouts  4.96 us
    all_gather x1, blocking collectives, local(): seconds = lax.all_gather(share, 'core', axis=0, tiled=True)  3.34 us
    all_gather x1, blocking collectives, local(): weight = lax.all_gather(spectral_weight, 'core', axis=0, tiled=True)  2.7 us
    all_gather x1, blocking collectives, local(): firsts = lax.all_gather(first, 'core', axis=0, tiled=True)  2.51 us
  transfers between devices with their start and end apart: 4, of which 3 were waited for; matrix products, arithmetic and copies ran while one was open for 1% of the time, Pallas kernels for 2%

profile of v3, /device:TPU:1, one launch (start us, length us, event | category | flops | bytes accessed | tf_op | source)
XLA Modules:
  0.0 110.6 jit_solution(9168192116969176083)
XLA Ops:
  0.6 0.0 copy-start
  0.6 1.2 %copy-done = bf16[8,2,32,1024]{3,2,1,0:T(8,128)(2,1)S(1)} copy-done((bf16[8,2,32,1024]{3,2,1,0:T(8,128)(2,1)S(1)}, bf16[8,2,32,1024]{3,2,1,0:T(8,128)(2,1)}, u32[]{:S(2)}) %copy-start) | copy-done | bytes 1048600
  1.9 0.0 copy-start.2
  1.9 0.9 copy-done.2
  2.8 0.0 copy-start.9
  2.8 1.9 %y_forward.1 = bf16[512,128]{1,0:T(8,128)(2,1)} custom-call(bf16[8,2,32,1024]{3,2,1,0:T(8,128)(2,1)S(1)} %copy-done, bf16[128,1024]{1,0:T(8,128)(2,1)S(1)} %copy-done.2), custom_call_target="tpu_custom_call" | custom-call | flops 200000000 | bytes 1048576 | tf_op jit(solution)/shard_map/y_forward/pallas_call | solution.py:323
  4.8 0.0 copy-start.4
  4.8 0.0 copy-start.5
  4.8 18.6 %all-to-all-start = ((bf16[128,4,128]{2,1,0:T(4,128)(2,1)}), bf16[128,4,128]{2,1,0:T(4,128)(2,1)S(1)}, u32[]{:S(2)}, u32[]{:S(2)}) async-start(bf16[128,4,128]{2,1,0:T(4,128)(2,1)} %bitcast), calls=%async_computation | async-start | bytes 262144 | tf_op jit(solution)/shard_map/all_to_all | solution.py:339
  23.4 0.0 copy-done.9
  23.4 2.7 %all_gather.12.weight = bf16[128,2048]{1,0:T(8,128)(2,1)S(1)} all-gather(bf16[64,2048]{1,0:T(8,128)(2,1)S(1)} %copy-done.9), channel_id=1, replica_groups=mesh['y'=8,'z'=8,'core'=2,'gz'=4] {'core'}, dimensions={0}, use_global_device_ids=true | all-gather | bytes 786432 | tf_op jit(solution)/shard_map/all_gather | solution.py:363
  26.1 9.5 %all-to-all-done = bf16[128,4,128]{2,1,0:T(4,128)(2,1)S(1)} async-done(((bf16[128,4,128]{2,1,0:T(4,128)(2,1)}), bf16[128,4,128]{2,1,0:T(4,128)(2,1)S(1)}, u32[]{:S(2)}, u32[]{:S(2)}) %all-to-all-start) | async-done | bytes 131104 | tf_op jit(solution)/shard_map/all_to_all | solution.py:339
  35.6 0.0 copy-done.4
  35.6 0.0 copy-done.5
  35.6 0.0 copy-start.1
  35.6 2.1 %mix.1 = (bf16[512,128]{1,0:T(8,128)(2,1)}, bf16[128,128]{1,0:T(8,128)(2,1)S(1)}) custom-call(bf16[512,128]{1,0:T(8,128)(2,1)S(1)} %bitcast.13, bf16[128,2048]{1,0:T(8,128)(2,1)S(1)} %all_gather.12.weight, bf16[256,1024]{1,0:T(8,128)(2,1)S(1)} %copy-done.5, bf16[256,1024]{1,0:T(8,128)(2,1)S(1)} %copy-done.4), custom_call_target="tpu_custom_call" | custom-call | flops 200000000 | bytes 1048576 | tf_op jit(solution)/shard_map/mix/pallas_call | solution.py:323
  37.7 0.0 copy-start.11
  37.7 0.0 copy-start.10
  37.7 6.3 %all-to-all-start.1 = ((bf16[128,4,128]{2,1,0:T(4,128)(2,1)}), bf16[128,4,128]{2,1,0:T(4,128)(2,1)S(1)}, u32[]{:S(2)}, u32[]{:S(2)}) async-start(bf16[128,4,128]{2,1,0:T(4,128)(2,1)} %bitcast.2), calls=%async_computation.1 | async-start | bytes 262144 | tf_op jit(solution)/shard_map/all_to_all | solution.py:339
  44.0 0.0 copy-done.11
  44.0 0.0 copy-start.12
  44.1 0.1 copy.13
  44.1 0.6 copy-done.12
  44.7 0.1 broadcast_in_dim_tile.4.bias4
  44.8 0.0 copy-done.10
  44.8 0.0 copy-start.3
  44.8 0.1 broadcast_multiply_fusion
  45.0 0.1 reshape.48.local4
  45.1 11.2 %all-to-all-done.1 = bf16[128,4,128]{2,1,0:T(4,128)(2,1)S(1)} async-done(((bf16[128,4,128]{2,1,0:T(4,128)(2,1)}), bf16[128,4,128]{2,1,0:T(4,128)(2,1)S(1)}, u32[]{:S(2)}, u32[]{:S(2)}) %all-to-all-start.1) | async-done | bytes 131104 | tf_op jit(solution)/shard_map/all_to_all | solution.py:339
  56.3 0.0 copy-done.1
  56.3 0.0 copy-done.3
  56.4 1.2 %copy-done.6 = bf16[8,2,32,1024]{3,2,1,0:T(8,128)(2,1)S(1)} copy-done((bf16[8,2,32,1024]{3,2,1,0:T(8,128)(2,1)S(1)}, bf16[8,2,32,1024]{3,2,1,0:T(8,128)(2,1)}, u32[]{:S(2)}) %copy-start.6) | copy-done | bytes 1048600
  57.6 4.3 %pointwise.1 = (bf16[1280,128]{1,0:T(8,128)(2,1)}, bf16[4,128,1024]{2,1,0:T(8,128)(2,1)S(1)}) custom-call(bf16[512,128]{1,0:T(8,128)(2,1)S(1)} %bitcast.12, bf16[8,2,32,1024]{3,2,1,0:T(8,128)(2,1)S(1)} %copy-done.1, bf16[8,2,32,1024]{3,2,1,0:T(8,128)(2,1)S(1)} %copy-done.6, bf16[128,128]{1,0:T(8,128)(2,1)S(1)} %reshape.48.local4, ...), custom_call_target="tpu_custom_call" | custom-call | flops 200000000 | bytes 1048576 | tf_op jit(solution)/shard_map/pointwise/pallas_call | solution.py:323
  61.9 0.0 copy-start.7
  61.9 1.0 copy-done.7
  62.9 6.2 %all-to-all-start.2 = ((bf16[128,5,2,128]{3,2,1,0:T(2,128)(2,1)}), bf16[128,5,2,128]{3,2,1,0:T(2,128)(2,1)S(1)}, u32[]{:S(2)}, u32[]{:S(2)}) async-start(bf16[128,5,2,128]{3,2,1,0:T(2,128)(2,1)} %bitcast.5), calls=%async_computation.2 | async-start | bytes 655360 | tf_op jit(solution)/shard_map/all_to_all | solution.py:339
  69.1 2.5 %all_gather.13.firsts = bf16[256,128]{1,0:T(8,128)(2,1)S(1)} all-gather(bf16[128,128]{1,0:T(8,128)(2,1)S(1)} %get-tuple-element.18), channel_id=1, replica_groups=mesh['y'=8,'z'=8,'core'=2,'gz'=4] {'core'}, dimensions={0}, use_global_device_ids=true | all-gather | bytes 98304 | tf_op jit(solution)/shard_map/all_gather | solution.py:372
  71.6 13.2 %all-to-all-done.2 = bf16[128,5,2,128]{3,2,1,0:T(2,128)(2,1)S(1)} async-done(((bf16[128,5,2,128]{3,2,1,0:T(2,128)(2,1)}), bf16[128,5,2,128]{3,2,1,0:T(2,128)(2,1)S(1)}, u32[]{:S(2)}, u32[]{:S(2)}) %all-to-all-start.2) | async-done | bytes 327712 | tf_op jit(solution)/shard_map/all_to_all | solution.py:339
  84.8 0.5 x_forward.1
  85.3 3.3 %all_gather.14.seconds = bf16[288,128]{1,0:T(8,128)(2,1)S(1)} all-gather(bf16[144,128]{1,0:T(8,128)(2,1)S(1)} %get-tuple-element.19), channel_id=1, replica_groups=mesh['y'=8,'z'=8,'core'=2,'gz'=4] {'core'}, dimensions={0}, use_global_device_ids=true | all-gather | bytes 110592 | tf_op jit(solution)/shard_map/all_gather | solution.py:396
  88.6 1.9 %adjoint.1 = (bf16[512,128]{1,0:T(8,128)(2,1)}, bf16[160,128]{1,0:T(8,128)(2,1)S(1)}) custom-call(f32[256,128]{1,0:T(8,128)S(1)} %get-tuple-element.17.kept, bf16[128,2048]{1,0:T(8,128)(2,1)S(1)} %all_gather.12.weight, bf16[256,1024]{1,0:T(8,128)(2,1)S(1)} %copy-done.4, bf16[256,128]{1,0:T(8,128)(2,1)S(1)} %all_gather.13.firsts, ...), custom_call_target="tpu_custom_call" | custom-call | flops 200000000 | bytes 1048576 | tf_op jit(solution)/shard_map/adjoint/pallas_call | solution.py:323
  90.5 5.7 %all-to-all-start.3 = ((bf16[128,4,128]{2,1,0:T(4,128)(2,1)}), bf16[128,4,128]{2,1,0:T(4,128)(2,1)S(1)}, u32[]{:S(2)}, u32[]{:S(2)}) async-start(bf16[128,4,128]{2,1,0:T(4,128)(2,1)} %bitcast.7), calls=%async_computation.3 | async-start | bytes 262144 | tf_op jit(solution)/shard_map/all_to_all | solution.py:339
  96.2 0.1 reshape.50.local4
  96.3 10.4 %all_gather.15.groups = bf16[640,128]{1,0:T(8,128)(2,1)S(1)} all-gather(bf16[160,128]{1,0:T(8,128)(2,1)S(1)} %get-tuple-element.22), channel_id=1, replica_groups=mesh['y'=8,'z'=8,'core'=2,'gz'=4] {'gz'}, dimensions={0}, use_global_device_ids=true | all-gather | bytes 204800 | tf_op jit(solution)/shard_map/all_gather | solution.py:405
  106.7 2.4 %outer.1 = (bf16[64,2048]{1,0:T(8,128)(2,1)}, f32[32,32]{1,0:T(8,128)}, f32[1,32]{1,0:T(1,128)}) custom-call(bf16[640,128]{1,0:T(8,128)(2,1)S(1)} %all_gather.15.groups), custom_call_target="tpu_custom_call" | custom-call | flops 200000000 | bytes 1048576 | tf_op jit(solution)/shard_map/outer/pallas_call | solution.py:323
  109.1 0.0 all-to-all-done.3
  109.1 0.0 copy-done.8
  109.1 1.3 %y_inverse.1 = bf16[8,2,32,1024]{3,2,1,0:T(8,128)(2,1)} custom-call(bf16[512,128]{1,0:T(8,128)(2,1)S(1)} %bitcast.11, bf16[4,128,1024]{2,1,0:T(8,128)(2,1)S(1)} %copy-done.8, bf16[128,128]{1,0:T(8,128)(2,1)S(1)} %reshape.50.local4, bf16[128,1024]{1,0:T(8,128)(2,1)S(1)} %copy-done.3), custom_call_target="tpu_custom_call" | custom-call | flops 200000000 | bytes 1048576 | tf_op jit(solution)/shard_map/y_inverse/pallas_call | solution.py:323
  (3 shorter events, 0.0 us)
Async XLA Ops:
  0.6 1.2 %copy-start = (bf16[8,2,32,1024]{3,2,1,0:T(8,128)(2,1)S(1)}, bf16[8,2,32,1024]{3,2,1,0:T(8,128)(2,1)}, u32[]{:S(2)}) copy-start(bf16[8,2,32,1024]{3,2,1,0:T(8,128)(2,1)} %field.3) | copy-start | bytes 3145732
  1.9 0.9 copy-start.2
  2.8 20.6 %copy-start.9 = (bf16[64,2048]{1,0:T(8,128)(2,1)S(1)}, bf16[64,2048]{1,0:T(8,128)(2,1)}, u32[]{:S(2)}) copy-start(bf16[64,2048]{1,0:T(8,128)(2,1)} %param.11) | copy-start | bytes 786436
  4.8 30.8 %copy-start.4 = (bf16[256,1024]{1,0:T(8,128)(2,1)S(1)}, bf16[256,1024]{1,0:T(8,128)(2,1)}, u32[]{:S(2)}) copy-start(bf16[256,1024]{1,0:T(8,128)(2,1)} %constant.10.clone.inverse) | copy-start | bytes 1572868
  4.8 30.8 %copy-start.5 = (bf16[256,1024]{1,0:T(8,128)(2,1)S(1)}, bf16[256,1024]{1,0:T(8,128)(2,1)}, u32[]{:S(2)}) copy-start(bf16[256,1024]{1,0:T(8,128)(2,1)} %constant.9.clone.forward) | copy-start | bytes 1572868
  4.8 30.8 %all-to-all-start = ((bf16[128,4,128]{2,1,0:T(4,128)(2,1)}), bf16[128,4,128]{2,1,0:T(4,128)(2,1)S(1)}, u32[]{:S(2)}, u32[]{:S(2)}) async-start(bf16[128,4,128]{2,1,0:T(4,128)(2,1)} %bitcast), calls=%async_computation | async-start | bytes 262144 | tf_op jit(solution)/shard_map/all_to_all | solution.py:339
  35.6 20.8 %copy-start.1 = (bf16[8,2,32,1024]{3,2,1,0:T(8,128)(2,1)S(1)}, bf16[8,2,32,1024]{3,2,1,0:T(8,128)(2,1)}, u32[]{:S(2)}) copy-start(bf16[8,2,32,1024]{3,2,1,0:T(8,128)(2,1)} %field.3) | copy-start | bytes 3145732
  37.7 6.3 %copy-start.11 = (bf16[32,32]{1,0:T(8,128)(2,1)S(1)}, bf16[32,32]{1,0:T(8,128)(2,1)}, u32[]{:S(2)}) copy-start(bf16[32,32]{1,0:T(8,128)(2,1)} %param.12) | copy-start | bytes 6148
  37.7 7.1 %copy-start.10 = (bf16[4,32,4,32]{3,2,1,0:T(4,128)(2,1)S(1)}, bf16[4,32,4,32]{3,2,1,0:T(4,128)(2,1)}, u32[]{:S(2)}) copy-start(bf16[4,32,4,32]{3,2,1,0:T(4,128)(2,1)} %constant.15) | copy-start | bytes 98308
  37.7 18.6 %all-to-all-start.1 = ((bf16[128,4,128]{2,1,0:T(4,128)(2,1)}), bf16[128,4,128]{2,1,0:T(4,128)(2,1)S(1)}, u32[]{:S(2)}, u32[]{:S(2)}) async-start(bf16[128,4,128]{2,1,0:T(4,128)(2,1)} %bitcast.2), calls=%async_computation.1 | async-start | bytes 262144 | tf_op jit(solution)/shard_map/all_to_all | solution.py:339
  44.0 0.7 copy-start.12
  44.8 11.5 %copy-start.3 = (bf16[128,1024]{1,0:T(8,128)(2,1)S(1)}, bf16[128,1024]{1,0:T(8,128)(2,1)}, u32[]{:S(2)}) copy-start(bf16[128,1024]{1,0:T(8,128)(2,1)} %constant.8.clone.ytab) | copy-start | bytes 786436
  56.3 1.2 %copy-start.6 = (bf16[8,2,32,1024]{3,2,1,0:T(8,128)(2,1)S(1)}, bf16[8,2,32,1024]{3,2,1,0:T(8,128)(2,1)}, u32[]{:S(2)}) copy-start(bf16[8,2,32,1024]{3,2,1,0:T(8,128)(2,1)} %cotangent.1) | copy-start | bytes 3145732
  61.9 1.0 copy-start.7
  62.9 21.9 %all-to-all-start.2 = ((bf16[128,5,2,128]{3,2,1,0:T(2,128)(2,1)}), bf16[128,5,2,128]{3,2,1,0:T(2,128)(2,1)S(1)}, u32[]{:S(2)}, u32[]{:S(2)}) async-start(bf16[128,5,2,128]{3,2,1,0:T(2,128)(2,1)} %bitcast.5), calls=%async_computation.2 | async-start | bytes 655360 | tf_op jit(solution)/shard_map/all_to_all | solution.py:339
  88.6 20.5 %copy-start.8 = (bf16[4,128,1024]{2,1,0:T(8,128)(2,1)S(1)}, bf16[4,128,1024]{2,1,0:T(8,128)(2,1)}, u32[]{:S(2)}) copy-start(bf16[4,128,1024]{2,1,0:T(8,128)(2,1)} %copy-done.7) | copy-start | bytes 3145732
  90.5 18.6 %all-to-all-start.3 = ((bf16[128,4,128]{2,1,0:T(4,128)(2,1)}), bf16[128,4,128]{2,1,0:T(4,128)(2,1)S(1)}, u32[]{:S(2)}, u32[]{:S(2)}) async-start(bf16[128,4,128]{2,1,0:T(4,128)(2,1)} %bitcast.7), calls=%async_computation.3 | async-start | bytes 262144 | tf_op jit(solution)/shard_map/all_to_all | solution.py:339

commit v4 on v3

--- a/solution.py
+++ b/solution.py
@@ -319,12 +319,20 @@
 
 
 def run(kernel, operands, outs, scratch, name, specs=None, out_specs=None):
-    shapes = [jax.ShapeDtypeStruct(shape, dtype) for shape, dtype in outs]
+    specs = specs or [VM] * len(operands)
+    out_specs = out_specs or [VM] * len(outs)
+    operands = [
+        pltpu.with_memory_space_constraint(operand, pltpu.HBM) if spec is HBM else operand
+        for operand, spec in zip(operands, specs)
+    ]
     return pl.pallas_call(
         kernel,
-        out_shape=shapes,
-        in_specs=specs or [VM] * len(operands),
-        out_specs=out_specs or [VM] * len(shapes),
+        out_shape=[
+            (pltpu.HBM if spec is HBM else jax.ShapeDtypeStruct)(*out)
+            for out, spec in zip(outs, out_specs)
+        ],
+        in_specs=specs,
+        out_specs=out_specs,
         scratch_shapes=scratch,
         compiler_params=pltpu.CompilerParams(vmem_limit_bytes=16 * 1024 * 1024),
         cost_estimate=pl.CostEstimate(

time: 112 us -> 109 us (0.973)
  local copies, waits for them, and re-layouts: 5.4 us -> 1.04 us
  Pallas kernels: 14.4 us -> 16 us
    unnamed x26 -> x18, local copies, waits for them, and re-layouts: 4.96 us -> 0.6 us
    pallas_call x7, Pallas kernels: 14.4 us -> 16 us  [run(): pl.pallas_call(kernel, out_shape=[(pltpu.HBM if spec is HBM else jax.Shap...]
where the time goes in v4:
time: 109 us; the launch traced here: 108 us
  starting transfers between devices  36.7 us (34%)
  waiting for transfers between devices  33.9 us (31%)
  blocking collectives  19 us (17%)
  Pallas kernels  16 us (15%)
    all_to_all x4, starting transfers between devices, exchange(): return lax.all_to_all(blocks, GX, 0, 0, tiled=True).reshape(values.shape)  36.7 us
    all_to_all x4, waiting for transfers between devices, exchange(): return lax.all_to_all(blocks, GX, 0, 0, tiled=True).reshape(values.shape)  33.9 us
    pallas_call x7, Pallas kernels, run(): pl.pallas_call(kernel, out_shape=[(pltpu.HBM if spec is HBM else jax.Shap...  16 us
    all_gather x1, blocking collectives, local(): groups = lax.all_gather(group, 'gz', axis=0, tiled=True)  10.4 us
    all_gather x1, blocking collectives, local(): seconds = lax.all_gather(share, 'core', axis=0, tiled=True)  3.34 us
    all_gather x1, blocking collectives, local(): weight = lax.all_gather(spectral_weight, 'core', axis=0, tiled=True)  2.7 us
    all_gather x1, blocking collectives, local(): firsts = lax.all_gather(first, 'core', axis=0, tiled=True)  2.51 us
  transfers between devices with their start and end apart: 4, of which 3 were waited for; matrix products, arithmetic and copies ran while one was open for 1% of the time, Pallas kernels for 2%

profile of v4, /device:TPU:1, one launch (start us, length us, event | category | flops | bytes accessed | tf_op | source)
XLA Modules:
  0.0 107.7 jit_solution(2252296065549906471)
XLA Ops:
  0.6 0.0 copy-start.5
  0.6 2.9 %y_forward.1 = bf16[512,128]{1,0:T(8,128)(2,1)} custom-call(bf16[8,2,32,1024]{3,2,1,0:T(8,128)(2,1)} %field.3, bf16[128,1024]{1,0:T(8,128)(2,1)} %constant.8.clone.ytab), custom_call_target="tpu_custom_call" | custom-call | flops 200000000 | bytes 1048576 | tf_op jit(solution)/shard_map/y_forward/pallas_call | solution.py:328
  3.6 0.0 copy-start.2
  3.6 0.0 copy-start.3
  3.6 18.6 %all-to-all-start = ((bf16[128,4,128]{2,1,0:T(4,128)(2,1)}), bf16[128,4,128]{2,1,0:T(4,128)(2,1)S(1)}, u32[]{:S(2)}, u32[]{:S(2)}) async-start(bf16[128,4,128]{2,1,0:T(4,128)(2,1)} %bitcast), calls=%async_computation | async-start | bytes 262144 | tf_op jit(solution)/shard_map/all_to_all | solution.py:347
  22.2 0.0 copy-done.5
  22.2 2.7 %all_gather.12.weight = bf16[128,2048]{1,0:T(8,128)(2,1)S(1)} all-gather(bf16[64,2048]{1,0:T(8,128)(2,1)S(1)} %copy-done.5), channel_id=1, replica_groups=mesh['y'=8,'z'=8,'core'=2,'gz'=4] {'core'}, dimensions={0}, use_global_device_ids=true | all-gather | bytes 786432 | tf_op jit(solution)/shard_map/all_gather | solution.py:371
  24.9 9.5 %all-to-all-done = bf16[128,4,128]{2,1,0:T(4,128)(2,1)S(1)} async-done(((bf16[128,4,128]{2,1,0:T(4,128)(2,1)}), bf16[128,4,128]{2,1,0:T(4,128)(2,1)S(1)}, u32[]{:S(2)}, u32[]{:S(2)}) %all-to-all-start) | async-done | bytes 131104 | tf_op jit(solution)/shard_map/all_to_all | solution.py:347
  34.4 0.0 copy-done.2
  34.4 0.0 copy-done.3
  34.4 0.0 copy-start
  34.4 2.1 %mix.1 = (bf16[512,128]{1,0:T(8,128)(2,1)}, bf16[128,128]{1,0:T(8,128)(2,1)S(1)}) custom-call(bf16[512,128]{1,0:T(8,128)(2,1)S(1)} %bitcast.13, bf16[128,2048]{1,0:T(8,128)(2,1)S(1)} %all_gather.12.weight, bf16[256,1024]{1,0:T(8,128)(2,1)S(1)} %copy-done.3, bf16[256,1024]{1,0:T(8,128)(2,1)S(1)} %copy-done.2), custom_call_target="tpu_custom_call" | custom-call | flops 200000000 | bytes 1048576 | tf_op jit(solution)/shard_map/mix/pallas_call | solution.py:328
  36.5 0.0 copy-start.7
  36.5 0.0 copy-start.6
  36.5 6.3 %all-to-all-start.1 = ((bf16[128,4,128]{2,1,0:T(4,128)(2,1)}), bf16[128,4,128]{2,1,0:T(4,128)(2,1)S(1)}, u32[]{:S(2)}, u32[]{:S(2)}) async-start(bf16[128,4,128]{2,1,0:T(4,128)(2,1)} %bitcast.2), calls=%async_computation.1 | async-start | bytes 262144 | tf_op jit(solution)/shard_map/all_to_all | solution.py:347
  42.8 0.0 copy-done.7
  42.9 0.0 copy-start.8
  42.9 0.1 copy.13
  43.0 0.6 copy-done.8
  43.5 0.1 broadcast_in_dim_tile.4.bias4
  43.6 0.0 copy-done.6
  43.6 0.0 copy-start.1
  43.7 0.1 broadcast_multiply_fusion
  43.8 0.1 reshape.48.local4
  43.9 11.2 %all-to-all-done.1 = bf16[128,4,128]{2,1,0:T(4,128)(2,1)S(1)} async-done(((bf16[128,4,128]{2,1,0:T(4,128)(2,1)}), bf16[128,4,128]{2,1,0:T(4,128)(2,1)S(1)}, u32[]{:S(2)}, u32[]{:S(2)}) %all-to-all-start.1) | async-done | bytes 131104 | tf_op jit(solution)/shard_map/all_to_all | solution.py:347
  55.2 0.0 copy-done
  55.2 0.0 copy-done.1
  55.2 4.9 %pointwise.1 = (bf16[1280,128]{1,0:T(8,128)(2,1)}, bf16[4,128,1024]{2,1,0:T(8,128)(2,1)}) custom-call(bf16[512,128]{1,0:T(8,128)(2,1)S(1)} %bitcast.12, bf16[8,2,32,1024]{3,2,1,0:T(8,128)(2,1)S(1)} %copy-done, bf16[8,2,32,1024]{3,2,1,0:T(8,128)(2,1)} %cotangent.1, bf16[128,128]{1,0:T(8,128)(2,1)S(1)} %reshape.48.local4, ...), custom_call_target="tpu_custom_call" | custom-call | flops 200000000 | bytes 1048576 | tf_op jit(solution)/shard_map/pointwise/pallas_call | solution.py:328
  60.1 6.2 %all-to-all-start.2 = ((bf16[128,5,2,128]{3,2,1,0:T(2,128)(2,1)}), bf16[128,5,2,128]{3,2,1,0:T(2,128)(2,1)S(1)}, u32[]{:S(2)}, u32[]{:S(2)}) async-start(bf16[128,5,2,128]{3,2,1,0:T(2,128)(2,1)} %bitcast.5), calls=%async_computation.2 | async-start | bytes 655360 | tf_op jit(solution)/shard_map/all_to_all | solution.py:347
  66.3 2.5 %all_gather.13.firsts = bf16[256,128]{1,0:T(8,128)(2,1)S(1)} all-gather(bf16[128,128]{1,0:T(8,128)(2,1)S(1)} %get-tuple-element.18), channel_id=1, replica_groups=mesh['y'=8,'z'=8,'core'=2,'gz'=4] {'core'}, dimensions={0}, use_global_device_ids=true | all-gather | bytes 98304 | tf_op jit(solution)/shard_map/all_gather | solution.py:380
  68.8 13.2 %all-to-all-done.2 = bf16[128,5,2,128]{3,2,1,0:T(2,128)(2,1)S(1)} async-done(((bf16[128,5,2,128]{3,2,1,0:T(2,128)(2,1)}), bf16[128,5,2,128]{3,2,1,0:T(2,128)(2,1)S(1)}, u32[]{:S(2)}, u32[]{:S(2)}) %all-to-all-start.2) | async-done | bytes 327712 | tf_op jit(solution)/shard_map/all_to_all | solution.py:347
  82.0 0.5 x_forward.1
  82.5 3.3 %all_gather.14.seconds = bf16[288,128]{1,0:T(8,128)(2,1)S(1)} all-gather(bf16[144,128]{1,0:T(8,128)(2,1)S(1)} %get-tuple-element.19), channel_id=1, replica_groups=mesh['y'=8,'z'=8,'core'=2,'gz'=4] {'core'}, dimensions={0}, use_global_device_ids=true | all-gather | bytes 110592 | tf_op jit(solution)/shard_map/all_gather | solution.py:404
  85.8 0.0 copy-start.4
  85.8 1.9 %adjoint.1 = (bf16[512,128]{1,0:T(8,128)(2,1)}, bf16[160,128]{1,0:T(8,128)(2,1)S(1)}) custom-call(f32[256,128]{1,0:T(8,128)S(1)} %get-tuple-element.17.kept, bf16[128,2048]{1,0:T(8,128)(2,1)S(1)} %all_gather.12.weight, bf16[256,1024]{1,0:T(8,128)(2,1)S(1)} %copy-done.2, bf16[256,128]{1,0:T(8,128)(2,1)S(1)} %all_gather.13.firsts, ...), custom_call_target="tpu_custom_call" | custom-call | flops 200000000 | bytes 1048576 | tf_op jit(solution)/shard_map/adjoint/pallas_call | solution.py:328
  87.7 5.7 %all-to-all-start.3 = ((bf16[128,4,128]{2,1,0:T(4,128)(2,1)}), bf16[128,4,128]{2,1,0:T(4,128)(2,1)S(1)}, u32[]{:S(2)}, u32[]{:S(2)}) async-start(bf16[128,4,128]{2,1,0:T(4,128)(2,1)} %bitcast.7), calls=%async_computation.3 | async-start | bytes 262144 | tf_op jit(solution)/shard_map/all_to_all | solution.py:347
  93.3 0.1 reshape.50.local4
  93.5 10.4 %all_gather.15.groups = bf16[640,128]{1,0:T(8,128)(2,1)S(1)} all-gather(bf16[160,128]{1,0:T(8,128)(2,1)S(1)} %get-tuple-element.22), channel_id=1, replica_groups=mesh['y'=8,'z'=8,'core'=2,'gz'=4] {'gz'}, dimensions={0}, use_global_device_ids=true | all-gather | bytes 204800 | tf_op jit(solution)/shard_map/all_gather | solution.py:413
  103.9 2.4 %outer.1 = (bf16[64,2048]{1,0:T(8,128)(2,1)}, f32[32,32]{1,0:T(8,128)}, f32[1,32]{1,0:T(1,128)}) custom-call(bf16[640,128]{1,0:T(8,128)(2,1)S(1)} %all_gather.15.groups), custom_call_target="tpu_custom_call" | custom-call | flops 200000000 | bytes 1048576 | tf_op jit(solution)/shard_map/outer/pallas_call | solution.py:328
  106.3 0.0 all-to-all-done.3
  106.3 0.0 copy-done.4
  106.3 1.3 %y_inverse.1 = bf16[8,2,32,1024]{3,2,1,0:T(8,128)(2,1)} custom-call(bf16[512,128]{1,0:T(8,128)(2,1)S(1)} %bitcast.11, bf16[4,128,1024]{2,1,0:T(8,128)(2,1)S(1)} %copy-done.4, bf16[128,128]{1,0:T(8,128)(2,1)S(1)} %reshape.50.local4, bf16[128,1024]{1,0:T(8,128)(2,1)S(1)} %copy-done.1), custom_call_target="tpu_custom_call" | custom-call | flops 200000000 | bytes 1048576 | tf_op jit(solution)/shard_map/y_inverse/pallas_call | solution.py:328
  (1 shorter events, 0.0 us)
Async XLA Ops:
  0.6 21.5 %copy-start.5 = (bf16[64,2048]{1,0:T(8,128)(2,1)S(1)}, bf16[64,2048]{1,0:T(8,128)(2,1)}, u32[]{:S(2)}) copy-start(bf16[64,2048]{1,0:T(8,128)(2,1)} %param.11) | copy-start | bytes 786436
  3.6 30.8 %copy-start.2 = (bf16[256,1024]{1,0:T(8,128)(2,1)S(1)}, bf16[256,1024]{1,0:T(8,128)(2,1)}, u32[]{:S(2)}) copy-start(bf16[256,1024]{1,0:T(8,128)(2,1)} %constant.10.clone.inverse) | copy-start | bytes 1572868
  3.6 30.8 %copy-start.3 = (bf16[256,1024]{1,0:T(8,128)(2,1)S(1)}, bf16[256,1024]{1,0:T(8,128)(2,1)}, u32[]{:S(2)}) copy-start(bf16[256,1024]{1,0:T(8,128)(2,1)} %constant.9.clone.forward) | copy-start | bytes 1572868
  3.6 30.8 %all-to-all-start = ((bf16[128,4,128]{2,1,0:T(4,128)(2,1)}), bf16[128,4,128]{2,1,0:T(4,128)(2,1)S(1)}, u32[]{:S(2)}, u32[]{:S(2)}) async-start(bf16[128,4,128]{2,1,0:T(4,128)(2,1)} %bitcast), calls=%async_computation | async-start | bytes 262144 | tf_op jit(solution)/shard_map/all_to_all | solution.py:347
  34.4 20.8 %copy-start = (bf16[8,2,32,1024]{3,2,1,0:T(8,128)(2,1)S(1)}, bf16[8,2,32,1024]{3,2,1,0:T(8,128)(2,1)}, u32[]{:S(2)}) copy-start(bf16[8,2,32,1024]{3,2,1,0:T(8,128)(2,1)} %field.3) | copy-start | bytes 3145732
  36.5 6.3 %copy-start.7 = (bf16[32,32]{1,0:T(8,128)(2,1)S(1)}, bf16[32,32]{1,0:T(8,128)(2,1)}, u32[]{:S(2)}) copy-start(bf16[32,32]{1,0:T(8,128)(2,1)} %param.12) | copy-start | bytes 6148
  36.5 7.1 %copy-start.6 = (bf16[4,32,4,32]{3,2,1,0:T(4,128)(2,1)S(1)}, bf16[4,32,4,32]{3,2,1,0:T(4,128)(2,1)}, u32[]{:S(2)}) copy-start(bf16[4,32,4,32]{3,2,1,0:T(4,128)(2,1)} %constant.15) | copy-start | bytes 98308
  36.5 18.6 %all-to-all-start.1 = ((bf16[128,4,128]{2,1,0:T(4,128)(2,1)}), bf16[128,4,128]{2,1,0:T(4,128)(2,1)S(1)}, u32[]{:S(2)}, u32[]{:S(2)}) async-start(bf16[128,4,128]{2,1,0:T(4,128)(2,1)} %bitcast.2), calls=%async_computation.1 | async-start | bytes 262144 | tf_op jit(solution)/shard_map/all_to_all | solution.py:347
  42.9 0.7 copy-start.8
  43.6 11.5 %copy-start.1 = (bf16[128,1024]{1,0:T(8,128)(2,1)S(1)}, bf16[128,1024]{1,0:T(8,128)(2,1)}, u32[]{:S(2)}) copy-start(bf16[128,1024]{1,0:T(8,128)(2,1)} %constant.8.clone.ytab) | copy-start | bytes 786436
  60.1 21.9 %all-to-all-start.2 = ((bf16[128,5,2,128]{3,2,1,0:T(2,128)(2,1)}), bf16[128,5,2,128]{3,2,1,0:T(2,128)(2,1)S(1)}, u32[]{:S(2)}, u32[]{:S(2)}) async-start(bf16[128,5,2,128]{3,2,1,0:T(2,128)(2,1)} %bitcast.5), calls=%async_computation.2 | async-start | bytes 655360 | tf_op jit(solution)/shard_map/all_to_all | solution.py:347
  85.8 20.5 %copy-start.4 = (bf16[4,128,1024]{2,1,0:T(8,128)(2,1)S(1)}, bf16[4,128,1024]{2,1,0:T(8,128)(2,1)}, u32[]{:S(2)}) copy-start(bf16[4,128,1024]{2,1,0:T(8,128)(2,1)} %get-tuple-element.21.delta) | copy-start | bytes 3145732
  87.7 18.6 %all-to-all-start.3 = ((bf16[128,4,128]{2,1,0:T(4,128)(2,1)}), bf16[128,4,128]{2,1,0:T(4,128)(2,1)S(1)}, u32[]{:S(2)}, u32[]{:S(2)}) async-start(bf16[128,4,128]{2,1,0:T(4,128)(2,1)} %bitcast.7), calls=%async_computation.3 | async-start | bytes 262144 | tf_op jit(solution)/shard_map/all_to_all | solution.py:347

commit v5 on v4

--- a/solution.py
+++ b/solution.py
@@ -104,10 +104,11 @@
         copies.append(pltpu.make_async_copy(part, rows.at[k], sems.at[k]))
     for copy in copies:
         copy.start()
-    copies[0].wait()
     for k in range(4):
         z, h = k // 2, k % 2
-        copies[1 + k].wait()
+        if h == 0:
+            for copy in copies[3 * z : 3 + 2 * z]:
+                copy.wait()
         out = nt(table[...], rows[k].reshape(128, N))
         for p in range(2):
             held[pl.ds(4 * z + 2 * p + h, KY, stride=8), :] = out[KY * p : KY * (p + 1)]
@@ -138,37 +139,53 @@
 
 
 def point_kernel(
-    recv, field, cotangent, local4, bias4, ytab, send, delta, held, wide, cots, grads, sems
+    recv, field, cotangent, local, bias, ytab, send, delta, held, wide, cot, grad, early, sems
 ):
-    copies = []
-    for k in range(4):
-        part = cotangent.at[pl.ds(4 * (k % 2), 4), k // 2]
-        copies.append(pltpu.make_async_copy(part, cots.at[k], sems.at[k]))
-        copies[k].start()
+    copies = [
+        pltpu.make_async_copy(cotangent, cot, sems.at[0]),
+        pltpu.make_async_copy(grad, delta, sems.at[1]),
+    ]
+    copies[0].start()
     held[...] = recv[...].astype(F32)
+    row = lax.broadcasted_iota(jnp.int32, (128, C), 0)
+    same = jnp.where((row & 31) == lax.broadcasted_iota(jnp.int32, (128, C), 1), 1.0, 0.0)
+    bias4 = jnp.sum(same * bias[...], axis=1, keepdims=True)
+    same = same.astype(BF16)
+    local4 = nt(nt(same, local[...]).astype(BF16), same)
+    row = lax.broadcasted_iota(jnp.int32, (128, 128), 0)
+    local4 = jnp.where((row >> 5) == block_of((128, 128)), local4, 0.0).astype(BF16)
+
+    def rows_of(ref, k):
+        return ref[4 * (k % 2) : 4 * (k % 2) + 4, k // 2].reshape(128, N)
+
+    lefts = []
+    for k in range(4):
+        spectrum = jnp.concatenate(
+            [held[pl.ds(4 * (k // 2) + 2 * p + k % 2, KY, stride=8), :] for p in range(2)], axis=0
+        )
+        lefts.append(jnp.concatenate([spectrum.T.astype(BF16), local4], axis=1))
+
+    def before(k, cols):
+        right = jnp.concatenate([ytab[:, cols], rows_of(field, k)[:, cols]], axis=0)
+        return nn(lefts[k], right) + bias4
+
+    parts = [slice(256 * part, 256 * (part + 1)) for part in range(4)]
+    for cols in parts:
+        early[:, cols] = before(0, cols)
+    copies[0].wait()
+    for k in range(4):
+        for cols in parts:
+            pre = early[:, cols] if k == 0 else before(k, cols)
+            sig = 0.5 * jnp.tanh(0.5 * pre) + 0.5
+            slope = sig * (1.0 + pre * (1.0 - sig))
+            grad[k, :, cols] = (rows_of(cot, k)[:, cols].astype(F32) * slope).astype(BF16)
+    copies[1].start()
     ones = jnp.ones((16, N), BF16)
     total = jnp.zeros((144, 128), F32)
     outs = []
     for k in range(4):
-        z, h = k // 2, k % 2
-        spectrum = jnp.concatenate(
-            [held[pl.ds(4 * z + 2 * p + h, KY, stride=8), :] for p in range(2)], axis=0
-        )
-        left = jnp.concatenate([spectrum.T.astype(BF16), local4[...]], axis=1)
-        rows = field[4 * h : 4 * h + 4, z].reshape(128, N)
-        copies[k].wait()
-        cot = cots[k].reshape(128, N)
-        for part in range(4):
-            cols = slice(256 * part, 256 * (part + 1))
-            right = jnp.concatenate([ytab[:, cols], rows[:, cols]], axis=0)
-            pre = nn(left, right) + bias4[...]
-            sig = 0.5 * jnp.tanh(0.5 * pre) + 0.5
-            slope = sig * (1.0 + pre * (1.0 - sig))
-            grads[k, :, cols] = (cot[:, cols].astype(F32) * slope).astype(BF16)
-        copies.append(pltpu.make_async_copy(grads.at[k], delta.at[k], sems.at[4 + k]))
-        copies[4 + k].start()
-        out = nt(jnp.concatenate([ytab[...], rows, ones], axis=0), grads[k])
-        outs.append((z, h, out[:128]))
+        out = nt(jnp.concatenate([ytab[...], rows_of(field, k), ones], axis=0), grad[k])
+        outs.append((k // 2, k % 2, out[:128]))
         total = total + out[128:]
     bias_total = total[128:]
     block = block_of((32, 128))
@@ -197,11 +214,10 @@
         for k, line in enumerate(lines):
             wide[pl.ds(10 * z + 4 + k, KY, stride=20), :] = jnp.broadcast_to(line, (KY, 128))
     send[...] = wide[...].astype(BF16)
-    for copy in copies[4:]:
-        copy.wait()
-
-
-def back_kernel(recv, forward, kept, share, held):
+    copies[1].wait()
+
+
+def back_kernel(recv, forward, first, kept, share, held):
     real, imag = x_forward(recv, forward, held, 10)
     factor = mode_weight()
     real = rounded(real * factor)
@@ -214,7 +230,7 @@
     ]
     total = jnp.concatenate(lines[:4], axis=0)
     bias = fold(lines[4])
-    share[KX:] = jnp.concatenate(
+    share[KX : KX + 16] = jnp.concatenate(
         [
             rounded(total),
             total - rounded(total),
@@ -224,9 +240,10 @@
         ],
         axis=0,
     ).astype(BF16)
-
-
-def adjoint_kernel(kept, weight, inverse, firsts, seconds, send, group, held, high, low):
+    share[KX + 16 :] = first[...]
+
+
+def adjoint_kernel(kept, weight, inverse, shares, send, group, held, high, low):
     dre = kept[:KX]
     dim = kept[KX:]
     for t in range(8):
@@ -245,17 +262,26 @@
     send[...] = held[...].astype(BF16)
     start = 64 * lax.axis_index("core")
     left = block_of((64, 128)) < 2
-    for k, (both, step) in enumerate(((firsts, KX), (seconds, KX + 16))):
-        one = both[pl.ds(pl.multiple_of(start, 16), 64), :].astype(F32)
-        two = both[pl.ds(pl.multiple_of(step + start, 16), 64), :].astype(F32)
+    step = 2 * KX + 16
+    for k, at in enumerate((KX + 16, 0)):
+        one = shares[pl.ds(pl.multiple_of(at + start, 16), 64), :].astype(F32)
+        two = shares[pl.ds(pl.multiple_of(step + at + start, 16), 64), :].astype(F32)
         group[64 * k : 64 * (k + 1)] = jnp.where(left, one, two).astype(BF16)
-    group[128:144] = seconds[KX : KX + 16]
-    group[144:160] = seconds[2 * KX + 16 : 2 * KX + 32]
-
-
-def grad_kernel(recv, delta, local4, ytab, field_grad, held, rows, sems):
+    group[128:144] = shares[KX : KX + 16]
+    group[144:160] = shares[step + KX : step + KX + 16]
+
+
+def final_kernel(
+    recv, delta, local4, ytab, groups, field_grad, spectral_grad, local_grad, bias_grad,
+    held, rows, out, tiles, out_local, out_bias, sems,
+):
     held[...] = recv[...].astype(F32)
-    copies = []
+    copies = [
+        pltpu.make_async_copy(rows, field_grad, sems.at[0]),
+        pltpu.make_async_copy(out, spectral_grad, sems.at[1]),
+        pltpu.make_async_copy(out_local, local_grad, sems.at[2]),
+        pltpu.make_async_copy(out_bias, bias_grad, sems.at[3]),
+    ]
     for k in range(4):
         z, h = k // 2, k % 2
         spectrum = jnp.concatenate(
@@ -265,16 +291,8 @@
         for part in range(4):
             cols = slice(256 * part, 256 * (part + 1))
             right = jnp.concatenate([ytab[:, cols], delta[k, :, cols]], axis=0)
-            rows[k, :, :, cols] = nn(left, right).astype(BF16).reshape(4, 32, 256)
-        copies.append(
-            pltpu.make_async_copy(rows.at[k], field_grad.at[pl.ds(4 * h, 4), z], sems.at[k])
-        )
-        copies[k].start()
-    for copy in copies:
-        copy.wait()
-
-
-def outer_kernel(groups, out, local_grad, bias_grad, tiles):
+            rows[4 * h : 4 * h + 4, z, :, cols] = nn(left, right).astype(BF16).reshape(4, 32, 256)
+    copies[0].start()
     lane = lax.broadcasted_iota(jnp.int32, (128, 1024), 1)
     k = lax.broadcasted_iota(jnp.int32, (128, 1024), 0)
     expand = jnp.where((lane >> 5) == k, 1.0, 0.0).astype(BF16)
@@ -314,8 +332,12 @@
         [total[0:4] + total[4:8], total[16:20] + total[20:24]], axis=0
     ) * gscale
     for q in range(4):
-        local_grad[pl.ds(q, 8, stride=4), :] = flat[:, 32 * q : 32 * (q + 1)]
-    bias_grad[...] = ((total[8:9] + total[9:10]) * gscale)[:, :32]
+        out_local[pl.ds(q, 8, stride=4), :] = flat[:, 32 * q : 32 * (q + 1)]
+    out_bias[...] = ((total[8:9] + total[9:10]) * gscale)[:, :32]
+    for copy in copies[1:]:
+        copy.start()
+    for copy in copies:
+        copy.wait()
 
 
 def run(kernel, operands, outs, scratch, name, specs=None, out_specs=None):
@@ -351,8 +373,6 @@
     ytab, forward, inverse = (jnp.asarray(table) for table in tables())
     same = jnp.asarray(np.kron(np.eye(4), np.ones((C, C))).astype(ml_dtypes.bfloat16))
     local_in = jnp.tile(local_weight, (4, 4)) * same
-    local_out = jnp.tile(local_weight.T, (4, 4)) * same
-    bias4 = jnp.tile(bias, 4)[:, None]
     slab = ((512, 128), BF16)
     slab_wide = ((1280, 128), BF16)
     held = pltpu.VMEM((512, 128), F32)
@@ -377,17 +397,17 @@
         "mix",
     )
     recv = exchange(send, 4, 128)
-    firsts = lax.all_gather(first, "core", axis=0, tiled=True)
     send, delta = run(
         point_kernel,
-        (recv, field, cotangent, local_out, bias4, ytab),
+        (recv, field, cotangent, local_weight, bias.reshape(1, C), ytab),
         [slab_wide, ((4, 128, N), BF16)],
         [
             held,
             held_wide,
-            quarters,
+            pltpu.VMEM((8, 2, C, N), BF16),
             pltpu.VMEM((4, 128, N), BF16),
-            pltpu.SemaphoreType.DMA((8,)),
+            pltpu.VMEM((128, N), F32),
+            pltpu.SemaphoreType.DMA((2,)),
         ],
         "pointwise",
         [VM, VM, HBM, VM, VM, VM],
@@ -396,36 +416,37 @@
     recv = exchange(send, 5, 2, 128)
     second, share = run(
         back_kernel,
-        (recv, forward),
-        [((2 * KX, 128), F32), ((KX + 16, 128), BF16)],
+        (recv, forward, first),
+        [((2 * KX, 128), F32), ((2 * KX + 16, 128), BF16)],
         [held_wide],
         "x_forward",
     )
-    seconds = lax.all_gather(share, "core", axis=0, tiled=True)
+    shares = lax.all_gather(share, "core", axis=0, tiled=True)
     send, group = run(
         adjoint_kernel,
-        (second, weight, inverse, firsts, seconds),
+        (second, weight, inverse, shares),
         [slab, ((160, 128), BF16)],
         [held, pltpu.VMEM((256, 1024), BF16), pltpu.VMEM((256, 1024), BF16)],
         "adjoint",
     )
     recv = exchange(send, 4, 128)
     groups = lax.all_gather(group, "gz", axis=0, tiled=True)
-    (field_grad,) = run(
-        grad_kernel,
-        (recv, delta, local_in, ytab),
-        [((8, 2, C, N), BF16)],
-        [held, quarters, pltpu.SemaphoreType.DMA((4,))],
-        "y_inverse",
+    field_grad, spectral_grad, local_grad, bias_grad = run(
+        final_kernel,
+        (recv, delta, local_in, ytab, groups),
+        [((8, 2, C, N), BF16), ((64, 2048), BF16), ((C, C), F32), ((1, C), F32)],
+        [
+            held,
+            pltpu.VMEM((8, 2, C, N), BF16),
+            pltpu.VMEM((64, 2048), BF16),
+            pltpu.VMEM((1024, 128), F32),
+            pltpu.VMEM((C, C), F32),
+            pltpu.VMEM((1, C), F32),
+            pltpu.SemaphoreType.DMA((4,)),
+        ],
+        "final",
         None,
-        [HBM],
-    )
-    spectral_grad, local_grad, bias_grad = run(
-        outer_kernel,
-        (groups,),
-        [((64, 2048), BF16), ((C, C), F32), ((1, C), F32)],
-        [pltpu.VMEM((1024, 128), F32)],
-        "outer",
+        [HBM] * 4,
     )
     return field_grad, spectral_grad, local_grad, bias_grad.reshape(C)
 

time: 109 us -> 106 us (0.972)
  blocking collectives: 19 us -> 55.7 us
  waiting for transfers between devices: 33.9 us -> 11.2 us
  starting transfers between devices: 36.7 us -> 24.4 us
  Pallas kernels: 16 us -> 12.2 us
    all_to_all x0 -> x2, blocking collectives: none -> 39.2 us  [exchange(): return lax.all_to_all(blocks, GX, 0, 0, tiled=True).reshape(values.shape)]
    all_to_all x4 -> x2, waiting for transfers between devices: 33.9 us -> 11.2 us  [exchange(): return lax.all_to_all(blocks, GX, 0, 0, tiled=True).reshape(values.shape)]
    all_to_all x4 -> x2, starting transfers between devices: 36.7 us -> 24.4 us  [exchange(): return lax.all_to_all(blocks, GX, 0, 0, tiled=True).reshape(values.shape)]
    pallas_call x7 -> x6, Pallas kernels: 16 us -> 12.2 us  [run(): pl.pallas_call(kernel, out_shape=[(pltpu.HBM if spec is HBM else jax.Shap...]
    all_gather x2 -> x1, blocking collectives: 5.86 us -> 3.39 us  [local(): shares = lax.all_gather(share, 'core', axis=0, tiled=True)]
  transfers between devices with their start and end apart: 4 -> 2, of which waited for: 3 -> 2; matrix products, arithmetic and copies ran while one was open for 1% -> 0% of each run, Pallas kernels for 2% -> 0%
where the time goes in v5:
time: 106 us; the launch traced here: 105 us
  blocking collectives  55.7 us (53%)
  starting transfers between devices  24.4 us (23%)
  Pallas kernels  12.2 us (12%)
  waiting for transfers between devices  11.2 us (11%)
    all_to_all x2, blocking collectives, exchange(): return lax.all_to_all(blocks, GX, 0, 0, tiled=True).reshape(values.shape)  39.2 us
    all_to_all x2, starting transfers between devices, exchange(): return lax.all_to_all(blocks, GX, 0, 0, tiled=True).reshape(values.shape)  24.4 us
    pallas_call x6, Pallas kernels, run(): pl.pallas_call(kernel, out_shape=[(pltpu.HBM if spec is HBM else jax.Shap...  12.2 us
    all_to_all x2, waiting for transfers between devices, exchange(): return lax.all_to_all(blocks, GX, 0, 0, tiled=True).reshape(values.shape)  11.2 us
    all_gather x1, blocking collectives, local(): groups = lax.all_gather(group, 'gz', axis=0, tiled=True)  10.4 us
    all_gather x1, blocking collectives, local(): shares = lax.all_gather(share, 'core', axis=0, tiled=True)  3.39 us
    all_gather x1, blocking collectives, local(): weight = lax.all_gather(spectral_weight, 'core', axis=0, tiled=True)  2.7 us
  transfers between devices with their start and end apart: 2, of which 2 were waited for; matrix products, arithmetic and copies ran while one was open for 0% of the time, Pallas kernels for 0%

profile of v5, /device:TPU:1, one launch (start us, length us, event | category | flops | bytes accessed | tf_op | source)
XLA Modules:
  0.0 105.3 jit_solution(4103771887008767608)
XLA Ops:
  0.6 0.0 copy-start.7
  0.6 2.5 %y_forward.1 = bf16[512,128]{1,0:T(8,128)(2,1)} custom-call(bf16[8,2,32,1024]{3,2,1,0:T(8,128)(2,1)} %field.3, bf16[128,1024]{1,0:T(8,128)(2,1)} %constant.8.clone.ytab), custom_call_target="tpu_custom_call" | custom-call | flops 200000000 | bytes 1048576 | tf_op jit(solution)/shard_map/y_forward/pallas_call | solution.py:350
  3.1 0.0 copy-start.2
  3.1 0.0 copy-start.3
  3.1 18.6 %all-to-all-start = ((bf16[128,4,128]{2,1,0:T(4,128)(2,1)}), bf16[128,4,128]{2,1,0:T(4,128)(2,1)S(1)}, u32[]{:S(2)}, u32[]{:S(2)}) async-start(bf16[128,4,128]{2,1,0:T(4,128)(2,1)} %bitcast), calls=%async_computation | async-start | bytes 262144 | tf_op jit(solution)/shard_map/all_to_all | solution.py:369
  21.7 0.0 copy-done.7
  21.7 2.7 %all_gather.9.weight = bf16[128,2048]{1,0:T(8,128)(2,1)S(1)} all-gather(bf16[64,2048]{1,0:T(8,128)(2,1)S(1)} %copy-done.7), channel_id=1, replica_groups=mesh['y'=8,'z'=8,'core'=2,'gz'=4] {'core'}, dimensions={0}, use_global_device_ids=true | all-gather | bytes 786432 | tf_op jit(solution)/shard_map/all_gather | solution.py:391
  24.4 0.0 copy-start
  24.4 9.5 %all-to-all-done = bf16[128,4,128]{2,1,0:T(4,128)(2,1)S(1)} async-done(((bf16[128,4,128]{2,1,0:T(4,128)(2,1)}), bf16[128,4,128]{2,1,0:T(4,128)(2,1)S(1)}, u32[]{:S(2)}, u32[]{:S(2)}) %all-to-all-start) | async-done | bytes 131104 | tf_op jit(solution)/shard_map/all_to_all | solution.py:369
  33.9 0.0 copy-done.2
  33.9 0.0 copy-done.3
  33.9 0.0 copy-start.5
  33.9 1.5 %mix.1 = (bf16[512,128]{1,0:T(8,128)(2,1)S(1)}, bf16[128,128]{1,0:T(8,128)(2,1)S(1)}) custom-call(bf16[512,128]{1,0:T(8,128)(2,1)S(1)} %bitcast.13, bf16[128,2048]{1,0:T(8,128)(2,1)S(1)} %all_gather.9.weight, bf16[256,1024]{1,0:T(8,128)(2,1)S(1)} %copy-done.2, bf16[256,1024]{1,0:T(8,128)(2,1)S(1)} %copy-done.3), custom_call_target="tpu_custom_call" | custom-call | flops 200000000 | bytes 1048576 | tf_op jit(solution)/shard_map/mix/pallas_call | solution.py:350
  35.4 0.0 copy-start.1
  35.4 18.3 %all_to_all.20 = bf16[128,4,128]{2,1,0:T(4,128)(2,1)S(1)} all-to-all(bf16[128,4,128]{2,1,0:T(4,128)(2,1)S(1)} %bitcast.15), channel_id=1, replica_groups=mesh['y'=8,'z'=8,'core'=2,'gz'=4] {'y','z','core'}, dimensions={0} | all-to-all | bytes 262144 | tf_op jit(solution)/shard_map/all_to_all | solution.py:369
  53.7 0.0 copy-start.6
  53.7 0.0 copy-done
  53.7 0.0 copy-done.5
  53.7 0.0 copy-done.1
  53.7 0.6 copy-done.6
  54.3 3.2 %pointwise.1 = (bf16[1280,128]{1,0:T(8,128)(2,1)S(1)}, bf16[4,128,1024]{2,1,0:T(8,128)(2,1)}) custom-call(bf16[512,128]{1,0:T(8,128)(2,1)S(1)} %bitcast.12, bf16[8,2,32,1024]{3,2,1,0:T(8,128)(2,1)S(1)} %copy-done, bf16[8,2,32,1024]{3,2,1,0:T(8,128)(2,1)} %cotangent.1, bf16[32,32]{1,0:T(8,128)(2,1)S(1)} %copy-done.5, f32[1,32]{1,0:T(1,128)S(1)} %bitcast.16, ...), custom_call_target="tpu_custom_call" | custom-call | flops 200000000 | bytes 1048576 | tf_op jit(solution)/shard_map/pointwise/pallas_call | solution.py:350
  57.6 20.9 %all_to_all.21 = bf16[128,5,2,128]{3,2,1,0:T(2,128)(2,1)S(1)} all-to-all(bf16[128,5,2,128]{3,2,1,0:T(2,128)(2,1)S(1)} %bitcast.14), channel_id=1, replica_groups=mesh['y'=8,'z'=8,'core'=2,'gz'=4] {'y','z','core'}, dimensions={0} | all-to-all | bytes 655360 | tf_op jit(solution)/shard_map/all_to_all | solution.py:369
  78.5 0.5 x_forward.1
  79.0 3.4 %all_gather.10.shares = bf16[544,128]{1,0:T(8,128)(2,1)S(1)} all-gather(bf16[272,128]{1,0:T(8,128)(2,1)S(1)} %get-tuple-element.20), channel_id=1, replica_groups=mesh['y'=8,'z'=8,'core'=2,'gz'=4] {'core'}, dimensions={0}, use_global_device_ids=true | all-gather | bytes 208896 | tf_op jit(solution)/shard_map/all_gather | solution.py:424
  82.4 0.0 copy-start.4
  82.4 1.9 %adjoint.1 = (bf16[512,128]{1,0:T(8,128)(2,1)}, bf16[160,128]{1,0:T(8,128)(2,1)S(1)}) custom-call(f32[256,128]{1,0:T(8,128)S(1)} %get-tuple-element.19.kept, bf16[128,2048]{1,0:T(8,128)(2,1)S(1)} %all_gather.9.weight, bf16[256,1024]{1,0:T(8,128)(2,1)S(1)} %copy-done.3, bf16[544,128]{1,0:T(8,128)(2,1)S(1)} %all_gather.10.shares), custom_call_target="tpu_custom_call" | custom-call | flops 200000000 | bytes 1048576 | tf_op jit(solution)/shard_map/adjoint/pallas_call | solution.py:350
  84.3 0.0 copy-start.8
  84.3 5.8 %all-to-all-start.3 = ((bf16[128,4,128]{2,1,0:T(4,128)(2,1)}), bf16[128,4,128]{2,1,0:T(4,128)(2,1)S(1)}, u32[]{:S(2)}, u32[]{:S(2)}) async-start(bf16[128,4,128]{2,1,0:T(4,128)(2,1)} %bitcast.7), calls=%async_computation.3 | async-start | bytes 262144 | tf_op jit(solution)/shard_map/all_to_all | solution.py:369
  90.1 0.0 copy-done.8
  90.1 0.1 broadcast_multiply_fusion
  90.2 0.1 reshape.50.local4
  90.3 10.4 %all_gather.11.groups = bf16[640,128]{1,0:T(8,128)(2,1)S(1)} all-gather(bf16[160,128]{1,0:T(8,128)(2,1)S(1)} %get-tuple-element.23), channel_id=1, replica_groups=mesh['y'=8,'z'=8,'core'=2,'gz'=4] {'gz'}, dimensions={0}, use_global_device_ids=true | all-gather | bytes 204800 | tf_op jit(solution)/shard_map/all_gather | solution.py:433
  100.8 1.7 %all-to-all-done.3 = bf16[128,4,128]{2,1,0:T(4,128)(2,1)S(1)} async-done(((bf16[128,4,128]{2,1,0:T(4,128)(2,1)}), bf16[128,4,128]{2,1,0:T(4,128)(2,1)S(1)}, u32[]{:S(2)}, u32[]{:S(2)}) %all-to-all-start.3) | async-done | bytes 131104 | tf_op jit(solution)/shard_map/all_to_all | solution.py:369
  102.4 0.0 copy-done.4
  102.4 2.7 %final.1 = (bf16[8,2,32,1024]{3,2,1,0:T(8,128)(2,1)}, bf16[64,2048]{1,0:T(8,128)(2,1)}, f32[32,32]{1,0:T(8,128)}, f32[1,32]{1,0:T(1,128)}) custom-call(bf16[512,128]{1,0:T(8,128)(2,1)S(1)} %bitcast.11, bf16[4,128,1024]{2,1,0:T(8,128)(2,1)S(1)} %copy-done.4, bf16[128,128]{1,0:T(8,128)(2,1)S(1)} %reshape.50.local4, bf16[128,1024]{1,0:T(8,128)(2,1)S(1)} %copy-done.1, ...), custom_call_target="tpu_custom_call" | custom-call | flops 200000000 | bytes 1048576 | tf_op jit(solution)/shard_map/final/pallas_call | solution.py:350
Async XLA Ops:
  0.6 21.1 %copy-start.7 = (bf16[64,2048]{1,0:T(8,128)(2,1)S(1)}, bf16[64,2048]{1,0:T(8,128)(2,1)}, u32[]{:S(2)}) copy-start(bf16[64,2048]{1,0:T(8,128)(2,1)} %param.11) | copy-start | bytes 786436
  3.1 30.8 %copy-start.2 = (bf16[256,1024]{1,0:T(8,128)(2,1)S(1)}, bf16[256,1024]{1,0:T(8,128)(2,1)}, u32[]{:S(2)}) copy-start(bf16[256,1024]{1,0:T(8,128)(2,1)} %constant.9.clone.forward) | copy-start | bytes 1572868
  3.1 30.8 %copy-start.3 = (bf16[256,1024]{1,0:T(8,128)(2,1)S(1)}, bf16[256,1024]{1,0:T(8,128)(2,1)}, u32[]{:S(2)}) copy-start(bf16[256,1024]{1,0:T(8,128)(2,1)} %constant.10.clone.inverse) | copy-start | bytes 1572868
  3.1 30.8 %all-to-all-start = ((bf16[128,4,128]{2,1,0:T(4,128)(2,1)}), bf16[128,4,128]{2,1,0:T(4,128)(2,1)S(1)}, u32[]{:S(2)}, u32[]{:S(2)}) async-start(bf16[128,4,128]{2,1,0:T(4,128)(2,1)} %bitcast), calls=%async_computation | async-start | bytes 262144 | tf_op jit(solution)/shard_map/all_to_all | solution.py:369
  24.4 29.3 %copy-start = (bf16[8,2,32,1024]{3,2,1,0:T(8,128)(2,1)S(1)}, bf16[8,2,32,1024]{3,2,1,0:T(8,128)(2,1)}, u32[]{:S(2)}) copy-start(bf16[8,2,32,1024]{3,2,1,0:T(8,128)(2,1)} %field.3) | copy-start | bytes 3145732
  33.9 19.8 %copy-start.5 = (bf16[32,32]{1,0:T(8,128)(2,1)S(1)}, bf16[32,32]{1,0:T(8,128)(2,1)}, u32[]{:S(2)}) copy-start(bf16[32,32]{1,0:T(8,128)(2,1)} %local.1) | copy-start | bytes 6148
  35.4 18.3 %copy-start.1 = (bf16[128,1024]{1,0:T(8,128)(2,1)S(1)}, bf16[128,1024]{1,0:T(8,128)(2,1)}, u32[]{:S(2)}) copy-start(bf16[128,1024]{1,0:T(8,128)(2,1)} %constant.8.clone.ytab) | copy-start | bytes 786436
  53.7 0.7 copy-start.6
  82.4 20.0 %copy-start.4 = (bf16[4,128,1024]{2,1,0:T(8,128)(2,1)S(1)}, bf16[4,128,1024]{2,1,0:T(8,128)(2,1)}, u32[]{:S(2)}) copy-start(bf16[4,128,1024]{2,1,0:T(8,128)(2,1)} %get-tuple-element.22.delta) | copy-start | bytes 3145732
  84.3 5.8 %copy-start.8 = (bf16[4,32,4,32]{3,2,1,0:T(4,128)(2,1)S(1)}, bf16[4,32,4,32]{3,2,1,0:T(4,128)(2,1)}, u32[]{:S(2)}) copy-start(bf16[4,32,4,32]{3,2,1,0:T(4,128)(2,1)} %constant.15) | copy-start | bytes 98308
  84.3 18.1 %all-to-all-start.3 = ((bf16[128,4,128]{2,1,0:T(4,128)(2,1)}), bf16[128,4,128]{2,1,0:T(4,128)(2,1)S(1)}, u32[]{:S(2)}, u32[]{:S(2)}) async-start(bf16[128,4,128]{2,1,0:T(4,128)(2,1)} %bitcast.7), calls=%async_computation.3 | async-start | bytes 262144 | tf_op jit(solution)/shard_map/all_to_all | solution.py:369

commit v6 on v5

--- a/solution.py
+++ b/solution.py
@@ -17,6 +17,7 @@
 GX = ("y", "z", "core")
 VM = pl.BlockSpec(memory_space=pltpu.VMEM)
 HBM = pl.BlockSpec(memory_space=pltpu.HBM)
+COST = {"mix": 800_000_000}
 
 
 def angles(freq, pos):
@@ -115,7 +116,9 @@
     send[...] = held[...].astype(BF16)
 
 
-def mix_kernel(recv, weight, forward, inverse, send, kept, held):
+def mix_kernel(recv, weight, forward, inverse, bias, send, kept, bias_row, held, sem):
+    copy = pltpu.make_async_copy(bias, bias_row, sem.at[0])
+    copy.start()
     real, imag = x_forward(recv, forward, held, 4)
     real = rounded(real)
     imag = rounded(imag)
@@ -136,56 +139,41 @@
     factor = mode_weight()
     x_inverse(rounded(fold(vre) * factor), rounded(fold(vim) * factor), inverse, held, 4)
     send[...] = held[...].astype(BF16)
-
-
-def point_kernel(
-    recv, field, cotangent, local, bias, ytab, send, delta, held, wide, cot, grad, early, sems
-):
-    copies = [
-        pltpu.make_async_copy(cotangent, cot, sems.at[0]),
-        pltpu.make_async_copy(grad, delta, sems.at[1]),
-    ]
-    copies[0].start()
+    copy.wait()
+
+
+def point_kernel(recv, field, cotangent, local, bias, ytab, send, delta, held, wide):
     held[...] = recv[...].astype(F32)
     row = lax.broadcasted_iota(jnp.int32, (128, C), 0)
     same = jnp.where((row & 31) == lax.broadcasted_iota(jnp.int32, (128, C), 1), 1.0, 0.0)
     bias4 = jnp.sum(same * bias[...], axis=1, keepdims=True)
-    same = same.astype(BF16)
-    local4 = nt(nt(same, local[...]).astype(BF16), same)
+    picks = same.astype(BF16)
+    local4 = nt(nt(picks, local[...]).astype(BF16), picks)
     row = lax.broadcasted_iota(jnp.int32, (128, 128), 0)
     local4 = jnp.where((row >> 5) == block_of((128, 128)), local4, 0.0).astype(BF16)
-
-    def rows_of(ref, k):
-        return ref[4 * (k % 2) : 4 * (k % 2) + 4, k // 2].reshape(128, N)
-
-    lefts = []
-    for k in range(4):
-        spectrum = jnp.concatenate(
-            [held[pl.ds(4 * (k // 2) + 2 * p + k % 2, KY, stride=8), :] for p in range(2)], axis=0
-        )
-        lefts.append(jnp.concatenate([spectrum.T.astype(BF16), local4], axis=1))
-
-    def before(k, cols):
-        right = jnp.concatenate([ytab[:, cols], rows_of(field, k)[:, cols]], axis=0)
-        return nn(lefts[k], right) + bias4
-
-    parts = [slice(256 * part, 256 * (part + 1)) for part in range(4)]
-    for cols in parts:
-        early[:, cols] = before(0, cols)
-    copies[0].wait()
-    for k in range(4):
-        for cols in parts:
-            pre = early[:, cols] if k == 0 else before(k, cols)
-            sig = 0.5 * jnp.tanh(0.5 * pre) + 0.5
-            slope = sig * (1.0 + pre * (1.0 - sig))
-            grad[k, :, cols] = (rows_of(cot, k)[:, cols].astype(F32) * slope).astype(BF16)
-    copies[1].start()
     ones = jnp.ones((16, N), BF16)
     total = jnp.zeros((144, 128), F32)
     outs = []
     for k in range(4):
-        out = nt(jnp.concatenate([ytab[...], rows_of(field, k), ones], axis=0), grad[k])
-        outs.append((k // 2, k % 2, out[:128]))
+        z, h = k // 2, k % 2
+        spectrum = jnp.concatenate(
+            [held[pl.ds(4 * z + 2 * p + h, KY, stride=8), :] for p in range(2)], axis=0
+        )
+        left = jnp.concatenate([spectrum.T.astype(BF16), local4], axis=1)
+        rows = field[4 * h : 4 * h + 4, z].reshape(128, N)
+        cot = cotangent[4 * h : 4 * h + 4, z].reshape(128, N)
+        for part in range(4):
+            cols = slice(256 * part, 256 * (part + 1))
+            right = jnp.concatenate([ytab[:, cols], rows[:, cols]], axis=0)
+            pre = nn(left, right) + bias4
+            sig = 0.5 * jnp.tanh(0.5 * pre) + 0.5
+            slope = sig * (1.0 + pre * (1.0 - sig))
+            delta[k, :, cols] = (cot[:, cols].astype(F32) * slope).astype(BF16)
+    for k in range(4):
+        z, h = k // 2, k % 2
+        rows = field[4 * h : 4 * h + 4, z].reshape(128, N)
+        out = nt(jnp.concatenate([ytab[...], rows, ones], axis=0), delta[k])
+        outs.append((z, h, out[:128]))
         total = total + out[128:]
     bias_total = total[128:]
     block = block_of((32, 128))
@@ -214,7 +202,6 @@
         for k, line in enumerate(lines):
             wide[pl.ds(10 * z + 4 + k, KY, stride=20), :] = jnp.broadcast_to(line, (KY, 128))
     send[...] = wide[...].astype(BF16)
-    copies[1].wait()
 
 
 def back_kernel(recv, forward, first, kept, share, held):
@@ -358,7 +345,7 @@
         scratch_shapes=scratch,
         compiler_params=pltpu.CompilerParams(vmem_limit_bytes=16 * 1024 * 1024),
         cost_estimate=pl.CostEstimate(
-            flops=200_000_000, bytes_accessed=1 << 20, transcendentals=0
+            flops=COST.get(name, 200_000_000), bytes_accessed=1 << 20, transcendentals=0
         ),
         name=name,
     )(*operands)
@@ -389,29 +376,24 @@
     )
     recv = exchange(send, 4, 128)
     weight = lax.all_gather(spectral_weight, "core", axis=0, tiled=True)
-    send, first = run(
+    send, first, bias_row = run(
         mix_kernel,
-        (recv, weight, forward, inverse),
-        [slab, ((KX, 128), BF16)],
-        [held],
+        (recv, weight, forward, inverse, bias.reshape(1, C)),
+        [slab, ((KX, 128), BF16), ((1, C), F32)],
+        [held, pltpu.SemaphoreType.DMA((1,))],
         "mix",
+        [VM, VM, VM, VM, HBM],
     )
     recv = exchange(send, 4, 128)
     send, delta = run(
         point_kernel,
-        (recv, field, cotangent, local_weight, bias.reshape(1, C), ytab),
+        (recv, field, cotangent, local_weight, bias_row, ytab),
         [slab_wide, ((4, 128, N), BF16)],
         [
             held,
             held_wide,
-            pltpu.VMEM((8, 2, C, N), BF16),
-            pltpu.VMEM((4, 128, N), BF16),
-            pltpu.VMEM((128, N), F32),
-            pltpu.SemaphoreType.DMA((2,)),
         ],
         "pointwise",
-        [VM, VM, HBM, VM, VM, VM],
-        [VM, HBM],
     )
     recv = exchange(send, 5, 2, 128)
     second, share = run(
@@ -430,10 +412,11 @@
         "adjoint",
     )
     recv = exchange(send, 4, 128)
-    groups = lax.all_gather(group, "gz", axis=0, tiled=True)
+    for pairs in ([[0, 1], [2, 3]], [[0, 3], [1, 2]]):
+        group = lax.all_gather(group, "gz", axis=0, tiled=True, axis_index_groups=pairs)
     field_grad, spectral_grad, local_grad, bias_grad = run(
         final_kernel,
-        (recv, delta, local_in, ytab, groups),
+        (recv, delta, local_in, ytab, group),
         [((8, 2, C, N), BF16), ((64, 2048), BF16), ((C, C), F32), ((1, C), F32)],
         [
             held,

time: 106 us -> 104 us (0.981)
  blocking collectives: 55.7 us -> 54.6 us
  waiting for transfers between devices: 11.2 us -> 12.3 us
    all_to_all x2, waiting for transfers between devices: 11.2 us -> 12.3 us  [exchange(): return lax.all_to_all(blocks, GX, 0, 0, tiled=True).reshape(values.shape)]
    all_gather x1 -> x2, blocking collectives: 10.4 us -> 9.29 us  [local(): lax.all_gather(group, 'gz', axis=0, tiled=True, axis_index_groups=pairs)]
where the time goes in v6:
time: 104 us
  blocking collectives  54.6 us (52%)
  starting transfers between devices  24.4 us (23%)
  waiting for transfers between devices  12.3 us (12%)
  Pallas kernels  11.3 us (11%)
    all_to_all x2, blocking collectives, exchange(): return lax.all_to_all(blocks, GX, 0, 0, tiled=True).reshape(values.shape)  39.2 us
    all_to_all x2, starting transfers between devices, exchange(): return lax.all_to_all(blocks, GX, 0, 0, tiled=True).reshape(values.shape)  24.4 us
    all_to_all x2, waiting for transfers between devices, exchange(): return lax.all_to_all(blocks, GX, 0, 0, tiled=True).reshape(values.shape)  12.3 us
    pallas_call x6, Pallas kernels, run(): pl.pallas_call(kernel, out_shape=[(pltpu.HBM if spec is HBM else jax.Shap...  11.3 us
    all_gather x2, blocking collectives, local(): lax.all_gather(group, 'gz', axis=0, tiled=True, axis_index_groups=pairs)  9.29 us
    all_gather x1, blocking collectives, local(): shares = lax.all_gather(share, 'core', axis=0, tiled=True)  3.38 us
    all_gather x1, blocking collectives, local(): weight = lax.all_gather(spectral_weight, 'core', axis=0, tiled=True)  2.7 us
  transfers between devices with their start and end apart: 2, of which 2 were waited for; matrix products, arithmetic and copies ran while one was open for 0% of the time, Pallas kernels for 0%

profile of v6, /device:TPU:1, one launch (start us, length us, event | category | flops | bytes accessed | tf_op | source)
XLA Modules:
  0.0 103.7 jit_solution(10646079292351974614)
XLA Ops:
  0.6 0.0 copy-start.6
  0.6 2.5 %y_forward.1 = bf16[512,128]{1,0:T(8,128)(2,1)} custom-call(bf16[8,2,32,1024]{3,2,1,0:T(8,128)(2,1)} %field.3, bf16[128,1024]{1,0:T(8,128)(2,1)} %constant.8.clone.ytab), custom_call_target="tpu_custom_call" | custom-call | flops 200000000 | bytes 1048576 | tf_op jit(solution)/shard_map/y_forward/pallas_call | solution.py:337
  3.1 0.0 copy-start.3
  3.1 0.0 copy-start.4
  3.1 18.6 %all-to-all-start = ((bf16[128,4,128]{2,1,0:T(4,128)(2,1)}), bf16[128,4,128]{2,1,0:T(4,128)(2,1)S(1)}, u32[]{:S(2)}, u32[]{:S(2)}) async-start(bf16[128,4,128]{2,1,0:T(4,128)(2,1)} %bitcast), calls=%async_computation | async-start | bytes 262144 | tf_op jit(solution)/shard_map/all_to_all | solution.py:356
  21.7 0.0 copy-done.6
  21.7 2.7 %all_gather.12.weight = bf16[128,2048]{1,0:T(8,128)(2,1)S(1)} all-gather(bf16[64,2048]{1,0:T(8,128)(2,1)S(1)} %copy-done.6), channel_id=1, replica_groups=mesh['y'=8,'z'=8,'core'=2,'gz'=4] {'core'}, dimensions={0}, use_global_device_ids=true | all-gather | bytes 786432 | tf_op jit(solution)/shard_map/all_gather | solution.py:378
  24.4 9.5 %all-to-all-done = bf16[128,4,128]{2,1,0:T(4,128)(2,1)S(1)} async-done(((bf16[128,4,128]{2,1,0:T(4,128)(2,1)}), bf16[128,4,128]{2,1,0:T(4,128)(2,1)S(1)}, u32[]{:S(2)}, u32[]{:S(2)}) %all-to-all-start) | async-done | bytes 131104 | tf_op jit(solution)/shard_map/all_to_all | solution.py:356
  33.9 0.0 copy-done.3
  33.9 0.0 copy-done.4
  33.9 0.0 copy-start
  33.9 0.0 copy-start.2
  33.9 0.0 copy-start.5
  33.9 1.6 %mix.1 = (bf16[512,128]{1,0:T(8,128)(2,1)S(1)}, bf16[128,128]{1,0:T(8,128)(2,1)S(1)}, f32[1,32]{1,0:T(1,128)S(1)}) custom-call(bf16[512,128]{1,0:T(8,128)(2,1)S(1)} %bitcast.14, bf16[128,2048]{1,0:T(8,128)(2,1)S(1)} %all_gather.12.weight, bf16[256,1024]{1,0:T(8,128)(2,1)S(1)} %copy-done.3, bf16[256,1024]{1,0:T(8,128)(2,1)S(1)} %copy-done.4, f32[1,32]{1,0:T(1,128)} %bitcast.16), custom_call_target="tpu_custom_call" | custom-call | flops 800000000 | bytes 1048576 | tf_op jit(solution)/shard_map/mix/pallas_call | solution.py:337
  35.6 0.0 copy-start.1
  35.6 18.3 %all_to_all.20 = bf16[128,4,128]{2,1,0:T(4,128)(2,1)S(1)} all-to-all(bf16[128,4,128]{2,1,0:T(4,128)(2,1)S(1)} %bitcast.15), channel_id=1, replica_groups=mesh['y'=8,'z'=8,'core'=2,'gz'=4] {'y','z','core'}, dimensions={0} | all-to-all | bytes 262144 | tf_op jit(solution)/shard_map/all_to_all | solution.py:356
  53.9 0.0 copy-done
  53.9 0.0 copy-done.2
  53.9 0.0 copy-done.5
  53.9 0.0 copy-done.1
  53.9 2.2 %pointwise.1 = (bf16[1280,128]{1,0:T(8,128)(2,1)S(1)}, bf16[4,128,1024]{2,1,0:T(8,128)(2,1)S(1)}) custom-call(bf16[512,128]{1,0:T(8,128)(2,1)S(1)} %bitcast.12, bf16[8,2,32,1024]{3,2,1,0:T(8,128)(2,1)S(1)} %copy-done, bf16[8,2,32,1024]{3,2,1,0:T(8,128)(2,1)S(1)} %copy-done.2, bf16[32,32]{1,0:T(8,128)(2,1)S(1)} %copy-done.5, ...), custom_call_target="tpu_custom_call" | custom-call | flops 200000000 | bytes 1048576 | tf_op jit(solution)/shard_map/pointwise/pallas_call | solution.py:337
  56.1 20.9 %all_to_all.21 = bf16[128,5,2,128]{3,2,1,0:T(2,128)(2,1)S(1)} all-to-all(bf16[128,5,2,128]{3,2,1,0:T(2,128)(2,1)S(1)} %bitcast.13), channel_id=1, replica_groups=mesh['y'=8,'z'=8,'core'=2,'gz'=4] {'y','z','core'}, dimensions={0} | all-to-all | bytes 655360 | tf_op jit(solution)/shard_map/all_to_all | solution.py:356
  77.0 0.5 x_forward.1
  77.5 3.4 %all_gather.13.shares = bf16[544,128]{1,0:T(8,128)(2,1)S(1)} all-gather(bf16[272,128]{1,0:T(8,128)(2,1)S(1)} %get-tuple-element.22), channel_id=1, replica_groups=mesh['y'=8,'z'=8,'core'=2,'gz'=4] {'core'}, dimensions={0}, use_global_device_ids=true | all-gather | bytes 208896 | tf_op jit(solution)/shard_map/all_gather | solution.py:406
  80.9 1.9 %adjoint.1 = (bf16[512,128]{1,0:T(8,128)(2,1)}, bf16[160,128]{1,0:T(8,128)(2,1)S(1)}) custom-call(f32[256,128]{1,0:T(8,128)S(1)} %get-tuple-element.21.kept, bf16[128,2048]{1,0:T(8,128)(2,1)S(1)} %all_gather.12.weight, bf16[256,1024]{1,0:T(8,128)(2,1)S(1)} %copy-done.4, bf16[544,128]{1,0:T(8,128)(2,1)S(1)} %all_gather.13.shares), custom_call_target="tpu_custom_call" | custom-call | flops 200000000 | bytes 1048576 | tf_op jit(solution)/shard_map/adjoint/pallas_call | solution.py:337
  82.8 0.0 copy-start.7
  82.8 5.8 %all-to-all-start.3 = ((bf16[128,4,128]{2,1,0:T(4,128)(2,1)}), bf16[128,4,128]{2,1,0:T(4,128)(2,1)S(1)}, u32[]{:S(2)}, u32[]{:S(2)}) async-start(bf16[128,4,128]{2,1,0:T(4,128)(2,1)} %bitcast.7), calls=%async_computation.3 | async-start | bytes 262144 | tf_op jit(solution)/shard_map/all_to_all | solution.py:356
  88.6 0.0 copy-done.7
  88.6 0.1 broadcast_multiply_fusion
  88.7 0.1 reshape.50.local4
  88.8 3.8 %all_gather.14 = bf16[320,128]{1,0:T(8,128)(2,1)S(1)} all-gather(bf16[160,128]{1,0:T(8,128)(2,1)S(1)} %get-tuple-element.25), channel_id=1, replica_groups={{0,1},{2,3},{4,5},{6,7},{8,9},{10,11},{12,13},{14,15},{16,17},{18,19},{..., dimensions={0}, use_global_device_ids=true | all-gather | bytes 122880 | tf_op jit(solution)/shard_map/all_gather | solution.py:416
  92.6 5.5 %all_gather.15.groups = bf16[640,128]{1,0:T(8,128)(2,1)S(1)} all-gather(bf16[320,128]{1,0:T(8,128)(2,1)S(1)} %all_gather.14), channel_id=1, replica_groups={{0,3},{1,2},{4,7},{5,6},{8,11},{9,10},{12,15},{13,14},{16,19},{17,18},{..., dimensions={0}, use_global_device_ids=true | all-gather | bytes 245760 | tf_op jit(solution)/shard_map/all_gather | solution.py:416
  98.1 2.8 %all-to-all-done.3 = bf16[128,4,128]{2,1,0:T(4,128)(2,1)S(1)} async-done(((bf16[128,4,128]{2,1,0:T(4,128)(2,1)}), bf16[128,4,128]{2,1,0:T(4,128)(2,1)S(1)}, u32[]{:S(2)}, u32[]{:S(2)}) %all-to-all-start.3) | async-done | bytes 131104 | tf_op jit(solution)/shard_map/all_to_all | solution.py:356
  100.9 2.7 %final.1 = (bf16[8,2,32,1024]{3,2,1,0:T(8,128)(2,1)}, bf16[64,2048]{1,0:T(8,128)(2,1)}, f32[32,32]{1,0:T(8,128)}, f32[1,32]{1,0:T(1,128)}) custom-call(bf16[512,128]{1,0:T(8,128)(2,1)S(1)} %bitcast.11, bf16[4,128,1024]{2,1,0:T(8,128)(2,1)S(1)} %get-tuple-element.24.delta, bf16[128,128]{1,0:T(8,128)(2,1)S(1)} %reshape.50.local4, ...), custom_call_target="tpu_custom_call" | custom-call | flops 200000000 | bytes 1048576 | tf_op jit(solution)/shard_map/final/pallas_call | solution.py:337
Async XLA Ops:
  0.6 21.1 %copy-start.6 = (bf16[64,2048]{1,0:T(8,128)(2,1)S(1)}, bf16[64,2048]{1,0:T(8,128)(2,1)}, u32[]{:S(2)}) copy-start(bf16[64,2048]{1,0:T(8,128)(2,1)} %param.11) | copy-start | bytes 786436
  3.1 30.8 %copy-start.3 = (bf16[256,1024]{1,0:T(8,128)(2,1)S(1)}, bf16[256,1024]{1,0:T(8,128)(2,1)}, u32[]{:S(2)}) copy-start(bf16[256,1024]{1,0:T(8,128)(2,1)} %constant.9.clone.forward) | copy-start | bytes 1572868
  3.1 30.8 %copy-start.4 = (bf16[256,1024]{1,0:T(8,128)(2,1)S(1)}, bf16[256,1024]{1,0:T(8,128)(2,1)}, u32[]{:S(2)}) copy-start(bf16[256,1024]{1,0:T(8,128)(2,1)} %constant.10.clone.inverse) | copy-start | bytes 1572868
  3.1 30.8 %all-to-all-start = ((bf16[128,4,128]{2,1,0:T(4,128)(2,1)}), bf16[128,4,128]{2,1,0:T(4,128)(2,1)S(1)}, u32[]{:S(2)}, u32[]{:S(2)}) async-start(bf16[128,4,128]{2,1,0:T(4,128)(2,1)} %bitcast), calls=%async_computation | async-start | bytes 262144 | tf_op jit(solution)/shard_map/all_to_all | solution.py:356
  33.9 20.0 %copy-start = (bf16[8,2,32,1024]{3,2,1,0:T(8,128)(2,1)S(1)}, bf16[8,2,32,1024]{3,2,1,0:T(8,128)(2,1)}, u32[]{:S(2)}) copy-start(bf16[8,2,32,1024]{3,2,1,0:T(8,128)(2,1)} %field.3) | copy-start | bytes 3145732
  33.9 20.0 %copy-start.2 = (bf16[8,2,32,1024]{3,2,1,0:T(8,128)(2,1)S(1)}, bf16[8,2,32,1024]{3,2,1,0:T(8,128)(2,1)}, u32[]{:S(2)}) copy-start(bf16[8,2,32,1024]{3,2,1,0:T(8,128)(2,1)} %cotangent.1) | copy-start | bytes 3145732
  33.9 20.0 %copy-start.5 = (bf16[32,32]{1,0:T(8,128)(2,1)S(1)}, bf16[32,32]{1,0:T(8,128)(2,1)}, u32[]{:S(2)}) copy-start(bf16[32,32]{1,0:T(8,128)(2,1)} %local.1) | copy-start | bytes 6148
  35.6 18.3 %copy-start.1 = (bf16[128,1024]{1,0:T(8,128)(2,1)S(1)}, bf16[128,1024]{1,0:T(8,128)(2,1)}, u32[]{:S(2)}) copy-start(bf16[128,1024]{1,0:T(8,128)(2,1)} %constant.8.clone.ytab) | copy-start | bytes 786436
  82.8 5.8 %copy-start.7 = (bf16[4,32,4,32]{3,2,1,0:T(4,128)(2,1)S(1)}, bf16[4,32,4,32]{3,2,1,0:T(4,128)(2,1)}, u32[]{:S(2)}) copy-start(bf16[4,32,4,32]{3,2,1,0:T(4,128)(2,1)} %constant.15) | copy-start | bytes 98308
  82.8 18.1 %all-to-all-start.3 = ((bf16[128,4,128]{2,1,0:T(4,128)(2,1)}), bf16[128,4,128]{2,1,0:T(4,128)(2,1)S(1)}, u32[]{:S(2)}, u32[]{:S(2)}) async-start(bf16[128,4,128]{2,1,0:T(4,128)(2,1)} %bitcast.7), calls=%async_computation.3 | async-start | bytes 262144 | tf_op jit(solution)/shard_map/all_to_all | solution.py:356

commit v7 on v6

--- a/solution.py
+++ b/solution.py
@@ -98,17 +98,19 @@
             ]
 
 
-def y_kernel(field, ytab, send, held, rows, table, sems):
+def y_kernel(field, ytab, bias, local, send, bias_row, local_near, held, rows, table, sems):
     copies = [pltpu.make_async_copy(ytab, table, sems.at[4])]
     for k in range(4):
         part = field.at[pl.ds(4 * (k % 2), 4), k // 2]
         copies.append(pltpu.make_async_copy(part, rows.at[k], sems.at[k]))
+    copies.append(pltpu.make_async_copy(bias, bias_row, sems.at[5]))
+    copies.append(pltpu.make_async_copy(local, local_near, sems.at[6]))
     for copy in copies:
         copy.start()
     for k in range(4):
         z, h = k // 2, k % 2
         if h == 0:
-            for copy in copies[3 * z : 3 + 2 * z]:
+            for copy in copies[3 * z : 3 + 4 * z]:
                 copy.wait()
         out = nt(table[...], rows[k].reshape(128, N))
         for p in range(2):
@@ -116,9 +118,7 @@
     send[...] = held[...].astype(BF16)
 
 
-def mix_kernel(recv, weight, forward, inverse, bias, send, kept, bias_row, held, sem):
-    copy = pltpu.make_async_copy(bias, bias_row, sem.at[0])
-    copy.start()
+def mix_kernel(recv, weight, forward, inverse, send, kept, held):
     real, imag = x_forward(recv, forward, held, 4)
     real = rounded(real)
     imag = rounded(imag)
@@ -139,18 +139,25 @@
     factor = mode_weight()
     x_inverse(rounded(fold(vre) * factor), rounded(fold(vim) * factor), inverse, held, 4)
     send[...] = held[...].astype(BF16)
-    copy.wait()
+
+
+def repeats():
+    row = lax.broadcasted_iota(jnp.int32, (128, C), 0)
+    return jnp.where((row & 31) == lax.broadcasted_iota(jnp.int32, (128, C), 1), 1.0, 0.0)
+
+
+def blocks(tall, picks):
+    row = lax.broadcasted_iota(jnp.int32, (128, 128), 0)
+    wide = nt(tall.astype(BF16), picks)
+    return jnp.where((row >> 5) == block_of((128, 128)), wide, 0.0).astype(BF16)
 
 
 def point_kernel(recv, field, cotangent, local, bias, ytab, send, delta, held, wide):
     held[...] = recv[...].astype(F32)
-    row = lax.broadcasted_iota(jnp.int32, (128, C), 0)
-    same = jnp.where((row & 31) == lax.broadcasted_iota(jnp.int32, (128, C), 1), 1.0, 0.0)
+    same = repeats()
     bias4 = jnp.sum(same * bias[...], axis=1, keepdims=True)
     picks = same.astype(BF16)
-    local4 = nt(nt(picks, local[...]).astype(BF16), picks)
-    row = lax.broadcasted_iota(jnp.int32, (128, 128), 0)
-    local4 = jnp.where((row >> 5) == block_of((128, 128)), local4, 0.0).astype(BF16)
+    local4 = blocks(nt(picks, local[...]), picks)
     ones = jnp.ones((16, N), BF16)
     total = jnp.zeros((144, 128), F32)
     outs = []
@@ -259,10 +266,12 @@
 
 
 def final_kernel(
-    recv, delta, local4, ytab, groups, field_grad, spectral_grad, local_grad, bias_grad,
+    recv, delta, local, ytab, groups, field_grad, spectral_grad, local_grad, bias_grad,
     held, rows, out, tiles, out_local, out_bias, sems,
 ):
     held[...] = recv[...].astype(F32)
+    picks = repeats().astype(BF16)
+    local4 = blocks(nn(picks, local[...]), picks)
     copies = [
         pltpu.make_async_copy(rows, field_grad, sems.at[0]),
         pltpu.make_async_copy(out, spectral_grad, sems.at[1]),
@@ -274,7 +283,7 @@
         spectrum = jnp.concatenate(
             [held[pl.ds(4 * z + 2 * p + h, KY, stride=8), :] for p in range(2)], axis=0
         )
-        left = jnp.concatenate([spectrum.T.astype(BF16), local4[...]], axis=1)
+        left = jnp.concatenate([spectrum.T.astype(BF16), local4], axis=1)
         for part in range(4):
             cols = slice(256 * part, 256 * (part + 1))
             right = jnp.concatenate([ytab[:, cols], delta[k, :, cols]], axis=0)
@@ -358,36 +367,33 @@
 
 def local(field, cotangent, spectral_weight, local_weight, bias):
     ytab, forward, inverse = (jnp.asarray(table) for table in tables())
-    same = jnp.asarray(np.kron(np.eye(4), np.ones((C, C))).astype(ml_dtypes.bfloat16))
-    local_in = jnp.tile(local_weight, (4, 4)) * same
     slab = ((512, 128), BF16)
     slab_wide = ((1280, 128), BF16)
     held = pltpu.VMEM((512, 128), F32)
     held_wide = pltpu.VMEM((1280, 128), F32)
     quarters = pltpu.VMEM((4, 4, C, N), BF16)
 
-    (send,) = run(
+    send, bias_row, local_near = run(
         y_kernel,
-        (field, ytab),
-        [slab],
-        [held, quarters, pltpu.VMEM((128, N), BF16), pltpu.SemaphoreType.DMA((5,))],
+        (field, ytab, bias.reshape(1, C), local_weight),
+        [slab, ((1, C), F32), ((C, C), BF16)],
+        [held, quarters, pltpu.VMEM((128, N), BF16), pltpu.SemaphoreType.DMA((7,))],
         "y_forward",
-        [HBM, HBM],
+        [HBM] * 4,
     )
     recv = exchange(send, 4, 128)
     weight = lax.all_gather(spectral_weight, "core", axis=0, tiled=True)
-    send, first, bias_row = run(
+    send, first = run(
         mix_kernel,
-        (recv, weight, forward, inverse, bias.reshape(1, C)),
-        [slab, ((KX, 128), BF16), ((1, C), F32)],
-        [held, pltpu.SemaphoreType.DMA((1,))],
+        (recv, weight, forward, inverse),
+        [slab, ((KX, 128), BF16)],
+        [held],
         "mix",
-        [VM, VM, VM, VM, HBM],
     )
     recv = exchange(send, 4, 128)
     send, delta = run(
         point_kernel,
-        (recv, field, cotangent, local_weight, bias_row, ytab),
+        (recv, field, cotangent, local_near, bias_row, ytab),
         [slab_wide, ((4, 128, N), BF16)],
         [
             held,
@@ -416,7 +422,7 @@
         group = lax.all_gather(group, "gz", axis=0, tiled=True, axis_index_groups=pairs)
     field_grad, spectral_grad, local_grad, bias_grad = run(
         final_kernel,
-        (recv, delta, local_in, ytab, group),
+        (recv, delta, local_near, ytab, group),
         [((8, 2, C, N), BF16), ((64, 2048), BF16), ((C, C), F32), ((1, C), F32)],
         [
             held,

time: 104 us -> 104 us (level)
  no operation moved by 1% of the time
where the time goes in v7:
time: 104 us; the launch traced here: 103 us
  blocking collectives  54.6 us (52%)
  starting transfers between devices  24.3 us (23%)
  waiting for transfers between devices  12.5 us (12%)
  Pallas kernels  11.1 us (11%)
    all_to_all x2, blocking collectives, exchange(): return lax.all_to_all(blocks, GX, 0, 0, tiled=True).reshape(values.shape)  39.2 us
    all_to_all x2, starting transfers between devices, exchange(): return lax.all_to_all(blocks, GX, 0, 0, tiled=True).reshape(values.shape)  24.3 us
    all_to_all x2, waiting for transfers between devices, exchange(): return lax.all_to_all(blocks, GX, 0, 0, tiled=True).reshape(values.shape)  12.5 us
    pallas_call x6, Pallas kernels, run(): pl.pallas_call(kernel, out_shape=[(pltpu.HBM if spec is HBM else jax.Shap...  11.1 us
    all_gather x2, blocking collectives, local(): lax.all_gather(group, 'gz', axis=0, tiled=True, axis_index_groups=pairs)  9.29 us
    all_gather x1, blocking collectives, local(): shares = lax.all_gather(share, 'core', axis=0, tiled=True)  3.38 us
    all_gather x1, blocking collectives, local(): weight = lax.all_gather(spectral_weight, 'core', axis=0, tiled=True)  2.7 us
  transfers between devices with their start and end apart: 2, of which 2 were waited for; matrix products, arithmetic and copies ran while one was open for 0% of the time, Pallas kernels for 0%

profile of v7, /device:TPU:1, one launch (start us, length us, event | category | flops | bytes accessed | tf_op | source)
XLA Modules:
  0.0 103.4 jit_solution(6193393133033663948)
XLA Ops:
  0.6 0.0 copy-start.5
  0.6 2.5 %y_forward.1 = (bf16[512,128]{1,0:T(8,128)(2,1)}, f32[1,32]{1,0:T(1,128)S(1)}, bf16[32,32]{1,0:T(8,128)(2,1)S(1)}) custom-call(bf16[8,2,32,1024]{3,2,1,0:T(8,128)(2,1)} %field.3, bf16[128,1024]{1,0:T(8,128)(2,1)} %constant.6.clone.ytab, f32[1,32]{1,0:T(1,128)} %bitcast.16, bf16[32,32]{1,0:T(8,128)(2,1)} %local.1), custom_call_target="tpu_custom_call" | custom-call | flops 200000000 | bytes 1048576 | tf_op jit(solution)/shard_map/y_forward/pallas_call | solution.py:346
  3.1 0.0 copy-start.3
  3.2 0.0 copy-start.4
  3.2 18.6 %all-to-all-start = ((bf16[128,4,128]{2,1,0:T(4,128)(2,1)}), bf16[128,4,128]{2,1,0:T(4,128)(2,1)S(1)}, u32[]{:S(2)}, u32[]{:S(2)}) async-start(bf16[128,4,128]{2,1,0:T(4,128)(2,1)} %bitcast.1), calls=%async_computation | async-start | bytes 262144 | tf_op jit(solution)/shard_map/all_to_all | solution.py:365
  21.7 0.0 copy-done.5
  21.7 2.7 %all_gather.12.weight = bf16[128,2048]{1,0:T(8,128)(2,1)S(1)} all-gather(bf16[64,2048]{1,0:T(8,128)(2,1)S(1)} %copy-done.5), channel_id=1, replica_groups=mesh['y'=8,'z'=8,'core'=2,'gz'=4] {'core'}, dimensions={0}, use_global_device_ids=true | all-gather | bytes 786432 | tf_op jit(solution)/shard_map/all_gather | solution.py:385
  24.4 9.5 %all-to-all-done = bf16[128,4,128]{2,1,0:T(4,128)(2,1)S(1)} async-done(((bf16[128,4,128]{2,1,0:T(4,128)(2,1)}), bf16[128,4,128]{2,1,0:T(4,128)(2,1)S(1)}, u32[]{:S(2)}, u32[]{:S(2)}) %all-to-all-start) | async-done | bytes 131104 | tf_op jit(solution)/shard_map/all_to_all | solution.py:365
  33.9 0.0 copy-done.3
  33.9 0.0 copy-done.4
  33.9 0.0 copy-start
  33.9 0.0 copy-start.2
  34.0 1.5 %mix.1 = (bf16[512,128]{1,0:T(8,128)(2,1)S(1)}, bf16[128,128]{1,0:T(8,128)(2,1)S(1)}) custom-call(bf16[512,128]{1,0:T(8,128)(2,1)S(1)} %bitcast.14, bf16[128,2048]{1,0:T(8,128)(2,1)S(1)} %all_gather.12.weight, bf16[256,1024]{1,0:T(8,128)(2,1)S(1)} %copy-done.3, bf16[256,1024]{1,0:T(8,128)(2,1)S(1)} %copy-done.4), custom_call_target="tpu_custom_call" | custom-call | flops 800000000 | bytes 1048576 | tf_op jit(solution)/shard_map/mix/pallas_call | solution.py:346
  35.4 0.0 copy-start.1
  35.4 18.3 %all_to_all.20 = bf16[128,4,128]{2,1,0:T(4,128)(2,1)S(1)} all-to-all(bf16[128,4,128]{2,1,0:T(4,128)(2,1)S(1)} %bitcast.15), channel_id=1, replica_groups=mesh['y'=8,'z'=8,'core'=2,'gz'=4] {'y','z','core'}, dimensions={0} | all-to-all | bytes 262144 | tf_op jit(solution)/shard_map/all_to_all | solution.py:365
  53.7 0.0 copy-done
  53.7 0.0 copy-done.2
  53.7 0.0 copy-done.1
  53.7 2.2 %pointwise.1 = (bf16[1280,128]{1,0:T(8,128)(2,1)S(1)}, bf16[4,128,1024]{2,1,0:T(8,128)(2,1)S(1)}) custom-call(bf16[512,128]{1,0:T(8,128)(2,1)S(1)} %bitcast.12, bf16[8,2,32,1024]{3,2,1,0:T(8,128)(2,1)S(1)} %copy-done, bf16[8,2,32,1024]{3,2,1,0:T(8,128)(2,1)S(1)} %copy-done.2, bf16[32,32]{1,0:T(8,128)(2,1)S(1)} %get-tuple-element.21.local, ...), custom_call_target="tpu_custom_call" | custom-call | flops 200000000 | bytes 1048576 | tf_op jit(solution)/shard_map/pointwise/pallas_call | solution.py:346
  55.9 20.9 %all_to_all.21 = bf16[128,5,2,128]{3,2,1,0:T(2,128)(2,1)S(1)} all-to-all(bf16[128,5,2,128]{3,2,1,0:T(2,128)(2,1)S(1)} %bitcast.13), channel_id=1, replica_groups=mesh['y'=8,'z'=8,'core'=2,'gz'=4] {'y','z','core'}, dimensions={0} | all-to-all | bytes 655360 | tf_op jit(solution)/shard_map/all_to_all | solution.py:365
  76.8 0.5 x_forward.1
  77.3 3.4 %all_gather.13.shares = bf16[544,128]{1,0:T(8,128)(2,1)S(1)} all-gather(bf16[272,128]{1,0:T(8,128)(2,1)S(1)} %get-tuple-element.26), channel_id=1, replica_groups=mesh['y'=8,'z'=8,'core'=2,'gz'=4] {'core'}, dimensions={0}, use_global_device_ids=true | all-gather | bytes 208896 | tf_op jit(solution)/shard_map/all_gather | solution.py:412
  80.7 1.9 %adjoint.1 = (bf16[512,128]{1,0:T(8,128)(2,1)}, bf16[160,128]{1,0:T(8,128)(2,1)S(1)}) custom-call(f32[256,128]{1,0:T(8,128)S(1)} %get-tuple-element.25.kept, bf16[128,2048]{1,0:T(8,128)(2,1)S(1)} %all_gather.12.weight, bf16[256,1024]{1,0:T(8,128)(2,1)S(1)} %copy-done.4, bf16[544,128]{1,0:T(8,128)(2,1)S(1)} %all_gather.13.shares), custom_call_target="tpu_custom_call" | custom-call | flops 200000000 | bytes 1048576 | tf_op jit(solution)/shard_map/adjoint/pallas_call | solution.py:346
  82.6 5.7 %all-to-all-start.3 = ((bf16[128,4,128]{2,1,0:T(4,128)(2,1)}), bf16[128,4,128]{2,1,0:T(4,128)(2,1)S(1)}, u32[]{:S(2)}, u32[]{:S(2)}) async-start(bf16[128,4,128]{2,1,0:T(4,128)(2,1)} %bitcast.7), calls=%async_computation.3 | async-start | bytes 262144 | tf_op jit(solution)/shard_map/all_to_all | solution.py:365
  88.3 3.8 %all_gather.14 = bf16[320,128]{1,0:T(8,128)(2,1)S(1)} all-gather(bf16[160,128]{1,0:T(8,128)(2,1)S(1)} %get-tuple-element.29), channel_id=1, replica_groups={{0,1},{2,3},{4,5},{6,7},{8,9},{10,11},{12,13},{14,15},{16,17},{18,19},{..., dimensions={0}, use_global_device_ids=true | all-gather | bytes 122880 | tf_op jit(solution)/shard_map/all_gather | solution.py:422
  92.1 5.5 %all_gather.15.groups = bf16[640,128]{1,0:T(8,128)(2,1)S(1)} all-gather(bf16[320,128]{1,0:T(8,128)(2,1)S(1)} %all_gather.14), channel_id=1, replica_groups={{0,3},{1,2},{4,7},{5,6},{8,11},{9,10},{12,15},{13,14},{16,19},{17,18},{..., dimensions={0}, use_global_device_ids=true | all-gather | bytes 245760 | tf_op jit(solution)/shard_map/all_gather | solution.py:422
  97.6 3.0 %all-to-all-done.3 = bf16[128,4,128]{2,1,0:T(4,128)(2,1)S(1)} async-done(((bf16[128,4,128]{2,1,0:T(4,128)(2,1)}), bf16[128,4,128]{2,1,0:T(4,128)(2,1)S(1)}, u32[]{:S(2)}, u32[]{:S(2)}) %all-to-all-start.3) | async-done | bytes 131104 | tf_op jit(solution)/shard_map/all_to_all | solution.py:365
  100.6 2.6 %final.1 = (bf16[8,2,32,1024]{3,2,1,0:T(8,128)(2,1)}, bf16[64,2048]{1,0:T(8,128)(2,1)}, f32[32,32]{1,0:T(8,128)}, f32[1,32]{1,0:T(1,128)}) custom-call(bf16[512,128]{1,0:T(8,128)(2,1)S(1)} %bitcast.11, bf16[4,128,1024]{2,1,0:T(8,128)(2,1)S(1)} %get-tuple-element.28.delta, bf16[32,32]{1,0:T(8,128)(2,1)S(1)} %get-tuple-element.21.local, ...), custom_call_target="tpu_custom_call" | custom-call | flops 200000000 | bytes 1048576 | tf_op jit(solution)/shard_map/final/pallas_call | solution.py:346
Async XLA Ops:
  0.6 21.1 %copy-start.5 = (bf16[64,2048]{1,0:T(8,128)(2,1)S(1)}, bf16[64,2048]{1,0:T(8,128)(2,1)}, u32[]{:S(2)}) copy-start(bf16[64,2048]{1,0:T(8,128)(2,1)} %param.10) | copy-start | bytes 786436
  3.1 30.8 %copy-start.3 = (bf16[256,1024]{1,0:T(8,128)(2,1)S(1)}, bf16[256,1024]{1,0:T(8,128)(2,1)}, u32[]{:S(2)}) copy-start(bf16[256,1024]{1,0:T(8,128)(2,1)} %constant.7.clone.forward) | copy-start | bytes 1572868
  3.2 30.8 %copy-start.4 = (bf16[256,1024]{1,0:T(8,128)(2,1)S(1)}, bf16[256,1024]{1,0:T(8,128)(2,1)}, u32[]{:S(2)}) copy-start(bf16[256,1024]{1,0:T(8,128)(2,1)} %constant.8.clone.inverse) | copy-start | bytes 1572868
  3.2 30.8 %all-to-all-start = ((bf16[128,4,128]{2,1,0:T(4,128)(2,1)}), bf16[128,4,128]{2,1,0:T(4,128)(2,1)S(1)}, u32[]{:S(2)}, u32[]{:S(2)}) async-start(bf16[128,4,128]{2,1,0:T(4,128)(2,1)} %bitcast.1), calls=%async_computation | async-start | bytes 262144 | tf_op jit(solution)/shard_map/all_to_all | solution.py:365
  33.9 19.8 %copy-start = (bf16[8,2,32,1024]{3,2,1,0:T(8,128)(2,1)S(1)}, bf16[8,2,32,1024]{3,2,1,0:T(8,128)(2,1)}, u32[]{:S(2)}) copy-start(bf16[8,2,32,1024]{3,2,1,0:T(8,128)(2,1)} %field.3) | copy-start | bytes 3145732
  33.9 19.8 %copy-start.2 = (bf16[8,2,32,1024]{3,2,1,0:T(8,128)(2,1)S(1)}, bf16[8,2,32,1024]{3,2,1,0:T(8,128)(2,1)}, u32[]{:S(2)}) copy-start(bf16[8,2,32,1024]{3,2,1,0:T(8,128)(2,1)} %cotangent.1) | copy-start | bytes 3145732
  35.4 18.3 %copy-start.1 = (bf16[128,1024]{1,0:T(8,128)(2,1)S(1)}, bf16[128,1024]{1,0:T(8,128)(2,1)}, u32[]{:S(2)}) copy-start(bf16[128,1024]{1,0:T(8,128)(2,1)} %constant.6.clone.ytab) | copy-start | bytes 786436
  82.6 18.0 %all-to-all-start.3 = ((bf16[128,4,128]{2,1,0:T(4,128)(2,1)}), bf16[128,4,128]{2,1,0:T(4,128)(2,1)S(1)}, u32[]{:S(2)}, u32[]{:S(2)}) async-start(bf16[128,4,128]{2,1,0:T(4,128)(2,1)} %bitcast.7), calls=%async_computation.3 | async-start | bytes 262144 | tf_op jit(solution)/shard_map/all_to_all | solution.py:365

commit v8 on v7

--- a/solution.py
+++ b/solution.py
@@ -82,8 +82,9 @@
     return fold(real) * (1.0 / 32.0), fold(imag) * (1.0 / 32.0)
 
 
-def paired(real, imag):
-    return jnp.where((block_of(real.shape) & 1) == 0, real, imag)
+def packed(real, imag):
+    both = jnp.where((block_of(real.shape) & 1) == 0, real, imag)
+    return jnp.where(block_of((64, 128)) < 2, both[:64], both[64:]).astype(BF16)
 
 
 def x_inverse(real, imag, table, held, stride):
@@ -122,7 +123,7 @@
     real, imag = x_forward(recv, forward, held, 4)
     real = rounded(real)
     imag = rounded(imag)
-    kept[...] = paired(real, imag).astype(BF16)
+    kept[...] = packed(real, imag)
     k = lax.broadcasted_iota(jnp.int32, (128, 1024), 0)
     lane = lax.broadcasted_iota(jnp.int32, (128, 1024), 1)
     expand = jnp.where((lane >> 5) == k, 1.0, 0.0).astype(BF16)
@@ -218,13 +219,14 @@
     imag = rounded(imag * factor)
     kept[:KX] = real
     kept[KX:] = imag
-    share[:KX] = paired(real, imag).astype(BF16)
+    share[:64] = first[...]
+    share[64:128] = packed(real, imag)
     lines = [
         jnp.sum(held[pl.ds(4 + k, 128, stride=10), :], axis=0, keepdims=True) for k in range(5)
     ]
     total = jnp.concatenate(lines[:4], axis=0)
     bias = fold(lines[4])
-    share[KX : KX + 16] = jnp.concatenate(
+    share[128:] = jnp.concatenate(
         [
             rounded(total),
             total - rounded(total),
@@ -234,10 +236,9 @@
         ],
         axis=0,
     ).astype(BF16)
-    share[KX + 16 :] = first[...]
-
-
-def adjoint_kernel(kept, weight, inverse, shares, send, group, held, high, low):
+
+
+def adjoint_kernel(kept, weight, inverse, share, send, group, held, high, low):
     dre = kept[:KX]
     dim = kept[KX:]
     for t in range(8):
@@ -254,15 +255,7 @@
     back = rounded(nn(high[...], gather) + nn(low[...], gather))
     x_inverse(back[:KX], back[KX:], inverse, held, 4)
     send[...] = held[...].astype(BF16)
-    start = 64 * lax.axis_index("core")
-    left = block_of((64, 128)) < 2
-    step = 2 * KX + 16
-    for k, at in enumerate((KX + 16, 0)):
-        one = shares[pl.ds(pl.multiple_of(at + start, 16), 64), :].astype(F32)
-        two = shares[pl.ds(pl.multiple_of(step + at + start, 16), 64), :].astype(F32)
-        group[64 * k : 64 * (k + 1)] = jnp.where(left, one, two).astype(BF16)
-    group[128:144] = shares[KX : KX + 16]
-    group[144:160] = shares[step + KX : step + KX + 16]
+    group[...] = share[...]
 
 
 def final_kernel(
@@ -292,15 +285,20 @@
     lane = lax.broadcasted_iota(jnp.int32, (128, 1024), 1)
     k = lax.broadcasted_iota(jnp.int32, (128, 1024), 0)
     expand = jnp.where((lane >> 5) == k, 1.0, 0.0).astype(BF16)
-    first = jnp.concatenate([groups[160 * g : 160 * g + 64] for g in range(4)], axis=0).astype(F32)
-    turned = [first] + [pltpu.roll(first, 128 - 32 * b, 1) for b in range(1, 4)]
-    compact = jnp.concatenate(turned, axis=0).astype(BF16)
+    second_half = lax.axis_index("core") == 1
+
+    def own(at):
+        both = groups[at : at + 64].astype(F32)
+        return jnp.where(second_half, pltpu.roll(both, 64, 1), both)
+
+    first = jnp.concatenate([own(144 * g) for g in range(8)], axis=0)
+    compact = jnp.concatenate([first, pltpu.roll(first, 96, 1)], axis=0).astype(BF16)
     block = block_of((64, 128))
-    for g in range(4):
-        second = groups[160 * g + 64 : 160 * g + 128].astype(F32)
-        for b in range(4):
-            tiles[64 * (4 * g + b) : 64 * (4 * g + b + 1)] = fold(
-                jnp.where(block == b, second, 0.0)
+    for g in range(8):
+        second = own(144 * g + 64)
+        for part in range(2):
+            tiles[64 * (8 * part + g) : 64 * (8 * part + g + 1)] = fold(
+                jnp.where(block == part, second, 0.0)
             )
     for pair in range(4):
         wide = nn(compact, expand[:, 256 * pair : 256 * (pair + 1)])
@@ -309,24 +307,25 @@
             cols = slice(128 * half, 128 * (half + 1))
             real = jnp.zeros((64, 128), F32)
             imag = jnp.zeros((64, 128), F32)
-            for g in range(4):
-                for z in range(2):
-                    b = 2 * z
-                    ure = wide[256 * b + 64 * g : 256 * b + 64 * (g + 1), cols]
-                    uim = wide[256 * (b + 1) + 64 * g : 256 * (b + 1) + 64 * (g + 1), cols]
-                    dre = tiles[64 * (4 * g + b) : 64 * (4 * g + b + 1)]
-                    dim = tiles[64 * (4 * g + b + 1) : 64 * (4 * g + b + 2)]
-                    real = real + (ure * dre + uim * dim)
-                    imag = imag + (ure * dim - uim * dre)
+            for g in range(8):
+                ure = wide[64 * g : 64 * (g + 1), cols]
+                uim = wide[512 + 64 * g : 512 + 64 * (g + 1), cols]
+                dre = tiles[64 * g : 64 * (g + 1)]
+                dim = tiles[512 + 64 * g : 512 + 64 * (g + 1)]
+                real = real + (ure * dre + uim * dim)
+                imag = imag + (ure * dim - uim * dre)
             out[:, 128 * t : 128 * (t + 1)] = real.astype(BF16)
             out[:, 1024 + 128 * t : 1024 + 128 * (t + 1)] = imag.astype(BF16)
     gscale = float((N * N * 8) ** -0.5)
-    total = groups[128:160].astype(F32)
-    for g in range(1, 4):
-        total = total + groups[160 * g + 128 : 160 * g + 160].astype(F32)
-    flat = jnp.concatenate(
-        [total[0:4] + total[4:8], total[16:20] + total[20:24]], axis=0
-    ) * gscale
+    halves = []
+    for c in range(2):
+        total = jnp.zeros((16, 128), F32)
+        for g in range(4):
+            at = 144 * (4 * c + g) + 128
+            total = total + groups[at : at + 16].astype(F32)
+        halves.append(total)
+    flat = jnp.concatenate([total[0:4] + total[4:8] for total in halves], axis=0) * gscale
+    total = halves[0]
     for q in range(4):
         out_local[pl.ds(q, 8, stride=4), :] = flat[:, 32 * q : 32 * (q + 1)]
     out_bias[...] = ((total[8:9] + total[9:10]) * gscale)[:, :32]
@@ -386,7 +385,7 @@
     send, first = run(
         mix_kernel,
         (recv, weight, forward, inverse),
-        [slab, ((KX, 128), BF16)],
+        [slab, ((64, 128), BF16)],
         [held],
         "mix",
     )
@@ -405,21 +404,21 @@
     second, share = run(
         back_kernel,
         (recv, forward, first),
-        [((2 * KX, 128), F32), ((2 * KX + 16, 128), BF16)],
+        [((2 * KX, 128), F32), ((144, 128), BF16)],
         [held_wide],
         "x_forward",
     )
-    shares = lax.all_gather(share, "core", axis=0, tiled=True)
     send, group = run(
         adjoint_kernel,
-        (second, weight, inverse, shares),
-        [slab, ((160, 128), BF16)],
+        (second, weight, inverse, share),
+        [slab, ((144, 128), BF16)],
         [held, pltpu.VMEM((256, 1024), BF16), pltpu.VMEM((256, 1024), BF16)],
         "adjoint",
     )
     recv = exchange(send, 4, 128)
     for pairs in ([[0, 1], [2, 3]], [[0, 3], [1, 2]]):
         group = lax.all_gather(group, "gz", axis=0, tiled=True, axis_index_groups=pairs)
+    group = lax.all_gather(group, "core", axis=0, tiled=True)
     field_grad, spectral_grad, local_grad, bias_grad = run(
         final_kernel,
         (recv, delta, local_near, ytab, group),

time: 104 us -> 104 us (level)
  waiting for transfers between devices: 12.5 us -> 9.49 us
  starting transfers between devices: 24.3 us -> 25.7 us
    all_to_all x2, waiting for transfers between devices: 12.5 us -> 9.49 us  [exchange(): return lax.all_to_all(blocks, GX, 0, 0, tiled=True).reshape(values.shape)]
    all_to_all x2, starting transfers between devices: 24.3 us -> 25.7 us  [exchange(): return lax.all_to_all(blocks, GX, 0, 0, tiled=True).reshape(values.shape)]
  transfers between devices with their start and end apart: 2 -> 2, of which waited for: 2 -> 1; matrix products, arithmetic and copies ran while one was open for 0% -> 0% of each run, Pallas kernels for 0% -> 0%
where the time goes in v8:
time: 104 us; the launch traced here: 103 us
  blocking collectives  55.4 us (53%)
  starting transfers between devices  25.7 us (25%)
  Pallas kernels  11.6 us (11%)
  waiting for transfers between devices  9.49 us (9%)
    all_to_all x2, blocking collectives, exchange(): return lax.all_to_all(blocks, GX, 0, 0, tiled=True).reshape(values.shape)  39.2 us
    all_to_all x2, starting transfers between devices, exchange(): return lax.all_to_all(blocks, GX, 0, 0, tiled=True).reshape(values.shape)  25.7 us
    pallas_call x6, Pallas kernels, run(): pl.pallas_call(kernel, out_shape=[(pltpu.HBM if spec is HBM else jax.Shap...  11.6 us
    all_to_all x2, waiting for transfers between devices, exchange(): return lax.all_to_all(blocks, GX, 0, 0, tiled=True).reshape(values.shape)  9.49 us
    all_gather x2, blocking collectives, local(): lax.all_gather(group, 'gz', axis=0, tiled=True, axis_index_groups=pairs)  9.15 us
    all_gather x1, blocking collectives, local(): group = lax.all_gather(group, 'core', axis=0, tiled=True)  4.36 us
    all_gather x1, blocking collectives, local(): weight = lax.all_gather(spectral_weight, 'core', axis=0, tiled=True)  2.7 us
  transfers between devices with their start and end apart: 2, of which 1 were waited for; matrix products, arithmetic and copies ran while one was open for 0% of the time, Pallas kernels for 0%

profile of v8, /device:TPU:1, one launch (start us, length us, event | category | flops | bytes accessed | tf_op | source)
XLA Modules:
  0.0 103.2 jit_solution(18082008574156224790)
XLA Ops:
  0.6 0.0 copy-start.5
  0.6 2.5 %y_forward.1 = (bf16[512,128]{1,0:T(8,128)(2,1)}, f32[1,32]{1,0:T(1,128)S(1)}, bf16[32,32]{1,0:T(8,128)(2,1)S(1)}) custom-call(bf16[8,2,32,1024]{3,2,1,0:T(8,128)(2,1)} %field.3, bf16[128,1024]{1,0:T(8,128)(2,1)} %constant.6.clone.ytab, f32[1,32]{1,0:T(1,128)} %bitcast.16, bf16[32,32]{1,0:T(8,128)(2,1)} %local.1), custom_call_target="tpu_custom_call" | custom-call | flops 200000000 | bytes 1048576 | tf_op jit(solution)/shard_map/y_forward/pallas_call | solution.py:345
  3.1 0.0 copy-start.3
  3.2 0.0 copy-start.4
  3.2 18.6 %all-to-all-start = ((bf16[128,4,128]{2,1,0:T(4,128)(2,1)}), bf16[128,4,128]{2,1,0:T(4,128)(2,1)S(1)}, u32[]{:S(2)}, u32[]{:S(2)}) async-start(bf16[128,4,128]{2,1,0:T(4,128)(2,1)} %bitcast.1), calls=%async_computation | async-start | bytes 262144 | tf_op jit(solution)/shard_map/all_to_all | solution.py:364
  21.7 0.0 copy-done.5
  21.7 2.7 %all_gather.12.weight = bf16[128,2048]{1,0:T(8,128)(2,1)S(1)} all-gather(bf16[64,2048]{1,0:T(8,128)(2,1)S(1)} %copy-done.5), channel_id=1, replica_groups=mesh['y'=8,'z'=8,'core'=2,'gz'=4] {'core'}, dimensions={0}, use_global_device_ids=true | all-gather | bytes 786432 | tf_op jit(solution)/shard_map/all_gather | solution.py:384
  24.4 9.5 %all-to-all-done = bf16[128,4,128]{2,1,0:T(4,128)(2,1)S(1)} async-done(((bf16[128,4,128]{2,1,0:T(4,128)(2,1)}), bf16[128,4,128]{2,1,0:T(4,128)(2,1)S(1)}, u32[]{:S(2)}, u32[]{:S(2)}) %all-to-all-start) | async-done | bytes 131104 | tf_op jit(solution)/shard_map/all_to_all | solution.py:364
  33.9 0.0 copy-done.3
  33.9 0.0 copy-done.4
  33.9 0.0 copy-start
  33.9 0.0 copy-start.2
  34.0 1.5 %mix.1 = (bf16[512,128]{1,0:T(8,128)(2,1)S(1)}, bf16[64,128]{1,0:T(8,128)(2,1)S(1)}) custom-call(bf16[512,128]{1,0:T(8,128)(2,1)S(1)} %bitcast.14, bf16[128,2048]{1,0:T(8,128)(2,1)S(1)} %all_gather.12.weight, bf16[256,1024]{1,0:T(8,128)(2,1)S(1)} %copy-done.4, bf16[256,1024]{1,0:T(8,128)(2,1)S(1)} %copy-done.3), custom_call_target="tpu_custom_call" | custom-call | flops 800000000 | bytes 1048576 | tf_op jit(solution)/shard_map/mix/pallas_call | solution.py:345
  35.4 0.0 copy-start.1
  35.4 18.3 %all_to_all.20 = bf16[128,4,128]{2,1,0:T(4,128)(2,1)S(1)} all-to-all(bf16[128,4,128]{2,1,0:T(4,128)(2,1)S(1)} %bitcast.15), channel_id=1, replica_groups=mesh['y'=8,'z'=8,'core'=2,'gz'=4] {'y','z','core'}, dimensions={0} | all-to-all | bytes 262144 | tf_op jit(solution)/shard_map/all_to_all | solution.py:364
  53.7 0.0 copy-done
  53.7 0.0 copy-done.2
  53.7 0.0 copy-done.1
  53.7 2.2 %pointwise.1 = (bf16[1280,128]{1,0:T(8,128)(2,1)S(1)}, bf16[4,128,1024]{2,1,0:T(8,128)(2,1)S(1)}) custom-call(bf16[512,128]{1,0:T(8,128)(2,1)S(1)} %bitcast.11, bf16[8,2,32,1024]{3,2,1,0:T(8,128)(2,1)S(1)} %copy-done, bf16[8,2,32,1024]{3,2,1,0:T(8,128)(2,1)S(1)} %copy-done.2, bf16[32,32]{1,0:T(8,128)(2,1)S(1)} %get-tuple-element.21.local, ...), custom_call_target="tpu_custom_call" | custom-call | flops 200000000 | bytes 1048576 | tf_op jit(solution)/shard_map/pointwise/pallas_call | solution.py:345
  55.9 20.9 %all_to_all.21 = bf16[128,5,2,128]{3,2,1,0:T(2,128)(2,1)S(1)} all-to-all(bf16[128,5,2,128]{3,2,1,0:T(2,128)(2,1)S(1)} %bitcast.13), channel_id=1, replica_groups=mesh['y'=8,'z'=8,'core'=2,'gz'=4] {'y','z','core'}, dimensions={0} | all-to-all | bytes 655360 | tf_op jit(solution)/shard_map/all_to_all | solution.py:364
  76.8 0.5 x_forward.1
  77.3 1.9 %adjoint.1 = (bf16[512,128]{1,0:T(8,128)(2,1)}, bf16[144,128]{1,0:T(8,128)(2,1)S(1)}) custom-call(f32[256,128]{1,0:T(8,128)S(1)} %get-tuple-element.25.kept, bf16[128,2048]{1,0:T(8,128)(2,1)S(1)} %all_gather.12.weight, bf16[256,1024]{1,0:T(8,128)(2,1)S(1)} %copy-done.3, bf16[144,128]{1,0:T(8,128)(2,1)S(1)} %get-tuple-element.26.share), custom_call_target="tpu_custom_call" | custom-call | flops 200000000 | bytes 1048576 | tf_op jit(solution)/shard_map/adjoint/pallas_call | solution.py:345
  79.2 7.2 %all-to-all-start.3 = ((bf16[128,4,128]{2,1,0:T(4,128)(2,1)}), bf16[128,4,128]{2,1,0:T(4,128)(2,1)S(1)}, u32[]{:S(2)}, u32[]{:S(2)}) async-start(bf16[128,4,128]{2,1,0:T(4,128)(2,1)} %bitcast.7), calls=%async_computation.3 | async-start | bytes 262144 | tf_op jit(solution)/shard_map/all_to_all | solution.py:364
  86.4 3.8 %all_gather.13 = bf16[288,128]{1,0:T(8,128)(2,1)S(1)} all-gather(bf16[144,128]{1,0:T(8,128)(2,1)S(1)} %get-tuple-element.29), channel_id=1, replica_groups={{0,1},{2,3},{4,5},{6,7},{8,9},{10,11},{12,13},{14,15},{16,17},{18,19},{..., dimensions={0}, use_global_device_ids=true | all-gather | bytes 110592 | tf_op jit(solution)/shard_map/all_gather | solution.py:420
  90.2 5.4 %all_gather.14 = bf16[576,128]{1,0:T(8,128)(2,1)S(1)} all-gather(bf16[288,128]{1,0:T(8,128)(2,1)S(1)} %all_gather.13), channel_id=1, replica_groups={{0,3},{1,2},{4,7},{5,6},{8,11},{9,10},{12,15},{13,14},{16,19},{17,18},{..., dimensions={0}, use_global_device_ids=true | all-gather | bytes 221184 | tf_op jit(solution)/shard_map/all_gather | solution.py:420
  95.5 4.4 %all_gather.15.groups = bf16[1152,128]{1,0:T(8,128)(2,1)S(1)} all-gather(bf16[576,128]{1,0:T(8,128)(2,1)S(1)} %all_gather.14), channel_id=1, replica_groups=mesh['y'=8,'z'=8,'core'=2,'gz'=4] {'core'}, dimensions={0}, use_global_device_ids=true | all-gather | bytes 442368 | tf_op jit(solution)/shard_map/all_gather | solution.py:421
  99.9 0.0 all-to-all-done.3
  99.9 3.1 %final.1 = (bf16[8,2,32,1024]{3,2,1,0:T(8,128)(2,1)}, bf16[64,2048]{1,0:T(8,128)(2,1)}, f32[32,32]{1,0:T(8,128)}, f32[1,32]{1,0:T(1,128)}) custom-call(bf16[512,128]{1,0:T(8,128)(2,1)S(1)} %bitcast.12, bf16[4,128,1024]{2,1,0:T(8,128)(2,1)S(1)} %get-tuple-element.28.delta, bf16[32,32]{1,0:T(8,128)(2,1)S(1)} %get-tuple-element.21.local, ...), custom_call_target="tpu_custom_call" | custom-call | flops 200000000 | bytes 1048576 | tf_op jit(solution)/shard_map/final/pallas_call | solution.py:345
Async XLA Ops:
  0.6 21.1 %copy-start.5 = (bf16[64,2048]{1,0:T(8,128)(2,1)S(1)}, bf16[64,2048]{1,0:T(8,128)(2,1)}, u32[]{:S(2)}) copy-start(bf16[64,2048]{1,0:T(8,128)(2,1)} %param.10) | copy-start | bytes 786436
  3.1 30.8 %copy-start.3 = (bf16[256,1024]{1,0:T(8,128)(2,1)S(1)}, bf16[256,1024]{1,0:T(8,128)(2,1)}, u32[]{:S(2)}) copy-start(bf16[256,1024]{1,0:T(8,128)(2,1)} %constant.8.clone.inverse) | copy-start | bytes 1572868
  3.2 30.8 %copy-start.4 = (bf16[256,1024]{1,0:T(8,128)(2,1)S(1)}, bf16[256,1024]{1,0:T(8,128)(2,1)}, u32[]{:S(2)}) copy-start(bf16[256,1024]{1,0:T(8,128)(2,1)} %constant.7.clone.forward) | copy-start | bytes 1572868
  3.2 30.8 %all-to-all-start = ((bf16[128,4,128]{2,1,0:T(4,128)(2,1)}), bf16[128,4,128]{2,1,0:T(4,128)(2,1)S(1)}, u32[]{:S(2)}, u32[]{:S(2)}) async-start(bf16[128,4,128]{2,1,0:T(4,128)(2,1)} %bitcast.1), calls=%async_computation | async-start | bytes 262144 | tf_op jit(solution)/shard_map/all_to_all | solution.py:364
  33.9 19.8 %copy-start = (bf16[8,2,32,1024]{3,2,1,0:T(8,128)(2,1)S(1)}, bf16[8,2,32,1024]{3,2,1,0:T(8,128)(2,1)}, u32[]{:S(2)}) copy-start(bf16[8,2,32,1024]{3,2,1,0:T(8,128)(2,1)} %field.3) | copy-start | bytes 3145732
  33.9 19.8 %copy-start.2 = (bf16[8,2,32,1024]{3,2,1,0:T(8,128)(2,1)S(1)}, bf16[8,2,32,1024]{3,2,1,0:T(8,128)(2,1)}, u32[]{:S(2)}) copy-start(bf16[8,2,32,1024]{3,2,1,0:T(8,128)(2,1)} %cotangent.1) | copy-start | bytes 3145732
  35.4 18.3 %copy-start.1 = (bf16[128,1024]{1,0:T(8,128)(2,1)S(1)}, bf16[128,1024]{1,0:T(8,128)(2,1)}, u32[]{:S(2)}) copy-start(bf16[128,1024]{1,0:T(8,128)(2,1)} %constant.6.clone.ytab) | copy-start | bytes 786436
  79.2 20.7 %all-to-all-start.3 = ((bf16[128,4,128]{2,1,0:T(4,128)(2,1)}), bf16[128,4,128]{2,1,0:T(4,128)(2,1)S(1)}, u32[]{:S(2)}, u32[]{:S(2)}) async-start(bf16[128,4,128]{2,1,0:T(4,128)(2,1)} %bitcast.7), calls=%async_computation.3 | async-start | bytes 262144 | tf_op jit(solution)/shard_map/all_to_all | solution.py:364

commit v9 on v8

--- a/solution.py
+++ b/solution.py
@@ -284,32 +284,29 @@
     copies[0].start()
     lane = lax.broadcasted_iota(jnp.int32, (128, 1024), 1)
     k = lax.broadcasted_iota(jnp.int32, (128, 1024), 0)
-    expand = jnp.where((lane >> 5) == k, 1.0, 0.0).astype(BF16)
-    second_half = lax.axis_index("core") == 1
-
-    def own(at):
-        both = groups[at : at + 64].astype(F32)
-        return jnp.where(second_half, pltpu.roll(both, 64, 1), both)
-
-    first = jnp.concatenate([own(144 * g) for g in range(8)], axis=0)
-    compact = jnp.concatenate([first, pltpu.roll(first, 96, 1)], axis=0).astype(BF16)
-    block = block_of((64, 128))
+    start = 64 * lax.axis_index("core")
+    expands = [
+        jnp.where((lane >> 5) + (start + 32 * part) == k, 1.0, 0.0).astype(BF16)
+        for part in range(2)
+    ]
+    compact = jnp.concatenate([groups[144 * g : 144 * g + 64] for g in range(8)], axis=0)
+    block = block_of((64, 128)) - 2 * lax.axis_index("core")
     for g in range(8):
-        second = own(144 * g + 64)
+        second = groups[144 * g + 64 : 144 * g + 128].astype(F32)
         for part in range(2):
             tiles[64 * (8 * part + g) : 64 * (8 * part + g + 1)] = fold(
                 jnp.where(block == part, second, 0.0)
             )
     for pair in range(4):
-        wide = nn(compact, expand[:, 256 * pair : 256 * (pair + 1)])
+        wide = [nn(compact, expand[:, 256 * pair : 256 * (pair + 1)]) for expand in expands]
         for half in range(2):
             t = 2 * pair + half
             cols = slice(128 * half, 128 * (half + 1))
             real = jnp.zeros((64, 128), F32)
             imag = jnp.zeros((64, 128), F32)
             for g in range(8):
-                ure = wide[64 * g : 64 * (g + 1), cols]
-                uim = wide[512 + 64 * g : 512 + 64 * (g + 1), cols]
+                ure = wide[0][64 * g : 64 * (g + 1), cols]
+                uim = wide[1][64 * g : 64 * (g + 1), cols]
                 dre = tiles[64 * g : 64 * (g + 1)]
                 dim = tiles[512 + 64 * g : 512 + 64 * (g + 1)]
                 real = real + (ure * dre + uim * dim)

time: 104 us -> 103 us (level)
  no operation moved by 1% of the time
where the time goes in v9:
time: 103 us; the launch traced here: 102 us
  blocking collectives  55.4 us (54%)
  starting transfers between devices  25.6 us (25%)
  Pallas kernels  11 us (11%)
  waiting for transfers between devices  9.49 us (9%)
    all_to_all x2, blocking collectives, exchange(): return lax.all_to_all(blocks, GX, 0, 0, tiled=True).reshape(values.shape)  39.2 us
    all_to_all x2, starting transfers between devices, exchange(): return lax.all_to_all(blocks, GX, 0, 0, tiled=True).reshape(values.shape)  25.6 us
    pallas_call x6, Pallas kernels, run(): pl.pallas_call(kernel, out_shape=[(pltpu.HBM if spec is HBM else jax.Shap...  11 us
    all_to_all x2, waiting for transfers between devices, exchange(): return lax.all_to_all(blocks, GX, 0, 0, tiled=True).reshape(values.shape)  9.49 us
    all_gather x2, blocking collectives, local(): lax.all_gather(group, 'gz', axis=0, tiled=True, axis_index_groups=pairs)  9.15 us
    all_gather x1, blocking collectives, local(): group = lax.all_gather(group, 'core', axis=0, tiled=True)  4.36 us
    all_gather x1, blocking collectives, local(): weight = lax.all_gather(spectral_weight, 'core', axis=0, tiled=True)  2.7 us
  transfers between devices with their start and end apart: 2, of which 1 were waited for; matrix products, arithmetic and copies ran while one was open for 0% of the time, Pallas kernels for 0%

profile of v9, /device:TPU:1, one launch (start us, length us, event | category | flops | bytes accessed | tf_op | source)
XLA Modules:
  0.0 102.3 jit_solution(11040920409524874571)
XLA Ops:
  0.6 0.0 copy-start.5
  0.6 2.5 %y_forward.1 = (bf16[512,128]{1,0:T(8,128)(2,1)}, f32[1,32]{1,0:T(1,128)S(1)}, bf16[32,32]{1,0:T(8,128)(2,1)S(1)}) custom-call(bf16[8,2,32,1024]{3,2,1,0:T(8,128)(2,1)} %field.3, bf16[128,1024]{1,0:T(8,128)(2,1)} %constant.6.clone.ytab, f32[1,32]{1,0:T(1,128)} %bitcast.16, bf16[32,32]{1,0:T(8,128)(2,1)} %local.1), custom_call_target="tpu_custom_call" | custom-call | flops 200000000 | bytes 1048576 | tf_op jit(solution)/shard_map/y_forward/pallas_call | solution.py:342
  3.1 0.0 copy-start.3
  3.2 0.0 copy-start.4
  3.2 18.6 %all-to-all-start = ((bf16[128,4,128]{2,1,0:T(4,128)(2,1)}), bf16[128,4,128]{2,1,0:T(4,128)(2,1)S(1)}, u32[]{:S(2)}, u32[]{:S(2)}) async-start(bf16[128,4,128]{2,1,0:T(4,128)(2,1)} %bitcast.1), calls=%async_computation | async-start | bytes 262144 | tf_op jit(solution)/shard_map/all_to_all | solution.py:361
  21.7 0.0 copy-done.5
  21.7 2.7 %all_gather.12.weight = bf16[128,2048]{1,0:T(8,128)(2,1)S(1)} all-gather(bf16[64,2048]{1,0:T(8,128)(2,1)S(1)} %copy-done.5), channel_id=1, replica_groups=mesh['y'=8,'z'=8,'core'=2,'gz'=4] {'core'}, dimensions={0}, use_global_device_ids=true | all-gather | bytes 786432 | tf_op jit(solution)/shard_map/all_gather | solution.py:381
  24.4 9.5 %all-to-all-done = bf16[128,4,128]{2,1,0:T(4,128)(2,1)S(1)} async-done(((bf16[128,4,128]{2,1,0:T(4,128)(2,1)}), bf16[128,4,128]{2,1,0:T(4,128)(2,1)S(1)}, u32[]{:S(2)}, u32[]{:S(2)}) %all-to-all-start) | async-done | bytes 131104 | tf_op jit(solution)/shard_map/all_to_all | solution.py:361
  33.9 0.0 copy-done.3
  33.9 0.0 copy-done.4
  33.9 0.0 copy-start
  33.9 0.0 copy-start.2
  34.0 1.5 %mix.1 = (bf16[512,128]{1,0:T(8,128)(2,1)S(1)}, bf16[64,128]{1,0:T(8,128)(2,1)S(1)}) custom-call(bf16[512,128]{1,0:T(8,128)(2,1)S(1)} %bitcast.14, bf16[128,2048]{1,0:T(8,128)(2,1)S(1)} %all_gather.12.weight, bf16[256,1024]{1,0:T(8,128)(2,1)S(1)} %copy-done.4, bf16[256,1024]{1,0:T(8,128)(2,1)S(1)} %copy-done.3), custom_call_target="tpu_custom_call" | custom-call | flops 800000000 | bytes 1048576 | tf_op jit(solution)/shard_map/mix/pallas_call | solution.py:342
  35.4 0.0 copy-start.1
  35.4 18.3 %all_to_all.20 = bf16[128,4,128]{2,1,0:T(4,128)(2,1)S(1)} all-to-all(bf16[128,4,128]{2,1,0:T(4,128)(2,1)S(1)} %bitcast.15), channel_id=1, replica_groups=mesh['y'=8,'z'=8,'core'=2,'gz'=4] {'y','z','core'}, dimensions={0} | all-to-all | bytes 262144 | tf_op jit(solution)/shard_map/all_to_all | solution.py:361
  53.7 0.0 copy-done
  53.7 0.0 copy-done.2
  53.7 0.0 copy-done.1
  53.7 2.2 %pointwise.1 = (bf16[1280,128]{1,0:T(8,128)(2,1)S(1)}, bf16[4,128,1024]{2,1,0:T(8,128)(2,1)S(1)}) custom-call(bf16[512,128]{1,0:T(8,128)(2,1)S(1)} %bitcast.11, bf16[8,2,32,1024]{3,2,1,0:T(8,128)(2,1)S(1)} %copy-done, bf16[8,2,32,1024]{3,2,1,0:T(8,128)(2,1)S(1)} %copy-done.2, bf16[32,32]{1,0:T(8,128)(2,1)S(1)} %get-tuple-element.21.local, ...), custom_call_target="tpu_custom_call" | custom-call | flops 200000000 | bytes 1048576 | tf_op jit(solution)/shard_map/pointwise/pallas_call | solution.py:342
  55.9 20.9 %all_to_all.21 = bf16[128,5,2,128]{3,2,1,0:T(2,128)(2,1)S(1)} all-to-all(bf16[128,5,2,128]{3,2,1,0:T(2,128)(2,1)S(1)} %bitcast.13), channel_id=1, replica_groups=mesh['y'=8,'z'=8,'core'=2,'gz'=4] {'y','z','core'}, dimensions={0} | all-to-all | bytes 655360 | tf_op jit(solution)/shard_map/all_to_all | solution.py:361
  76.8 0.5 x_forward.1
  77.3 1.9 %adjoint.1 = (bf16[512,128]{1,0:T(8,128)(2,1)}, bf16[144,128]{1,0:T(8,128)(2,1)S(1)}) custom-call(f32[256,128]{1,0:T(8,128)S(1)} %get-tuple-element.25.kept, bf16[128,2048]{1,0:T(8,128)(2,1)S(1)} %all_gather.12.weight, bf16[256,1024]{1,0:T(8,128)(2,1)S(1)} %copy-done.3, bf16[144,128]{1,0:T(8,128)(2,1)S(1)} %get-tuple-element.26.share), custom_call_target="tpu_custom_call" | custom-call | flops 200000000 | bytes 1048576 | tf_op jit(solution)/shard_map/adjoint/pallas_call | solution.py:342
  79.2 7.0 %all-to-all-start.3 = ((bf16[128,4,128]{2,1,0:T(4,128)(2,1)}), bf16[128,4,128]{2,1,0:T(4,128)(2,1)S(1)}, u32[]{:S(2)}, u32[]{:S(2)}) async-start(bf16[128,4,128]{2,1,0:T(4,128)(2,1)} %bitcast.7), calls=%async_computation.3 | async-start | bytes 262144 | tf_op jit(solution)/shard_map/all_to_all | solution.py:361
  86.2 3.8 %all_gather.13 = bf16[288,128]{1,0:T(8,128)(2,1)S(1)} all-gather(bf16[144,128]{1,0:T(8,128)(2,1)S(1)} %get-tuple-element.29), channel_id=1, replica_groups={{0,1},{2,3},{4,5},{6,7},{8,9},{10,11},{12,13},{14,15},{16,17},{18,19},{..., dimensions={0}, use_global_device_ids=true | all-gather | bytes 110592 | tf_op jit(solution)/shard_map/all_gather | solution.py:417
  90.0 5.4 %all_gather.14 = bf16[576,128]{1,0:T(8,128)(2,1)S(1)} all-gather(bf16[288,128]{1,0:T(8,128)(2,1)S(1)} %all_gather.13), channel_id=1, replica_groups={{0,3},{1,2},{4,7},{5,6},{8,11},{9,10},{12,15},{13,14},{16,19},{17,18},{..., dimensions={0}, use_global_device_ids=true | all-gather | bytes 221184 | tf_op jit(solution)/shard_map/all_gather | solution.py:417
  95.4 4.4 %all_gather.15.groups = bf16[1152,128]{1,0:T(8,128)(2,1)S(1)} all-gather(bf16[576,128]{1,0:T(8,128)(2,1)S(1)} %all_gather.14), channel_id=1, replica_groups=mesh['y'=8,'z'=8,'core'=2,'gz'=4] {'core'}, dimensions={0}, use_global_device_ids=true | all-gather | bytes 442368 | tf_op jit(solution)/shard_map/all_gather | solution.py:418
  99.7 0.0 all-to-all-done.3
  99.7 2.5 %final.1 = (bf16[8,2,32,1024]{3,2,1,0:T(8,128)(2,1)}, bf16[64,2048]{1,0:T(8,128)(2,1)}, f32[32,32]{1,0:T(8,128)}, f32[1,32]{1,0:T(1,128)}) custom-call(bf16[512,128]{1,0:T(8,128)(2,1)S(1)} %bitcast.12, bf16[4,128,1024]{2,1,0:T(8,128)(2,1)S(1)} %get-tuple-element.28.delta, bf16[32,32]{1,0:T(8,128)(2,1)S(1)} %get-tuple-element.21.local, ...), custom_call_target="tpu_custom_call" | custom-call | flops 200000000 | bytes 1048576 | tf_op jit(solution)/shard_map/final/pallas_call | solution.py:342
Async XLA Ops:
  0.6 21.1 %copy-start.5 = (bf16[64,2048]{1,0:T(8,128)(2,1)S(1)}, bf16[64,2048]{1,0:T(8,128)(2,1)}, u32[]{:S(2)}) copy-start(bf16[64,2048]{1,0:T(8,128)(2,1)} %param.10) | copy-start | bytes 786436
  3.1 30.8 %copy-start.3 = (bf16[256,1024]{1,0:T(8,128)(2,1)S(1)}, bf16[256,1024]{1,0:T(8,128)(2,1)}, u32[]{:S(2)}) copy-start(bf16[256,1024]{1,0:T(8,128)(2,1)} %constant.8.clone.inverse) | copy-start | bytes 1572868
  3.2 30.8 %copy-start.4 = (bf16[256,1024]{1,0:T(8,128)(2,1)S(1)}, bf16[256,1024]{1,0:T(8,128)(2,1)}, u32[]{:S(2)}) copy-start(bf16[256,1024]{1,0:T(8,128)(2,1)} %constant.7.clone.forward) | copy-start | bytes 1572868
  3.2 30.8 %all-to-all-start = ((bf16[128,4,128]{2,1,0:T(4,128)(2,1)}), bf16[128,4,128]{2,1,0:T(4,128)(2,1)S(1)}, u32[]{:S(2)}, u32[]{:S(2)}) async-start(bf16[128,4,128]{2,1,0:T(4,128)(2,1)} %bitcast.1), calls=%async_computation | async-start | bytes 262144 | tf_op jit(solution)/shard_map/all_to_all | solution.py:361
  33.9 19.8 %copy-start = (bf16[8,2,32,1024]{3,2,1,0:T(8,128)(2,1)S(1)}, bf16[8,2,32,1024]{3,2,1,0:T(8,128)(2,1)}, u32[]{:S(2)}) copy-start(bf16[8,2,32,1024]{3,2,1,0:T(8,128)(2,1)} %field.3) | copy-start | bytes 3145732
  33.9 19.8 %copy-start.2 = (bf16[8,2,32,1024]{3,2,1,0:T(8,128)(2,1)S(1)}, bf16[8,2,32,1024]{3,2,1,0:T(8,128)(2,1)}, u32[]{:S(2)}) copy-start(bf16[8,2,32,1024]{3,2,1,0:T(8,128)(2,1)} %cotangent.1) | copy-start | bytes 3145732
  35.4 18.3 %copy-start.1 = (bf16[128,1024]{1,0:T(8,128)(2,1)S(1)}, bf16[128,1024]{1,0:T(8,128)(2,1)}, u32[]{:S(2)}) copy-start(bf16[128,1024]{1,0:T(8,128)(2,1)} %constant.6.clone.ytab) | copy-start | bytes 786436
  79.2 20.5 %all-to-all-start.3 = ((bf16[128,4,128]{2,1,0:T(4,128)(2,1)}), bf16[128,4,128]{2,1,0:T(4,128)(2,1)S(1)}, u32[]{:S(2)}, u32[]{:S(2)}) async-start(bf16[128,4,128]{2,1,0:T(4,128)(2,1)} %bitcast.7), calls=%async_computation.3 | async-start | bytes 262144 | tf_op jit(solution)/shard_map/all_to_all | solution.py:361

commit v10 on v9

--- a/solution.py
+++ b/solution.py
@@ -318,7 +318,7 @@
     for c in range(2):
         total = jnp.zeros((16, 128), F32)
         for g in range(4):
-            at = 144 * (4 * c + g) + 128
+            at = 144 * (2 * g + c) + 128
             total = total + groups[at : at + 16].astype(F32)
         halves.append(total)
     flat = jnp.concatenate([total[0:4] + total[4:8] for total in halves], axis=0) * gscale
@@ -413,9 +413,9 @@
         "adjoint",
     )
     recv = exchange(send, 4, 128)
+    group = lax.all_gather(group, "core", axis=0, tiled=True)
     for pairs in ([[0, 1], [2, 3]], [[0, 3], [1, 2]]):
         group = lax.all_gather(group, "gz", axis=0, tiled=True, axis_index_groups=pairs)
-    group = lax.all_gather(group, "core", axis=0, tiled=True)
     field_grad, spectral_grad, local_grad, bias_grad = run(
         final_kernel,
         (recv, delta, local_near, ytab, group),

time: 103 us -> 102 us (level)
    all_gather x1, blocking collectives: 4.36 us -> 2.52 us  [local(): group = lax.all_gather(group, 'core', axis=0, tiled=True)]
    all_gather x2, blocking collectives: 9.15 us -> 10.3 us  [local(): lax.all_gather(group, 'gz', axis=0, tiled=True, axis_index_groups=pairs)]
where the time goes in v10:
time: 102 us
  blocking collectives  54.8 us (54%)
  starting transfers between devices  25.6 us (25%)
  Pallas kernels  11 us (11%)
  waiting for transfers between devices  9.49 us (9%)
    all_to_all x2, blocking collectives, exchange(): return lax.all_to_all(blocks, GX, 0, 0, tiled=True).reshape(values.shape)  39.2 us
    all_to_all x2, starting transfers between devices, exchange(): return lax.all_to_all(blocks, GX, 0, 0, tiled=True).reshape(values.shape)  25.6 us
    pallas_call x6, Pallas kernels, run(): pl.pallas_call(kernel, out_shape=[(pltpu.HBM if spec is HBM else jax.Shap...  11 us
    all_gather x2, blocking collectives, local(): lax.all_gather(group, 'gz', axis=0, tiled=True, axis_index_groups=pairs)  10.3 us
    all_to_all x2, waiting for transfers between devices, exchange(): return lax.all_to_all(blocks, GX, 0, 0, tiled=True).reshape(values.shape)  9.49 us
    all_gather x1, blocking collectives, local(): weight = lax.all_gather(spectral_weight, 'core', axis=0, tiled=True)  2.7 us
    all_gather x1, blocking collectives, local(): group = lax.all_gather(group, 'core', axis=0, tiled=True)  2.52 us
  transfers between devices with their start and end apart: 2, of which 1 were waited for; matrix products, arithmetic and copies ran while one was open for 0% of the time, Pallas kernels for 0%

profile of v10, /device:TPU:1, one launch (start us, length us, event | category | flops | bytes accessed | tf_op | source)
XLA Modules:
  0.0 101.6 jit_solution(8180851875451715647)
XLA Ops:
  0.6 0.0 copy-start.5
  0.6 2.5 %y_forward.1 = (bf16[512,128]{1,0:T(8,128)(2,1)}, f32[1,32]{1,0:T(1,128)S(1)}, bf16[32,32]{1,0:T(8,128)(2,1)S(1)}) custom-call(bf16[8,2,32,1024]{3,2,1,0:T(8,128)(2,1)} %field.3, bf16[128,1024]{1,0:T(8,128)(2,1)} %constant.6.clone.ytab, f32[1,32]{1,0:T(1,128)} %bitcast.16, bf16[32,32]{1,0:T(8,128)(2,1)} %local.1), custom_call_target="tpu_custom_call" | custom-call | flops 200000000 | bytes 1048576 | tf_op jit(solution)/shard_map/y_forward/pallas_call | solution.py:342
  3.1 0.0 copy-start.3
  3.2 0.0 copy-start.4
  3.2 18.6 %all-to-all-start = ((bf16[128,4,128]{2,1,0:T(4,128)(2,1)}), bf16[128,4,128]{2,1,0:T(4,128)(2,1)S(1)}, u32[]{:S(2)}, u32[]{:S(2)}) async-start(bf16[128,4,128]{2,1,0:T(4,128)(2,1)} %bitcast.1), calls=%async_computation | async-start | bytes 262144 | tf_op jit(solution)/shard_map/all_to_all | solution.py:361
  21.7 0.0 copy-done.5
  21.7 2.7 %all_gather.12.weight = bf16[128,2048]{1,0:T(8,128)(2,1)S(1)} all-gather(bf16[64,2048]{1,0:T(8,128)(2,1)S(1)} %copy-done.5), channel_id=1, replica_groups=mesh['y'=8,'z'=8,'core'=2,'gz'=4] {'core'}, dimensions={0}, use_global_device_ids=true | all-gather | bytes 786432 | tf_op jit(solution)/shard_map/all_gather | solution.py:381
  24.4 9.5 %all-to-all-done = bf16[128,4,128]{2,1,0:T(4,128)(2,1)S(1)} async-done(((bf16[128,4,128]{2,1,0:T(4,128)(2,1)}), bf16[128,4,128]{2,1,0:T(4,128)(2,1)S(1)}, u32[]{:S(2)}, u32[]{:S(2)}) %all-to-all-start) | async-done | bytes 131104 | tf_op jit(solution)/shard_map/all_to_all | solution.py:361
  33.9 0.0 copy-done.3
  33.9 0.0 copy-done.4
  33.9 0.0 copy-start
  33.9 0.0 copy-start.2
  34.0 1.5 %mix.1 = (bf16[512,128]{1,0:T(8,128)(2,1)S(1)}, bf16[64,128]{1,0:T(8,128)(2,1)S(1)}) custom-call(bf16[512,128]{1,0:T(8,128)(2,1)S(1)} %bitcast.14, bf16[128,2048]{1,0:T(8,128)(2,1)S(1)} %all_gather.12.weight, bf16[256,1024]{1,0:T(8,128)(2,1)S(1)} %copy-done.4, bf16[256,1024]{1,0:T(8,128)(2,1)S(1)} %copy-done.3), custom_call_target="tpu_custom_call" | custom-call | flops 800000000 | bytes 1048576 | tf_op jit(solution)/shard_map/mix/pallas_call | solution.py:342
  35.4 0.0 copy-start.1
  35.4 18.3 %all_to_all.20 = bf16[128,4,128]{2,1,0:T(4,128)(2,1)S(1)} all-to-all(bf16[128,4,128]{2,1,0:T(4,128)(2,1)S(1)} %bitcast.15), channel_id=1, replica_groups=mesh['y'=8,'z'=8,'core'=2,'gz'=4] {'y','z','core'}, dimensions={0} | all-to-all | bytes 262144 | tf_op jit(solution)/shard_map/all_to_all | solution.py:361
  53.7 0.0 copy-done
  53.7 0.0 copy-done.2
  53.7 0.0 copy-done.1
  53.7 2.2 %pointwise.1 = (bf16[1280,128]{1,0:T(8,128)(2,1)S(1)}, bf16[4,128,1024]{2,1,0:T(8,128)(2,1)S(1)}) custom-call(bf16[512,128]{1,0:T(8,128)(2,1)S(1)} %bitcast.11, bf16[8,2,32,1024]{3,2,1,0:T(8,128)(2,1)S(1)} %copy-done, bf16[8,2,32,1024]{3,2,1,0:T(8,128)(2,1)S(1)} %copy-done.2, bf16[32,32]{1,0:T(8,128)(2,1)S(1)} %get-tuple-element.21.local, ...), custom_call_target="tpu_custom_call" | custom-call | flops 200000000 | bytes 1048576 | tf_op jit(solution)/shard_map/pointwise/pallas_call | solution.py:342
  55.9 20.9 %all_to_all.21 = bf16[128,5,2,128]{3,2,1,0:T(2,128)(2,1)S(1)} all-to-all(bf16[128,5,2,128]{3,2,1,0:T(2,128)(2,1)S(1)} %bitcast.13), channel_id=1, replica_groups=mesh['y'=8,'z'=8,'core'=2,'gz'=4] {'y','z','core'}, dimensions={0} | all-to-all | bytes 655360 | tf_op jit(solution)/shard_map/all_to_all | solution.py:361
  76.8 0.5 x_forward.1
  77.3 1.9 %adjoint.1 = (bf16[512,128]{1,0:T(8,128)(2,1)}, bf16[144,128]{1,0:T(8,128)(2,1)S(1)}) custom-call(f32[256,128]{1,0:T(8,128)S(1)} %get-tuple-element.25.kept, bf16[128,2048]{1,0:T(8,128)(2,1)S(1)} %all_gather.12.weight, bf16[256,1024]{1,0:T(8,128)(2,1)S(1)} %copy-done.3, bf16[144,128]{1,0:T(8,128)(2,1)S(1)} %get-tuple-element.26.share), custom_call_target="tpu_custom_call" | custom-call | flops 200000000 | bytes 1048576 | tf_op jit(solution)/shard_map/adjoint/pallas_call | solution.py:342
  79.2 7.0 %all-to-all-start.3 = ((bf16[128,4,128]{2,1,0:T(4,128)(2,1)}), bf16[128,4,128]{2,1,0:T(4,128)(2,1)S(1)}, u32[]{:S(2)}, u32[]{:S(2)}) async-start(bf16[128,4,128]{2,1,0:T(4,128)(2,1)} %bitcast.7), calls=%async_computation.3 | async-start | bytes 262144 | tf_op jit(solution)/shard_map/all_to_all | solution.py:361
  86.2 2.5 %all_gather.13 = bf16[288,128]{1,0:T(8,128)(2,1)S(1)} all-gather(bf16[144,128]{1,0:T(8,128)(2,1)S(1)} %get-tuple-element.29), channel_id=1, replica_groups=mesh['y'=8,'z'=8,'core'=2,'gz'=4] {'core'}, dimensions={0}, use_global_device_ids=true | all-gather | bytes 110592 | tf_op jit(solution)/shard_map/all_gather | solution.py:416
  88.7 4.2 %all_gather.14 = bf16[576,128]{1,0:T(8,128)(2,1)S(1)} all-gather(bf16[288,128]{1,0:T(8,128)(2,1)S(1)} %all_gather.13), channel_id=1, replica_groups={{0,1},{2,3},{4,5},{6,7},{8,9},{10,11},{12,13},{14,15},{16,17},{18,19},{..., dimensions={0}, use_global_device_ids=true | all-gather | bytes 221184 | tf_op jit(solution)/shard_map/all_gather | solution.py:418
  92.9 6.2 %all_gather.15.groups = bf16[1152,128]{1,0:T(8,128)(2,1)S(1)} all-gather(bf16[576,128]{1,0:T(8,128)(2,1)S(1)} %all_gather.14), channel_id=1, replica_groups={{0,3},{1,2},{4,7},{5,6},{8,11},{9,10},{12,15},{13,14},{16,19},{17,18},{..., dimensions={0}, use_global_device_ids=true | all-gather | bytes 442368 | tf_op jit(solution)/shard_map/all_gather | solution.py:418
  99.1 0.0 all-to-all-done.3
  99.1 2.5 %final.1 = (bf16[8,2,32,1024]{3,2,1,0:T(8,128)(2,1)}, bf16[64,2048]{1,0:T(8,128)(2,1)}, f32[32,32]{1,0:T(8,128)}, f32[1,32]{1,0:T(1,128)}) custom-call(bf16[512,128]{1,0:T(8,128)(2,1)S(1)} %bitcast.12, bf16[4,128,1024]{2,1,0:T(8,128)(2,1)S(1)} %get-tuple-element.28.delta, bf16[32,32]{1,0:T(8,128)(2,1)S(1)} %get-tuple-element.21.local, ...), custom_call_target="tpu_custom_call" | custom-call | flops 200000000 | bytes 1048576 | tf_op jit(solution)/shard_map/final/pallas_call | solution.py:342
Async XLA Ops:
  0.6 21.1 %copy-start.5 = (bf16[64,2048]{1,0:T(8,128)(2,1)S(1)}, bf16[64,2048]{1,0:T(8,128)(2,1)}, u32[]{:S(2)}) copy-start(bf16[64,2048]{1,0:T(8,128)(2,1)} %param.10) | copy-start | bytes 786436
  3.1 30.8 %copy-start.3 = (bf16[256,1024]{1,0:T(8,128)(2,1)S(1)}, bf16[256,1024]{1,0:T(8,128)(2,1)}, u32[]{:S(2)}) copy-start(bf16[256,1024]{1,0:T(8,128)(2,1)} %constant.8.clone.inverse) | copy-start | bytes 1572868
  3.2 30.8 %copy-start.4 = (bf16[256,1024]{1,0:T(8,128)(2,1)S(1)}, bf16[256,1024]{1,0:T(8,128)(2,1)}, u32[]{:S(2)}) copy-start(bf16[256,1024]{1,0:T(8,128)(2,1)} %constant.7.clone.forward) | copy-start | bytes 1572868
  3.2 30.8 %all-to-all-start = ((bf16[128,4,128]{2,1,0:T(4,128)(2,1)}), bf16[128,4,128]{2,1,0:T(4,128)(2,1)S(1)}, u32[]{:S(2)}, u32[]{:S(2)}) async-start(bf16[128,4,128]{2,1,0:T(4,128)(2,1)} %bitcast.1), calls=%async_computation | async-start | bytes 262144 | tf_op jit(solution)/shard_map/all_to_all | solution.py:361
  33.9 19.8 %copy-start = (bf16[8,2,32,1024]{3,2,1,0:T(8,128)(2,1)S(1)}, bf16[8,2,32,1024]{3,2,1,0:T(8,128)(2,1)}, u32[]{:S(2)}) copy-start(bf16[8,2,32,1024]{3,2,1,0:T(8,128)(2,1)} %field.3) | copy-start | bytes 3145732
  33.9 19.8 %copy-start.2 = (bf16[8,2,32,1024]{3,2,1,0:T(8,128)(2,1)S(1)}, bf16[8,2,32,1024]{3,2,1,0:T(8,128)(2,1)}, u32[]{:S(2)}) copy-start(bf16[8,2,32,1024]{3,2,1,0:T(8,128)(2,1)} %cotangent.1) | copy-start | bytes 3145732
  35.4 18.3 %copy-start.1 = (bf16[128,1024]{1,0:T(8,128)(2,1)S(1)}, bf16[128,1024]{1,0:T(8,128)(2,1)}, u32[]{:S(2)}) copy-start(bf16[128,1024]{1,0:T(8,128)(2,1)} %constant.6.clone.ytab) | copy-start | bytes 786436
  79.2 19.9 %all-to-all-start.3 = ((bf16[128,4,128]{2,1,0:T(4,128)(2,1)}), bf16[128,4,128]{2,1,0:T(4,128)(2,1)S(1)}, u32[]{:S(2)}, u32[]{:S(2)}) async-start(bf16[128,4,128]{2,1,0:T(4,128)(2,1)} %bitcast.7), calls=%async_computation.3 | async-start | bytes 262144 | tf_op jit(solution)/shard_map/all_to_all | solution.py:361
